TPU v7x, 32 devices: a whole 2x2x4 slice. The times are simulated.
32 devices in a mesh: dp: 4 (over z), ctx: 8 (over y, x, core).
Axes of the slice: x: 2, y: 2, z: 4, core: 2. Of those that a mesh axis runs over, the one named last changes fastest.
Arguments:
- inputs: bfloat16 [4, 2048, 2048], P('dp', 'ctx'), may hold values from -6 to 6
- places: int32 [4, 2048], P('dp', 'ctx'), may hold values from 0 to 2047, as said below
- cotangent: bfloat16 [4, 2048, 2048], P('dp', 'ctx'), may hold values from -6 to 6
- attn_gain: float32 [2048], replicated, may hold values from 0.5 to 1.5
- w_qkv: bfloat16 [2048, 1536], P(('dp', 'ctx')), may hold values from -0.125 to 0.125
- q_gain: float32 [64], replicated, may hold values from 0.1 to 1.9
- k_gain: float32 [64], replicated, may hold values from 0.1 to 1.9
- w_out: bfloat16 [1024, 2048], P(('dp', 'ctx')), may hold values from -6 to 6
- ffn_gain: float32 [2048], replicated, may hold values from 0.5 to 1.5
- w_gateup: bfloat16 [2048, 2048], P(('dp', 'ctx')), may hold values from -0.125 to 0.125
- w_down: bfloat16 [1024, 2048], P(('dp', 'ctx')), may hold values from -0.1875 to 0.1875
Outputs:
- layer_output: bfloat16 [4, 2048, 2048], P('dp', 'ctx')
- grad_inputs: bfloat16 [4, 2048, 2048], P('dp', 'ctx')
- grad_attn_gain: float32 [2048], replicated
- grad_w_qkv: float32 [2048, 1536], P(('dp', 'ctx'))
- grad_q_gain: float32 [64], replicated
- grad_k_gain: float32 [64], replicated
- grad_w_out: float32 [1024, 2048], P(('dp', 'ctx'))
- grad_ffn_gain: float32 [2048], replicated
- grad_w_gateup: float32 [2048, 2048], P(('dp', 'ctx'))
- grad_w_down: float32 [1024, 2048], P(('dp', 'ctx'))
Inputs may be any that keep to these rules, and one draw needn't show every extreme that they name: Each row of places holds every position 0 to 2047 once. Cut a sequence into 16 blocks of 128 consecutive positions; each aligned block of 256 entries (one device's tokens) is a block b in increasing order followed by block 15 - b in increasing order.
All inputs are finite; a program needn't handle non-finite values.
Results may differ from a plain program's by a relative error of at most 0.02.
Values may be sent and summed in bfloat16 or wider, within the bound.
A program may use at most 128 MiB of HBM per device.

v0:
```python
import functools
import math

import jax
import jax.numpy as jnp
from jax import lax
from jax.experimental import pallas as pl
from jax.experimental.pallas import tpu as pltpu
from jax.sharding import PartitionSpec as P

HEADS = 16
GROUPS = 4
HEAD_DIM = 64
FF = 1024
f32 = jnp.float32
bf16 = jnp.bfloat16
MESH = pl.DeviceIdType.MESH
NZ = 4
EPS = 1e-06


class Place:
    def __init__(self):
        self.z = lax.axis_index("dp")
        spot = lax.axis_index("ctx")
        self.core = spot % 2
        self.x = (spot // 2) % 2
        self.y = spot // 4

    def at(self, z=None, y=None, x=None, core=None):
        z = self.z if z is None else z
        y = self.y if y is None else y
        x = self.x if x is None else x
        core = self.core if core is None else core
        return (z, y * 4 + x * 2 + core)

    def xn(self):
        return self.at(x=1 - self.x)

    def yn(self):
        return self.at(y=1 - self.y)

    def sn(self):
        return self.at(core=1 - self.core)

    def up(self):
        return self.at(z=self.z + 1)

    def down(self):
        return self.at(z=self.z - 1)


def barrier(pc):
    bar = pltpu.get_barrier_semaphore()

    def greet(device):
        pl.semaphore_signal(bar, inc=1, device_id=device, device_id_type=MESH)

    for device in (pc.xn(), pc.yn(), pc.sn()):
        greet(device)

    @pl.when(pc.z < NZ - 1)
    def _():
        greet(pc.up())

    @pl.when(pc.z > 0)
    def _():
        greet(pc.down())

    pl.semaphore_wait(bar, 3 + (1 - pc.z // (NZ - 1)) + (pc.z + NZ - 1) // NZ)


def far(z, i):
    m = z // 2
    zz = z + m * (3 - 2 * z)
    lo = 3 - i if i < 2 else (1 - zz if i == 2 else zz)
    return lo + m * (3 - 2 * lo)


def near(z, i):
    return far(z, NZ - 1 - i)


def remote(src, dst, dev, send, recv):
    return pltpu.make_async_remote_copy(
        src_ref=src, dst_ref=dst, send_sem=send, recv_sem=recv, device_id=dev, device_id_type=MESH
    )


def halves(rows):
    return pl.ds(0, rows // 2), pl.ds(rows // 2, rows // 2)


KZ, KX, KY, KD0, KD1, KS, KU = range(7)


class Gather:
    def __init__(self, pc, buf, send, recv):
        self.pc, self.buf, self.send, self.recv = pc, buf, send, recv
        self.h = halves(buf.shape[-2])

    def cp(self, idx, dev, ks, kr, slot):
        ref = self.buf.at[idx]
        return remote(ref, ref, dev, self.send.at[ks, slot], self.recv.at[kr, slot])

    def c_up(self, z0):
        p = self.pc
        return self.cp((z0, p.y, p.x, p.core), p.up(), KU, KZ, z0)

    def c_down(self, z0):
        p = self.pc
        return self.cp((z0, p.y, p.x, p.core), p.down(), KZ, KZ, z0)

    def c_x(self, z0):
        p = self.pc
        return self.cp((z0, p.y, p.x, p.core), p.xn(), KX, KX, z0)

    def c_y(self, z0):
        p = self.pc
        return self.cp((z0, p.y, p.x, p.core), p.yn(), KY, KY, z0)

    def c_d0(self, z0):
        p = self.pc
        return self.cp((z0, p.y, 1 - p.x, p.core, self.h[0]), p.yn(), KD0, KD0, z0)

    def c_d1(self, z0):
        p = self.pc
        return self.cp((z0, 1 - p.y, p.x, p.core, self.h[1]), p.xn(), KD1, KD1, z0)

    def c_s(self, z0):
        p = self.pc
        return self.cp((z0, slice(None), slice(None), p.core), p.sn(), KS, KS, z0)

    def plane_send(self, i):
        z0 = near(self.pc.z, i)
        self.c_x(z0).start()
        self.c_y(z0).start()

    def own_z(self):
        z = self.pc.z

        @pl.when(z < NZ - 1)
        def _():
            self.c_up(z).start()

        @pl.when(z > 0)
        def _():
            self.c_down(z).start()

    def z_event(self, i, plane=True):
        z = self.pc.z
        z0 = near(z, i)

        @pl.when(z0 < z)
        def _():
            self.c_up(z0).wait_recv()

            @pl.when(z < NZ - 1)
            def _():
                self.c_up(z0).start()

        @pl.when(z0 > z)
        def _():
            self.c_down(z0).wait_recv()

            @pl.when(z > 0)
            def _():
                self.c_down(z0).start()

        if plane:
            self.plane_send(i)

    def plane_event(self, i):
        z0 = near(self.pc.z, i)
        self.c_x(z0).wait_recv()
        self.c_d0(z0).start()
        self.c_y(z0).wait_recv()
        self.c_d1(z0).start()

    def core_event(self, i):
        z0 = near(self.pc.z, i)
        self.c_d0(z0).wait_recv()
        self.c_d1(z0).wait_recv()
        self.c_s(z0).start()

    def done_event(self, i):
        self.c_s(near(self.pc.z, i)).wait_recv()

    def finish(self):
        z = self.pc.z
        for z0 in range(NZ):
            for c in (self.c_x, self.c_y, self.c_d0, self.c_d1, self.c_s):
                c(z0).wait_send()

            @pl.when((z < NZ - 1) & (z0 <= z))
            def _():
                self.c_up(z0).wait_send()

            @pl.when((z > 0) & (z0 >= z))
            def _():
                self.c_down(z0).wait_send()


class GatherPlane:
    def __init__(self, pc, buf, send, recv):
        self.pc, self.buf, self.send, self.recv = pc, buf, send, recv
        self.h = halves(buf.shape[-2])

    def cp(self, idx, dev, s, r):
        ref = self.buf.at[idx]
        return remote(ref, ref, dev, self.send.at[s], self.recv.at[r])

    def yx(self, k):
        p = self.pc
        return (p.y if k < 2 else 1 - p.y), (p.x if k % 2 == 0 else 1 - p.x)

    def c_x(self):
        p = self.pc
        return self.cp((p.z, p.y, p.x, p.core), p.xn(), (KX, 0), (KX, 0))

    def c_y(self):
        p = self.pc
        return self.cp((p.z, p.y, p.x, p.core), p.yn(), (KY, 0), (KY, 0))

    def c_d0(self):
        p = self.pc
        return self.cp((p.z, p.y, 1 - p.x, p.core, self.h[0]), p.yn(), (KD0, 0), (KD0, 0))

    def c_d1(self):
        p = self.pc
        return self.cp((p.z, 1 - p.y, p.x, p.core, self.h[1]), p.xn(), (KD1, 0), (KD1, 0))

    def c_up(self, z0, k):
        p = self.pc
        y, x = self.yx(k)
        return self.cp((z0, y, x, p.core), p.up(), (10 + z0, k), (10 + z0, k))

    def c_down(self, z0, k):
        p = self.pc
        y, x = self.yx(k)
        return self.cp((z0, y, x, p.core), p.down(), (14 + z0, k), (10 + z0, k))

    def c_s(self, z0):
        p = self.pc
        return self.cp((z0, slice(None), slice(None), p.core), p.sn(), (KS, z0), (KS, z0))

    def z_send(self, k):
        z = self.pc.z

        @pl.when(z < NZ - 1)
        def _():
            self.c_up(z, k).start()

        @pl.when(z > 0)
        def _():
            self.c_down(z, k).start()

    def own_plane(self):
        self.c_x().start()
        self.c_y().start()

    def own_z(self):
        self.z_send(0)

    def plane_event(self):
        self.c_x().wait_recv()
        self.c_d0().start()
        self.z_send(1)
        self.c_y().wait_recv()
        self.c_d1().start()
        self.z_send(2)

    def diag_event(self):
        self.c_d0().wait_recv()
        self.c_d1().wait_recv()
        self.z_send(3)
        self.c_s(self.pc.z).start()

    def z_event(self, i, k):
        z = self.pc.z
        z0 = near(z, i)

        @pl.when(z0 < z)
        def _():
            self.c_up(z0, k).wait_recv()

            @pl.when(z < NZ - 1)
            def _():
                self.c_up(z0, k).start()

        @pl.when(z0 > z)
        def _():
            self.c_down(z0, k).wait_recv()

            @pl.when(z > 0)
            def _():
                self.c_down(z0, k).start()

    def core_event(self, i):
        self.c_s(near(self.pc.z, i)).start()

    def done_event(self, i):
        self.c_s(near(self.pc.z, i)).wait_recv()

    def finish(self):
        z = self.pc.z
        for c in (self.c_x, self.c_y, self.c_d0, self.c_d1):
            c().wait_send()
        for z0 in range(NZ):
            self.c_s(z0).wait_send()
            for k in range(4):

                @pl.when((z < NZ - 1) & (z0 <= z))
                def _():
                    self.c_up(z0, k).wait_send()

                @pl.when((z > 0) & (z0 >= z))
                def _():
                    self.c_down(z0, k).wait_send()


class GatherSequence:
    def __init__(self, pc, buf, send, recv):
        self.pc, self.buf, self.send, self.recv = pc, buf, send, recv
        rows = buf.shape[-2]
        self.h = (pl.ds(0, 128), pl.ds(128, rows - 128))

    def cp(self, idx, dev, k):
        ref = self.buf.at[idx]
        return remote(ref, ref, dev, self.send.at[k], self.recv.at[k])

    def c_x(self):
        p = self.pc
        return self.cp((p.y, p.x, p.core), p.xn(), 0)

    def c_y(self):
        p = self.pc
        return self.cp((p.y, p.x, p.core), p.yn(), 1)

    def c_d0(self):
        p = self.pc
        return self.cp((p.y, 1 - p.x, p.core, self.h[0]), p.yn(), 2)

    def c_d1(self):
        p = self.pc
        return self.cp((1 - p.y, p.x, p.core, self.h[1]), p.xn(), 3)

    def c_s(self, k):
        p = self.pc
        y, x = (p.y if k < 2 else 1 - p.y), (p.x if k % 2 == 0 else 1 - p.x)
        return self.cp((y, x, p.core), p.sn(), 4 + k)

    def own(self):
        for c in (self.c_x(), self.c_y(), self.c_s(0)):
            c.start()

    def plane_event(self):
        self.c_x().wait_recv()
        self.c_d0().start()
        self.c_s(1).start()
        self.c_y().wait_recv()
        self.c_d1().start()
        self.c_s(2).start()

    def core_event(self):
        self.c_d0().wait_recv()
        self.c_d1().wait_recv()
        self.c_s(3).start()

    def done_event(self):
        for k in range(4):
            self.c_s(k).wait_recv()

    def finish(self):
        for c in (self.c_x(), self.c_y(), self.c_d0(), self.c_d1()):
            c.wait_send()
        for k in range(4):
            self.c_s(k).wait_send()


LOG2E = math.log2(math.e)
VMEM = pltpu.VMEM


def dot(a, b):
    return jnp.dot(a, b, preferred_element_type=f32)


def dot_t(a, b):
    return lax.dot_general(a, b, (((1,), (1,)), ((), ())), preferred_element_type=f32)


def lanes(shape):
    return lax.broadcasted_iota(jnp.int32, shape, 1)


def roll_half(v):
    return pltpu.roll(v, 64, 1)


def swap_rot(v):
    first = lanes(v.shape) % 64 < 32
    return jnp.where(first, pltpu.roll(v, 96, 1), pltpu.roll(v, 32, 1))


def head_sums(v):
    row = lax.broadcasted_iota(jnp.int32, (128, 128), 0) // 64
    col = lax.broadcasted_iota(jnp.int32, (128, 128), 1) // 64
    ones = jnp.where(row == col, 1.0, 0.0).astype(bf16)
    high = v.astype(bf16)
    low = (v - high.astype(f32)).astype(bf16)
    return dot(high, ones) + dot(low, ones)


def cols(i, width):
    return pl.ds(pl.multiple_of(i * width, width), width)


def norm_into(src, gain, dst):
    def body(i, _):
        rows = pl.ds(pl.multiple_of(i * 32, 32), 32)
        v = src[rows, :].astype(f32)
        scale = lax.rsqrt(jnp.mean(v * v, axis=-1, keepdims=True) + EPS)
        dst[rows, :] = (v * scale * gain[...]).astype(dst.dtype)
        return 0

    lax.fori_loop(0, src.shape[0] // 32, body, 0)


def ticked(tick, first, events):
    for k, event in enumerate(events):
        if event is not None:

            @pl.when(tick == first + k)
            def _(event=event):
                event()


def turn(src, rows, core, mine, theirs):
    def body(t, _):
        v = jnp.transpose(src[:, cols(t, 128)])
        for k in range(64 // rows):
            a, b = v[2 * k * rows : (2 * k + 1) * rows], v[(2 * k + 1) * rows : (2 * k + 2) * rows]
            own, other = jnp.where(core == 0, a, b), jnp.where(core == 0, b, a)
            spot = t * (64 // rows) + k
            mine[spot, :, pl.ds(0, v.shape[1])] = own
            theirs[spot, pl.ds(0, rows), :] = other
        return 0

    lax.fori_loop(0, src.shape[1] // 128, body, 0)


def forward_kernel(dims, *refs):
    (tok, width, n_dev, heads_w, kv_w, ff) = dims
    (
        x_ref, cot_ref, hi_ref, cos_ref, sin_ref, g_attn, g_q, g_k, g_ffn,
        s_qkv, s_out, s_down, s_gu,
        o_y, o_tattn, o_tmix, o_tffn, o_tact, o_cot, o_ggu, o_kv, o_q2, o_linv, o_mixf, o_res,
        o_kk, o_va, o_mask, o_wqkv, o_wout, o_wgu,
        w_qkv, w_out, w_down, w_gu, kk, va, mask, mask_t, o2, gu, gact,
        y_ref, hattn_ref, qkv_ref, q2_ref, kvb, linv_ref, mixf_ref, mixb_ref, res_ref, hffn_ref,
        act_ref, cot2, ggu2, t_attn, t_mix, t_ffn, t_act, turn_a, turn_b,
        send, recv, kv_send, kv_recv, lsem, osem, ex_send, ex_recv,
    ) = refs
    pc = Place()
    shards = (s_qkv, s_out, s_down, s_gu)
    bufs = (w_qkv, w_out, w_down, w_gu)
    local = [
        pltpu.make_async_copy(s, b.at[pc.z, pc.y, pc.x, pc.core], lsem.at[k])
        for k, (s, b) in enumerate(zip(shards, bufs))
    ]
    for c in local:
        c.start()
    barrier(pc)
    for c in local:
        c.wait()
    qkv = Gather(pc, w_qkv, send.at[0], recv.at[0])
    out = GatherPlane(pc, w_out, send.at[1], recv.at[1])
    down = Gather(pc, w_down, send.at[2], recv.at[2])
    gateup = Gather(pc, w_gu, send.at[3], recv.at[3])
    seq = GatherSequence(pc, kvb, kv_send, kv_recv)
    part = functools.partial
    z = pc.z
    emitted = []

    def emit(src, dst):
        c = pltpu.make_async_copy(src, dst, osem.at[len(emitted)])
        emitted.append(c)
        c.start()

    def exchange(k, src, dst):
        return remote(src, dst, pc.sn(), ex_send.at[k], ex_recv.at[k])

    back = pl.ds(tok, tok)
    sent_cot = exchange(0, cot_ref, cot2.at[back, :])
    sent_attn = exchange(1, turn_a, t_attn.at[:, :, back])
    sent_mix = exchange(2, turn_b.at[:, pl.ds(0, s_out.shape[0]), :], t_mix.at[:, :, back])
    sent_ffn = exchange(3, turn_a, t_ffn.at[:, :, back])
    sent_act = exchange(4, turn_b.at[:, pl.ds(0, s_down.shape[0]), :], t_act.at[:, :, back])
    sent_ggu = exchange(5, ggu2.at[pl.ds(0, tok), :], ggu2.at[back, :])

    qkv.own_z()
    qkv.plane_send(0)
    norm_into(x_ref, g_attn, hattn_ref)
    qkv.z_event(1)
    sent_cot.start()
    cot2[pl.ds(0, tok), :] = cot_ref[...]
    turn(hattn_ref, s_qkv.shape[0], pc.core, t_attn, turn_a)
    sent_attn.start()
    qkv.plane_event(0)
    qkv.z_event(2)
    out.own_plane()
    out.own_z()
    down.own_z()
    gateup.own_z()
    qkv.z_event(3)
    qkv.plane_event(1)
    qkv.core_event(0)
    down.plane_send(0)
    gateup.plane_send(0)
    qkv.plane_event(2)
    qkv.core_event(1)
    down.z_event(1)
    gateup.z_event(1)
    qkv.plane_event(3)
    out.plane_event()

    def qkv_step(i):
        qkv.done_event(i)
        z0 = near(z, i)
        depth = width // NZ

        def body(n, _):
            c = cols(n, 256)
            w = w_qkv[z0, :, :, :, :, c].reshape(depth, 256)
            prod = dot(hattn_ref[:, cols(z0, depth)], w)
            if i == 0:
                qkv_ref[:, c] = prod
            else:
                qkv_ref[:, c] += prod
            return 0

        lax.fori_loop(0, qkv_ref.shape[1] // 256, body, 0)

    qkv_step(0)
    qkv.core_event(2)
    qkv_step(1)
    qkv.core_event(3)
    down.plane_event(0)
    gateup.plane_event(0)
    qkv_step(2)
    qkv_step(3)

    low = lanes((tok, 128)) < 64

    def head_tile(t, gain):
        u = qkv_ref[:, cols(t, 128)]
        n = u * lax.rsqrt(head_sums(u * u) * (1.0 / 64) + EPS) * gain[...]
        return n * cos_ref[...] + swap_rot(n) * sin_ref[...]

    for t in range(kv_w // 128):
        kvb[pc.y, pc.x, pc.core, pl.ds(0, tok), pl.ds(t * 128, 128)] = head_tile(
            heads_w // 128 + t, g_k
        ).astype(bf16)
    kvb[pc.y, pc.x, pc.core, pl.ds(0, tok), pl.ds(kv_w, kv_w)] = qkv_ref[
        :, pl.ds(heads_w + kv_w, kv_w)
    ].astype(bf16)
    blocks_row = jnp.broadcast_to(hi_ref[...], (16, tok)).astype(bf16)
    kvb[pc.y, pc.x, pc.core, pl.ds(tok, 16), pl.ds(0, tok)] = blocks_row
    kvb[pc.y, pc.x, pc.core, pl.ds(tok, 16), pl.ds(tok, tok)] = blocks_row
    seq.own()

    def query_tile(t, _):
        q = (head_tile(t, g_q) * 0.125).astype(bf16)
        zero = jnp.zeros_like(q)
        q2_ref[t, pl.ds(0, tok), :] = jnp.where(low, q, zero)
        q2_ref[t, pl.ds(tok, tok), :] = jnp.where(low, zero, q)
        return 0

    lax.fori_loop(0, heads_w // 128, query_tile, 0)
    emit(qkv_ref, o_kv)
    emit(q2_ref, o_q2)
    emit(w_qkv, o_wqkv)
    sent_cot.wait_recv()
    emit(cot2, o_cot)
    sent_attn.wait_recv()
    emit(t_attn, o_tattn)

    down.z_event(2)
    gateup.z_event(2)
    out.diag_event()
    down.plane_event(1)
    gateup.plane_event(1)
    seq.plane_event()
    down.z_event(3)
    for j in range(4):
        out.z_event(1, j)
    gateup.z_event(3)
    down.core_event(0)
    gateup.core_event(0)
    seq.core_event()
    seq.done_event()

    def unpack(b, _):
        y, x, c = b // 4, (b // 2) % 2, b % 2
        rows = pl.ds(pl.multiple_of(b * tok, tok), tok)
        for t in range(kv_w // 128):
            k = kvb[y, x, c, pl.ds(0, tok), pl.ds(t * 128, 128)].astype(f32)
            v = kvb[y, x, c, pl.ds(0, tok), pl.ds(kv_w + t * 128, 128)].astype(f32)
            k_r, v_r = roll_half(k), roll_half(v)
            kk[2 * t, rows, :] = jnp.where(low, k, k_r).astype(bf16)
            kk[2 * t + 1, rows, :] = jnp.where(low, k_r, k).astype(bf16)
            va[2 * t, rows, :] = jnp.where(low, v, 1.0).astype(bf16)
            va[2 * t + 1, rows, :] = jnp.where(low, v_r, 1.0).astype(bf16)
        step = tok // 2
        key_hi = kvb[y, x, c, pl.ds(tok, 16), pl.ds(0, tok)].astype(f32)[:1, :]
        for a in range(2):
            own = hi_ref[:, a * step : (a + 1) * step].astype(f32)
            row = lax.broadcasted_iota(jnp.int32, (step, step), 0).astype(f32)
            col = lanes((step, step)).astype(f32)
            for d in range(2):
                theirs = key_hi[:, d * step : (d + 1) * step]
                gap = (own - theirs) * float(step) + row - col
                place = pl.ds(pl.multiple_of(b * tok + d * step, step), step)
                mask[pl.ds(a * step, step), place] = jnp.where(gap >= 0, 1.0, 0.0).astype(bf16)
                gap = (own - theirs) * float(step) + col - row
                mask_t[place, pl.ds(a * step, step)] = jnp.where(gap >= 0, 1.0, 0.0).astype(bf16)
        return 0

    lax.fori_loop(0, n_dev, unpack, 0)
    emit(kk, o_kk)
    emit(va, o_va)
    emit(mask_t, o_mask)

    events = [part(out.z_event, 2, j) for j in range(4)] + [
        part(out.core_event, 1), part(down.plane_event, 2), part(gateup.plane_event, 2),
        part(down.core_event, 1), part(gateup.core_event, 1),
    ] + [part(out.z_event, 3, j) for j in range(4)] + [
        part(out.core_event, 2),
        part(down.plane_event, 3), part(gateup.plane_event, 3),
        part(down.core_event, 2), part(gateup.core_event, 2), part(out.core_event, 3),
    ]
    chunk = 512
    n_chunk = n_dev * tok // chunk

    def attend(tick, _):
        t, kc = tick // n_chunk, tick % n_chunk
        g = t // 2
        rows = pl.ds(pl.multiple_of(kc * chunk, chunk), chunk)
        s = dot_t(q2_ref[t], kk[g, rows, :])
        e = jnp.exp2(s * LOG2E).astype(bf16).reshape(2, tok, chunk) * mask[:, rows][None]
        o = dot(e.reshape(2 * tok, chunk), va[g, rows, :])

        @pl.when(kc == 0)
        def _():
            o2[...] = o

        @pl.when(kc > 0)
        def _():
            o2[...] += o

        @pl.when(kc == n_chunk - 1)
        def _():
            even, odd = o2[pl.ds(0, tok), :], o2[pl.ds(tok, tok), :]
            total = jnp.where(low, roll_half(even), odd)
            inv = 1.0 / total
            mixed = jnp.where(low, even, roll_half(odd)) * inv
            linv_ref[:, cols(t, 128)] = inv
            mixf_ref[:, cols(t, 128)] = mixed
            mixb_ref[:, cols(t, 128)] = mixed.astype(bf16)

        ticked(tick, 2, events)
        return 0

    lax.fori_loop(0, heads_w // 128 * n_chunk, attend, 0)

    emit(linv_ref, o_linv)
    emit(mixf_ref, o_mixf)
    turn(mixb_ref, s_out.shape[0], pc.core, t_mix, turn_b)
    sent_mix.start()
    for i in range(NZ):
        out.done_event(i)
    emit(w_out, o_wout)

    def residual_step(n, _):
        c = cols(n, 256)
        w = w_out[:, :, :, :, :, c].reshape(heads_w, 256)
        res_ref[:, c] = x_ref[:, c].astype(f32) + dot(mixb_ref[...], w)
        return 0

    lax.fori_loop(0, width // 256, residual_step, 0)
    norm_into(res_ref, g_ffn, hffn_ref)
    emit(res_ref, o_res)
    sent_mix.wait_recv()
    emit(t_mix, o_tmix)
    sent_attn.wait_send()
    turn(hffn_ref, s_gu.shape[0], pc.core, t_ffn, turn_a)
    sent_ffn.start()

    def gateup_step(i):
        gateup.done_event(i)
        z0 = near(z, i)
        depth = width // NZ

        def body(n, _):
            c = cols(n, 256)
            w = w_gu[z0, :, :, :, :, c].reshape(depth, 256)
            prod = dot(hffn_ref[:, cols(z0, depth)], w)
            if i == 0:
                gu[:, c] = prod
            else:
                gu[:, c] += prod
            return 0

        lax.fori_loop(0, 2 * ff // 256, body, 0)

    def grad_act_step(i):
        down.done_event(i)
        z0 = near(z, i)
        depth = ff // NZ
        gact[:, cols(z0, depth)] = dot_t(cot_ref[...], w_down[z0].reshape(depth, width))

    gateup_step(0)
    grad_act_step(0)
    gateup_step(1)
    grad_act_step(1)
    down.core_event(3)
    gateup_step(2)
    grad_act_step(2)
    gateup.core_event(3)
    grad_act_step(3)
    gateup_step(3)

    def gate_step(n, _):
        c = cols(n, 256)
        c2 = cols(n + ff // 256, 256)
        gate, up, grad = gu[:, c], gu[:, c2], gact[:, c]
        sig = 1.0 / (1.0 + jnp.exp(-gate))
        silu = gate * sig
        act_ref[:, c] = (silu * up).astype(bf16)
        ggu2[pl.ds(0, tok), c] = (grad * up * (sig * (1.0 + gate * (1.0 - sig)))).astype(bf16)
        ggu2[pl.ds(0, tok), c2] = (grad * silu).astype(bf16)
        return 0

    lax.fori_loop(0, ff // 256, gate_step, 0)
    sent_ggu.start()
    sent_mix.wait_send()
    turn(act_ref, s_down.shape[0], pc.core, t_act, turn_b)
    sent_act.start()
    emit(w_gu, o_wgu)
    sent_ffn.wait_recv()
    emit(t_ffn, o_tffn)

    def output_step(n, _):
        c = cols(n, 256)
        w = w_down[:, :, :, :, :, c].reshape(ff, 256)
        y_ref[:, c] = (res_ref[:, c] + dot(act_ref[...], w)).astype(bf16)
        return 0

    lax.fori_loop(0, width // 256, output_step, 0)
    emit(y_ref, o_y)
    sent_ggu.wait_recv()
    emit(ggu2, o_ggu)
    sent_act.wait_recv()
    emit(t_act, o_tact)
    for g in (qkv, out, down, gateup, seq):
        g.finish()
    for c in (sent_cot, sent_ffn, sent_act, sent_ggu):
        c.wait_send()
    for c in emitted:
        c.wait()


def forward(x, cot, blocks, cosine, sine, g_attn, g_q, g_k, g_ffn, s_qkv, s_out, s_down, s_gu, n_dev):
    tok, width = x.shape
    heads_w, kv_w = HEADS * HEAD_DIM, GROUPS * HEAD_DIM
    ff = s_down.shape[0] * n_dev * NZ
    length = n_dev * tok
    tiles = heads_w // 128
    shape = jax.ShapeDtypeStruct
    seven = [(NZ, 2, 2, 2) + s.shape for s in (s_qkv, s_out, s_down, s_gu)]
    qkv_rows, out_rows, down_rows, gu_rows = [s.shape[0] for s in (s_qkv, s_out, s_down, s_gu)]
    spots = n_dev * NZ // 2
    kv_buf = ((2, 2, 2, tok + 16, 2 * kv_w), bf16)
    turned = [((spots, r, 2 * tok), bf16) for r in (qkv_rows, out_rows, gu_rows, down_rows)]
    keep = [
        ((tok, width), bf16),
        *turned,
        ((2 * tok, width), bf16),
        ((2 * tok, 2 * ff), bf16),
        ((tok, s_qkv.shape[1]), f32),
        ((tiles, 2 * tok, 128), bf16),
        ((tok, heads_w), f32),
        ((tok, heads_w), f32),
        ((tok, width), f32),
        ((GROUPS, length, 128), bf16),
        ((GROUPS, length, 128), bf16),
        ((length, tok), bf16),
        (seven[0], bf16),
        (seven[1], bf16),
        (seven[3], bf16),
    ]
    outs = [shape(*k) for k in keep]
    vm = pl.BlockSpec(memory_space=VMEM)
    anyw = pl.BlockSpec(memory_space=pl.ANY)
    dma = pltpu.SemaphoreType.DMA
    flops = 2 * tok * (width * (s_qkv.shape[1] + heads_w + 2 * ff + 2 * ff) + 2 * heads_w * length)
    return pl.pallas_call(
        functools.partial(forward_kernel, (tok, width, n_dev, heads_w, kv_w, ff)),
        out_shape=outs,
        in_specs=[vm] * 9 + [anyw] * 4,
        out_specs=[anyw] * len(outs),
        scratch_shapes=[VMEM(s, bf16) for s in seven]
        + [
            VMEM((GROUPS, length, 128), bf16),
            VMEM((GROUPS, length, 128), bf16),
            VMEM((tok, length), bf16),
            VMEM((length, tok), bf16),
            VMEM((2 * tok, 128), f32),
            VMEM((tok, 2 * ff), f32),
            VMEM((tok, ff), f32),
            VMEM((tok, width), bf16),
            VMEM((tok, width), bf16),
            VMEM((tok, s_qkv.shape[1]), f32),
            VMEM((tiles, 2 * tok, 128), bf16),
            VMEM(*kv_buf),
            VMEM((tok, heads_w), f32),
            VMEM((tok, heads_w), f32),
            VMEM((tok, heads_w), bf16),
            VMEM((tok, width), f32),
            VMEM((tok, width), bf16),
            VMEM((tok, ff), bf16),
            VMEM((2 * tok, width), bf16),
            VMEM((2 * tok, 2 * ff), bf16),
            *[VMEM(*t) for t in turned],
            VMEM((spots, qkv_rows, tok), bf16),
            VMEM((spots, out_rows, tok), bf16),
            dma((4, 18, NZ)),
            dma((4, 14, NZ)),
            dma((8,)),
            dma((8,)),
            dma((4,)),
            dma((len(outs),)),
            dma((6,)),
            dma((6,)),
        ],
        compiler_params=pltpu.CompilerParams(
            collective_id=0, has_side_effects=True, vmem_limit_bytes=60 << 20
        ),
        cost_estimate=pl.CostEstimate(flops=flops, bytes_accessed=50 << 20, transcendentals=0),
        name="forward",
    )(x, cot, blocks, cosine, sine, g_attn, g_q, g_k, g_ffn, s_qkv, s_out, s_down, s_gu)


SD0, SD1, SX0, SX1, SY0, SY1, SA, SB = range(8)


class PlaneSum:
    def plane_setup(self, pc, rd, rx, ry, send, recv):
        self.pc, self.rd, self.rx, self.ry, self.send, self.recv = pc, rd, rx, ry, send, recv

    def cp(self, src, dst, dev, k, s):
        return remote(src, dst, dev, self.send.at[k, s], self.recv.at[k, s])

    def d0(self, s):
        p = self.pc
        return self.cp(self.piece(s, 1 - p.y, 1 - p.x, 0), self.rd.at[s, 0], p.yn(), SD0, s)

    def d1(self, s):
        p = self.pc
        return self.cp(self.piece(s, 1 - p.y, 1 - p.x, 1), self.rd.at[s, 1], p.xn(), SD1, s)

    def x1(self, s):
        p = self.pc
        return self.cp(self.piece(s, p.y, 1 - p.x, 1), self.rx.at[s, 1], p.xn(), SX1, s)

    def y0(self, s):
        p = self.pc
        return self.cp(self.piece(s, 1 - p.y, p.x, 0), self.ry.at[s, 0], p.yn(), SY0, s)

    def x0(self, s):
        return self.cp(self.rd.at[s, 0], self.rx.at[s, 0], self.pc.xn(), SX0, s)

    def y1(self, s):
        return self.cp(self.rd.at[s, 1], self.ry.at[s, 1], self.pc.yn(), SY1, s)

    def plane_first(self, s):
        for c in (self.d0, self.d1, self.x1, self.y0):
            c(s).start()

    def plane_second(self, s):
        p = self.pc
        self.d0(s).wait_recv()
        self.rd[s, 0] = self.rd[s, 0] + self.piece(s, p.y, 1 - p.x, 0)[...]
        self.x0(s).start()
        self.d1(s).wait_recv()
        self.rd[s, 1] = self.rd[s, 1] + self.piece(s, 1 - p.y, p.x, 1)[...]
        self.y1(s).start()

    def plane_arrived(self, s):
        for c in (self.x1, self.y0, self.x0, self.y1):
            c(s).wait_recv()

    def plane_total(self, s, k):
        p = self.pc
        own = self.piece(s, p.y, p.x, k)[...].astype(f32)
        return own + self.rx[s, k].astype(f32) + self.ry[s, k].astype(f32)

    def plane_finish(self, s):
        for c in (self.d0, self.d1, self.x1, self.y0, self.x0, self.y1):
            c(s).wait_send()


class Scatter(PlaneSum):
    def __init__(self, pc, part, bufs, out, send, recv):
        rd, rx, ry, self.zz = bufs
        self.plane_setup(pc, rd, rx, ry, send, recv)
        self.part, self.out = part, out
        self.h = halves(part.shape[-2])

    @staticmethod
    def scratch(rows, columns):
        half = VMEM((NZ, 2, rows // 2, columns), bf16)
        return [half, half, half, VMEM((NZ + 1, 2, rows // 2, columns), bf16)]

    def piece(self, s, y, x, k):
        return self.part.at[s, y, x, self.h[k]]

    def down(self, zp):
        return self.cp(self.rx.at[zp], self.zz.at[zp], self.pc.down(), SA, zp)

    def up(self, zp):
        gap = zp - (self.pc.z + 1)
        spot = zp + (1 - (gap + NZ - 1) // NZ) * (NZ - zp)
        return self.cp(self.rx.at[zp], self.zz.at[spot], self.pc.up(), SB, zp)

    def first(self, i):
        self.plane_first(far(self.pc.z, i))

    def d_event(self, i):
        self.plane_second(far(self.pc.z, i))

    def xy_event(self, i):
        zp = far(self.pc.z, i)
        self.plane_arrived(zp)
        for k in range(2):
            self.rx[zp, k] = self.plane_total(zp, k).astype(bf16)

    def z_event(self, i):
        z = self.pc.z
        zp = far(z, i)

        @pl.when(zp < z)
        def _():
            @pl.when(z < NZ - 1)
            def _():
                self.down(zp).wait_recv()
                self.rx[zp] = self.rx[zp] + self.zz[zp]

            self.down(zp).start()

        @pl.when(zp > z)
        def _():
            @pl.when(z > 0)
            def _():
                self.up(zp).wait_recv()
                self.rx[zp] = self.rx[zp] + self.zz[zp]

            self.up(zp).start()

    def final(self):
        z = self.pc.z
        self.plane_arrived(z)
        for k in range(2):
            self.out[self.h[k], :] = self.plane_total(z, k)

        @pl.when(z < NZ - 1)
        def _():
            self.down(z).wait_recv()
            for k in range(2):
                self.out[self.h[k], :] += self.zz[z, k].astype(f32)

        @pl.when(z > 0)
        def _():
            self.up(z).wait_recv()
            for k in range(2):
                self.out[self.h[k], :] += self.zz[NZ, k].astype(f32)

    def finish(self):
        z = self.pc.z
        for zp in range(NZ):
            self.plane_finish(zp)

            @pl.when(zp < z)
            def _():
                self.down(zp).wait_send()

            @pl.when(zp > z)
            def _():
                self.up(zp).wait_send()


class ScatterZ(PlaneSum):
    def __init__(self, pc, part, bufs, out, send, recv):
        rd, rx, ry, self.zz, self.sm = bufs
        self.plane_setup(pc, rd, rx, ry, send, recv)
        self.part, self.out = part, out
        self.h = halves(part.shape[-2])

    @staticmethod
    def scratch(rows, columns):
        half = VMEM((1, 2, rows // 2, columns), bf16)
        return [half, half, half, VMEM((NZ + 1, 4, rows, columns), bf16), VMEM((4, rows, columns), bf16)]

    def piece(self, s, y, x, k):
        return self.sm.at[y * 2 + x, self.h[k]]

    def down(self, zp, k, src):
        return self.cp(src, self.zz.at[zp, k], self.pc.down(), 8 + zp, k)

    def up(self, zp, k, src):
        gap = zp - (self.pc.z + 1)
        spot = zp + (1 - (gap + NZ - 1) // NZ) * (NZ - zp)
        return self.cp(src, self.zz.at[spot, k], self.pc.up(), 12 + zp, k)

    def first(self, i):
        z = self.pc.z
        zp = far(z, i)
        for k in range(4):
            src = self.part.at[zp, k // 2, k % 2]

            @pl.when((z == NZ - 1) & (zp < z))
            def _():
                self.down(zp, k, src).start()

            @pl.when((z == 0) & (zp > z))
            def _():
                self.up(zp, k, src).start()

    def z_event(self, i, k):
        z = self.pc.z
        zp = far(z, i)
        held = self.zz.at[zp, k]

        @pl.when((zp < z) & (z < NZ - 1))
        def _():
            self.down(zp, k, held).wait_recv()
            self.zz[zp, k] = self.zz[zp, k] + self.part[zp, k // 2, k % 2]
            self.down(zp, k, held).start()

        @pl.when((zp > z) & (z > 0))
        def _():
            self.up(zp, k, held).wait_recv()
            self.zz[zp, k] = self.zz[zp, k] + self.part[zp, k // 2, k % 2]
            self.up(zp, k, held).start()

    def own_event(self, k):
        z = self.pc.z

        @pl.when(z < NZ - 1)
        def _():
            self.down(z, k, self.zz.at[z, k]).wait_recv()

        @pl.when(z > 0)
        def _():
            self.up(z, k, self.zz.at[z, k]).wait_recv()

        own = self.part[z, k // 2, k % 2].astype(f32)

        @pl.when(z == 0)
        def _():
            self.sm[k] = (own + self.zz[z, k].astype(f32)).astype(bf16)

        @pl.when(z == NZ - 1)
        def _():
            self.sm[k] = (own + self.zz[NZ, k].astype(f32)).astype(bf16)

        @pl.when((z > 0) & (z < NZ - 1))
        def _():
            both = self.zz[z, k].astype(f32) + self.zz[NZ, k].astype(f32)
            self.sm[k] = (own + both).astype(bf16)

    def plane_send(self):
        self.plane_first(0)

    def plane_event(self):
        self.plane_second(0)

    def final(self):
        self.plane_arrived(0)
        for k in range(2):
            self.out[self.h[k], :] = self.plane_total(0, k)

    def finish(self):
        z = self.pc.z
        self.plane_finish(0)
        for zp in range(NZ):
            for k in range(4):

                @pl.when(zp < z)
                def _():
                    self.down(zp, k, self.zz.at[zp, k]).wait_send()

                @pl.when(zp > z)
                def _():
                    self.up(zp, k, self.zz.at[zp, k]).wait_send()


class SequenceSum(PlaneSum):
    def __init__(self, pc, terms, bufs, send, recv, core_send, core_recv):
        rd, rx, ry, self.theirs = bufs
        self.plane_setup(pc, rd, rx, ry, send, recv)
        self.terms, self.core_send, self.core_recv = terms, core_send, core_recv
        self.h = halves(terms.shape[-2])

    @staticmethod
    def scratch(rows, columns):
        half = VMEM((1, 2, rows // 2, columns), bf16)
        return [half, half, half, VMEM((2, 2, rows, columns), bf16)]

    def piece(self, s, y, x, k):
        return self.theirs.at[y, x, self.h[k]]

    def swap(self):
        p = self.pc
        return remote(
            self.terms.at[:, :, 1 - p.core], self.theirs, p.sn(), self.core_send, self.core_recv
        )

    def core_event(self):
        p = self.pc
        self.swap().wait_recv()
        for y in range(2):
            for x in range(2):
                self.theirs[y, x] = self.theirs[y, x] + self.terms[y, x, p.core]
        self.plane_first(0)

    def finish(self):
        self.swap().wait_send()
        self.plane_finish(0)


def norm_back(src, gain, grad, part_ref, part_row, emit):
    part_ref[pl.ds(part_row, 1), :] = jnp.zeros((1, part_ref.shape[1]), f32)

    def body(i, _):
        rows = pl.ds(pl.multiple_of(i * 32, 32), 32)
        v, g = src[rows, :].astype(f32), grad[rows, :]
        inv = lax.rsqrt(jnp.mean(v * v, axis=-1, keepdims=True) + EPS)
        unit = v * inv
        part_ref[pl.ds(part_row, 1), :] += jnp.sum(g * unit, axis=0, keepdims=True)
        gg = g * gain[...]
        emit(rows, inv * (gg - unit * jnp.mean(gg * unit, axis=-1, keepdims=True)))
        return 0

    lax.fori_loop(0, src.shape[0] // 32, body, 0)


def weight_grad(left, zp, right, part):
    rows, columns = part.shape[-2:]
    lhs = left[pl.ds(zp * 4, 4)].reshape(4 * rows, left.shape[-1])
    step = 512

    def body(n, _):
        c = cols(n, step)
        part[zp, :, :, :, c] = dot(lhs, right[:, c]).astype(bf16).reshape(2, 2, rows, step)
        return 0

    lax.fori_loop(0, columns // step, body, 0)


def backward_kernel(dims, *refs):
    (tok, width, n_dev, heads_w, kv_w, ff) = dims
    (
        cos_ref, sin_ref, g_q, g_k, g_ffn,
        i_tmix, i_tffn, i_tact, i_cot, i_ggu, i_qkv, i_q2, i_linv, i_mixf, i_res, i_kk, i_va,
        i_mask, i_wout, i_wgu,
        gqkv2, res, gains, out_wout, out_wgu, out_wdown,
        t_mix, t_ffn, t_act, cot2, ggu2, qkv, q2, linv, mixf, kk, va, mask_t, w_gu,
        part_out, part_gu, part_down, gh, gattn2, acc_k, acc_v, acc_q, aug, gm, terms,
        send, recv, kv_send, kv_recv, ex_send, ex_recv, lsem,
    ) = refs[:57]
    bufs = refs[57:]
    pc = Place()
    z = pc.z
    part = functools.partial
    loads = {}

    def load(name, src, dst):
        c = pltpu.make_async_copy(src, dst, lsem.at[len(loads)])
        loads[name] = c
        c.start()

    load("act", i_tact, t_act)
    load("cot", i_cot, cot2)
    load("ffn", i_tffn, t_ffn)
    load("ggu", i_ggu, ggu2)
    load("wgu", i_wgu, w_gu)
    load("res", i_res, res)
    load("mix", i_tmix, t_mix)
    load("mixf", i_mixf, mixf)
    load("linv", i_linv, linv)
    load("q2", i_q2, q2)
    load("kk", i_kk, kk)
    load("va", i_va, va)
    load("mask", i_mask, mask_t)
    load("qkv", i_qkv, qkv)
    barrier(pc)
    down = Scatter(pc, part_down, bufs[0:4], out_wdown, send.at[0], recv.at[0])
    gateup = Scatter(pc, part_gu, bufs[4:8], out_wgu, send.at[1], recv.at[1])
    out = ScatterZ(pc, part_out, bufs[8:13], out_wout, send.at[2], recv.at[2])
    seq = SequenceSum(pc, terms, bufs[13:17], kv_send, kv_recv, ex_send.at[2], ex_recv.at[2])

    loads["act"].wait()
    loads["cot"].wait()
    for i in range(NZ):
        weight_grad(t_act, far(z, i), cot2, part_down)
        down.first(i)
    loads["ffn"].wait()
    loads["ggu"].wait()
    for i in range(NZ):
        weight_grad(t_ffn, far(z, i), ggu2, part_gu)
        gateup.first(i)
        if i == 2:
            down.d_event(0)
    own = pl.ds(0, tok)
    back = pl.ds(tok, tok)
    loads["wgu"].wait()
    first_events = [part(gateup.d_event, 0), None, part(down.d_event, 1), None, part(down.xy_event, 0),
                    part(down.z_event, 0), None, None]

    def h_step(n, _):
        w = w_gu[n // 2, n % 2].reshape(width // 8, 2 * ff)
        gh[:, cols(n, width // 8)] = dot_t(ggu2[own, :], w)
        ticked(n, 0, first_events)
        return 0

    lax.fori_loop(0, 8, h_step, 0)
    load("wout", i_wout, w_gu.at[:, :, :, :, pl.ds(0, part_out.shape[-2]), :])
    loads["res"].wait()

    def keep_residual(rows, grad):
        total = cot2[rows, :].astype(f32) + grad
        res[rows, :] = total
        gattn2[rows, :] = total.astype(bf16)

    gains[...] = jnp.zeros_like(gains)
    norm_back(res, g_ffn, gh, gains, 1, keep_residual)
    sent_attn = remote(gattn2.at[own, :], gattn2.at[back, :], pc.sn(), ex_send.at[0], ex_recv.at[0])
    sent_attn.start()
    gateup.d_event(1)
    loads["wout"].wait()

    def m_step(n, _):
        w = w_gu[n, :, :, :, pl.ds(0, part_out.shape[-2]), :].reshape(heads_w // NZ, width)
        gm[:, cols(n, heads_w // NZ)] = dot_t(gattn2[own, :], w).astype(bf16)
        return 0

    lax.fori_loop(0, NZ, m_step, 0)
    sent_attn.wait_recv()
    loads["mix"].wait()
    for i in range(NZ):
        weight_grad(t_mix, far(z, i), gattn2, part_out)
        out.first(i)
    gateup.xy_event(0)
    gateup.z_event(0)
    down.d_event(2)
    down.xy_event(1)
    for name in ("mixf", "linv", "q2", "kk", "va", "mask", "qkv"):
        loads[name].wait()

    low = lanes((tok, 128)) < 64
    chunk = 512
    n_chunk = n_dev * tok // chunk
    events = [
        part(down.z_event, 1), part(gateup.d_event, 2), part(gateup.xy_event, 1),
        part(gateup.z_event, 1), part(down.d_event, 3), part(down.xy_event, 2),
        part(down.z_event, 2),
    ] + [part(out.z_event, 0, k) for k in range(4)] + [
        part(gateup.d_event, 3), part(gateup.xy_event, 2), part(gateup.z_event, 2),
    ] + [part(out.z_event, 1, k) for k in range(4)] + [part(out.z_event, 2, k) for k in range(4)]

    def attend(tick, _):
        t, kc = tick // n_chunk, tick % n_chunk
        g = t // 2
        rows = pl.ds(pl.multiple_of(kc * chunk, chunk), chunk)

        @pl.when(kc == 0)
        def _():
            c = cols(t, 128)
            grad = gm[:, c].astype(f32)
            delta = head_sums(grad * mixf[:, c]) * linv[:, c]
            grad = grad * linv[:, c]
            lane = lanes((tok, 128))
            for half in range(2):
                d = roll_half(delta) if half == 0 else delta
                v = grad if half == 0 else roll_half(grad)
                high = d.astype(bf16).astype(f32)
                rest = jnp.where(lane == 64, -high, jnp.where(lane == 65, high - d, 0.0))
                aug[pl.ds(half * tok, tok), :] = jnp.where(low, v, rest).astype(bf16)

        seen = mask_t[rows, :]
        e = jnp.exp2(dot_t(kk[g, rows, :], q2[t]) * LOG2E).astype(bf16)
        e = e * jnp.concatenate([seen, seen], axis=1)
        dv = dot(e, aug[...])
        ds = e * dot_t(va[g, rows, :], aug[...]).astype(bf16)
        dk = dot(ds, q2[t])
        dq = lax.dot_general(kk[g, rows, :], ds, (((0,), (0,)), ((), ())), preferred_element_type=f32)

        @pl.when(t % 2 == 0)
        def _():
            acc_k[rows, :] = dk
            acc_v[rows, :] = dv

        @pl.when(t % 2 == 1)
        def _():
            both_k = acc_k[rows, :] + dk
            both_v = acc_v[rows, :] + dv
            both_k = both_k + roll_half(both_k)
            lower = lanes((chunk, 128)) < 64
            both_v = jnp.where(lower, both_v, roll_half(both_v))
            mine = (lanes((chunk, 128)) // 64) == (g % 2)
            for b in range(chunk // tok):
                spot = kc * (chunk // tok) + b
                y, x, c = spot // 4, (spot // 2) % 2, spot % 2
                cut = slice(b * tok, (b + 1) * tok)
                for base, value in ((0, both_k), (kv_w, both_v)):
                    place = pl.ds(pl.multiple_of(base + (g // 2) * 128, 128), 128)
                    old = terms[y, x, c, :, place].astype(f32)
                    terms[y, x, c, :, place] = jnp.where(mine[cut], value[cut], old).astype(bf16)

        @pl.when(kc == 0)
        def _():
            acc_q[...] = dq

        @pl.when(kc > 0)
        def _():
            acc_q[...] += dq

        @pl.when(kc == n_chunk - 1)
        def _():
            turned = jnp.transpose(acc_q[...])
            gh[:, cols(t, 128)] = jnp.where(low, turned[:tok], turned[tok:]) * 0.125

        ticked(tick, 1, events)
        return 0

    lax.fori_loop(0, heads_w // 128 * n_chunk, attend, 0)
    seq.swap().start()

    def head_back(t, grad, gain, row):
        c = cols(t, 128)
        u = qkv[:, c]
        inv = lax.rsqrt(head_sums(u * u) * (1.0 / 64) + EPS)
        unit = u * inv
        grad = grad * cos_ref[...] - swap_rot(grad) * sin_ref[...]
        gains[pl.ds(row, 1), pl.ds(0, 128)] += jnp.sum(grad * unit, axis=0, keepdims=True)
        gg = grad * gain[...]
        gqkv2[own, c] = (inv * (gg - unit * head_sums(gg * unit) * (1.0 / 64))).astype(bf16)

    def query_back(t, _):
        head_back(t, gh[:, cols(t, 128)], g_q, 2)
        return 0

    lax.fori_loop(0, heads_w // 128 // 2, query_back, 0)
    seq.core_event()
    lax.fori_loop(heads_w // 128 // 2, heads_w // 128, query_back, 0)
    for k in range(4):
        out.own_event(k)
    seq.plane_second(0)
    out.plane_send()
    down.final()
    seq.plane_arrived(0)
    for k in range(2):
        rows = seq.h[k]
        gh[rows, pl.ds(0, 2 * kv_w)] = seq.plane_total(0, k)
    for t in range(kv_w // 128):
        head_back(heads_w // 128 + t, gh[:, pl.ds(t * 128, 128)], g_k, 3)
    gqkv2[own, pl.ds(heads_w + kv_w, kv_w)] = gh[:, pl.ds(kv_w, kv_w)].astype(bf16)
    sent_qkv = remote(gqkv2.at[own, :], gqkv2.at[back, :], pc.sn(), ex_send.at[1], ex_recv.at[1])
    sent_qkv.start()
    out.plane_event()
    gateup.final()
    out.final()
    sent_qkv.wait_recv()
    for g in (down, gateup, out, seq):
        g.finish()
    sent_attn.wait_send()
    sent_qkv.wait_send()


def last_kernel(dims, *refs):
    (tok, width, n_dev, heads_w, kv_w, ff) = dims
    (
        x_ref, g_attn, gqkv2, res, gains, i_tattn, i_wqkv,
        dx, o_attn, o_q, o_k, o_ffn, out_wqkv,
        t_attn, w_qkv, part_qkv, gh, held, came,
        send, recv, g_send, g_recv, lsem,
    ) = refs[:24]
    pc = Place()
    z = pc.z
    part = functools.partial
    load_t = pltpu.make_async_copy(i_tattn, t_attn, lsem.at[0])
    load_w = pltpu.make_async_copy(i_wqkv, w_qkv, lsem.at[1])
    load_t.start()
    load_w.start()
    bar = pltpu.get_barrier_semaphore()
    for device in (pc.xn(), pc.yn(), pc.sn()):
        pl.semaphore_signal(bar, inc=1, device_id=device, device_id_type=MESH)
    for k in range(1, NZ):
        there = pc.at(z=(z + k) % NZ)
        pl.semaphore_signal(bar, inc=1, device_id=there, device_id_type=MESH)
    pl.semaphore_wait(bar, 3 + NZ - 1)
    qkv = Scatter(pc, part_qkv, refs[24:28], out_wqkv, send, recv)
    load_t.wait()
    for i in range(NZ):
        weight_grad(t_attn, far(z, i), gqkv2, part_qkv)
        qkv.first(i)
    load_w.wait()
    columns = w_qkv.shape[-1]
    events = [None, None, part(qkv.d_event, 0), None, None, part(qkv.d_event, 1), part(qkv.xy_event, 0),
              part(qkv.z_event, 0)]

    def h_step(n, _):
        w = w_qkv[n // 2, n % 2].reshape(width // 8, columns)
        gh[:, cols(n, width // 8)] = dot_t(gqkv2[pl.ds(0, tok), :], w)
        ticked(n, 0, events)
        return 0

    lax.fori_loop(0, 8, h_step, 0)

    def keep_input(rows, grad):
        dx[rows, :] = (res[rows, :] + grad).astype(bf16)

    held[...] = gains[...]
    norm_back(x_ref, g_attn, gh, held, 0, keep_input)

    def hop(k, device):
        return remote(held, came.at[k], device, g_send.at[k], g_recv.at[k])

    hops = [hop(0, pc.sn()), hop(1, pc.xn()), hop(2, pc.yn())]
    between = [
        [part(qkv.d_event, 2), part(qkv.xy_event, 1), part(qkv.z_event, 1)],
        [part(qkv.d_event, 3), part(qkv.xy_event, 2), part(qkv.z_event, 2)],
        [],
    ]
    for k, c in enumerate(hops):
        c.start()
        for event in between[k]:
            event()
        c.wait()
        held[...] += came[k]
    came[3 + z] = held[...]
    ring = []
    for k in range(1, NZ):
        c = remote(held, came.at[3 + z], pc.at(z=(z + k) % NZ), g_send.at[2 + k], g_recv.at[3 + z])
        c.start()
        ring.append(c)
    qkv.final()
    for k in range(1, NZ):
        there = (z + k) % NZ
        remote(held, came.at[3 + there], pc.at(z=there), g_send.at[2 + k], g_recv.at[3 + there]).wait_recv()
    total = came[3]
    for k in range(1, NZ):
        total = total + came[3 + k]
    o_attn[...] = total[0:1]
    o_ffn[...] = total[1:2]
    for o, row in ((o_q, 2), (o_k, 3)):
        v = total[:, :128]
        o[...] = (v + roll_half(v))[row : row + 1, :64]
    for c in ring:
        c.wait_send()
    qkv.finish()


def backward(x, cosine, sine, g_attn, g_q, g_k, g_ffn, kept, rows, n_dev):
    (t_attn, t_mix, t_ffn, t_act, cot2, ggu2, qkv, q2, linv, mixf, res, kk, va, mask_t, w_qkv, w_out, w_gu) = kept
    tok, width = x.shape
    heads_w, kv_w = HEADS * HEAD_DIM, GROUPS * HEAD_DIM
    ff = ggu2.shape[1] // 2
    length = n_dev * tok
    columns = qkv.shape[1]
    dims = (tok, width, n_dev, heads_w, kv_w, ff)
    shape = jax.ShapeDtypeStruct
    vm = pl.BlockSpec(memory_space=VMEM)
    anyw = pl.BlockSpec(memory_space=pl.ANY)
    dma = pltpu.SemaphoreType.DMA
    r_qkv, r_out, r_gu, r_down = rows
    partial = [VMEM((NZ, 2, 2, r, width), bf16) for r in (r_out, r_gu, r_down)]
    like = [VMEM(v.shape, v.dtype) for v in (t_mix, t_ffn, t_act, cot2, ggu2, qkv, q2, linv, mixf, kk, va, mask_t, w_gu)]
    gqkv2, grad_res, gains, own_out, own_gu, own_down = pl.pallas_call(
        functools.partial(backward_kernel, dims),
        out_shape=[
            shape((2 * tok, columns), bf16),
            shape((tok, width), f32),
            shape((8, width), f32),
            shape((r_out, width), f32),
            shape((r_gu, width), f32),
            shape((r_down, width), f32),
        ],
        in_specs=[vm] * 5 + [anyw] * 15,
        out_specs=[vm] * 6,
        scratch_shapes=like
        + partial
        + [
            VMEM((tok, width), f32),
            VMEM((2 * tok, width), bf16),
            VMEM((length, 128), f32),
            VMEM((length, 128), f32),
            VMEM((128, 2 * tok), f32),
            VMEM((2 * tok, 128), bf16),
            VMEM((tok, heads_w), bf16),
            VMEM((2, 2, 2, tok, 2 * kv_w), bf16),
            dma((3, 16, NZ)),
            dma((3, 16, NZ)),
            dma((8, 1)),
            dma((8, 1)),
            dma((3,)),
            dma((3,)),
            dma((15,)),
        ]
        + Scatter.scratch(r_down, width)
        + Scatter.scratch(r_gu, width)
        + ScatterZ.scratch(r_out, width)
        + SequenceSum.scratch(tok, 2 * kv_w),
        compiler_params=pltpu.CompilerParams(
            collective_id=1, has_side_effects=True, vmem_limit_bytes=63 << 20
        ),
        cost_estimate=pl.CostEstimate(flops=20 * tok * width * width, bytes_accessed=60 << 20, transcendentals=0),
        name="backward",
    )(cosine, sine, g_q, g_k, g_ffn, t_mix, t_ffn, t_act, cot2, ggu2, qkv, q2, linv, mixf, res, kk, va, mask_t, w_out, w_gu)
    last = pl.pallas_call(
        functools.partial(last_kernel, dims),
        out_shape=[
            shape((tok, width), bf16),
            shape((1, width), f32),
            shape((1, 64), f32),
            shape((1, 64), f32),
            shape((1, width), f32),
            shape((r_qkv, columns), f32),
        ],
        in_specs=[vm] * 5 + [anyw] * 2,
        out_specs=[vm] * 6,
        scratch_shapes=[
            VMEM(t_attn.shape, bf16),
            VMEM(w_qkv.shape, bf16),
            VMEM((NZ, 2, 2, r_qkv, columns), bf16),
            VMEM((tok, width), f32),
            VMEM((8, width), f32),
            VMEM((3 + NZ, 8, width), f32),
            dma((8, NZ)),
            dma((8, NZ)),
            dma((3 + NZ,)),
            dma((3 + NZ,)),
            dma((2,)),
        ]
        + Scatter.scratch(r_qkv, columns),
        compiler_params=pltpu.CompilerParams(
            collective_id=2, has_side_effects=True, vmem_limit_bytes=60 << 20
        ),
        cost_estimate=pl.CostEstimate(flops=8 * tok * width * columns, bytes_accessed=20 << 20, transcendentals=0),
        name="last",
    )(x, g_attn, gqkv2, grad_res, gains, t_attn, w_qkv)
    dx, grad_attn, grad_q, grad_k, grad_ffn, own_qkv = last
    return dx, grad_attn[0], own_qkv, grad_q[0], grad_k[0], own_out, grad_ffn[0], own_gu, own_down


epsilon = 1e-06


def norm_rows(values, gain_vec):
    return (
        values * lax.rsqrt(jnp.mean(values * values, axis=-1, keepdims=True) + epsilon) * gain_vec
    )


def rotate(values, positions):
    half_dim = values.shape[-1] // 2
    frequency = jnp.exp(
        jnp.arange(half_dim).astype(jnp.float32) * (-2.0 * math.log(10000.0) / values.shape[-1])
    )
    angles = positions.astype(jnp.float32)[:, None] * frequency[None, :]
    cosine = jnp.cos(angles)[:, None, :]
    sine = jnp.sin(angles)[:, None, :]
    first = values[..., :half_dim]
    second = values[..., half_dim:]
    return jnp.concatenate(
        [first * cosine - second * sine, second * cosine + first * sine], axis=-1
    )


def project_heads(qkv_all, positions, q_gain, k_gain):
    tok_rows = qkv_all.shape[0]
    q_cols = HEADS * HEAD_DIM
    k_cols = GROUPS * HEAD_DIM
    queries = qkv_all[:, :q_cols].reshape(tok_rows, HEADS, HEAD_DIM)
    keys_raw = qkv_all[:, q_cols : q_cols + k_cols].reshape(tok_rows, GROUPS, HEAD_DIM)
    values = qkv_all[:, q_cols + k_cols :].reshape(tok_rows, GROUPS, HEAD_DIM)
    return (
        rotate(norm_rows(queries, q_gain), positions),
        rotate(norm_rows(keys_raw, k_gain), positions),
        values,
    )


def gated(gate_up):
    return jax.nn.silu(gate_up[:, :FF]) * gate_up[:, FF:]


def per_device_plain(
    inputs, places, cotangent, attn_gain, w_qkv, q_gain, k_gain, w_out, ffn_gain, w_gateup, w_down
):
    tok_rows = inputs.shape[1]
    repeat = HEADS // GROUPS
    score_scale = HEAD_DIM ** (-0.5)
    here_f = inputs[0].astype(jnp.float32)
    own_places = places[0]
    qkv_w, out_w = (
        lax.all_gather(w_qkv, ("dp", "ctx"), axis=0, tiled=True),
        lax.all_gather(w_out, ("dp", "ctx"), axis=0, tiled=True),
    )
    h_attn_f, pull_attn = jax.vjp(norm_rows, here_f, attn_gain)
    h_attn = h_attn_f.astype(jnp.bfloat16)
    qkv_all = jnp.dot(h_attn, qkv_w, preferred_element_type=jnp.float32)

    def heads_of(qkv_in, gain_q, gain_k):
        return project_heads(qkv_in, own_places, gain_q, gain_k)

    (queries, keys_f, values), pull_heads = jax.vjp(heads_of, qkv_all, q_gain, k_gain)
    query_b = queries.astype(jnp.bfloat16).reshape(tok_rows, GROUPS, repeat, HEAD_DIM)
    key_b = keys_f.astype(jnp.bfloat16)
    value_b = values.astype(jnp.bfloat16)
    all_keys, all_values = (
        lax.all_gather(key_b, "ctx", axis=0, tiled=True),
        lax.all_gather(value_b, "ctx", axis=0, tiled=True),
    )
    all_places = lax.all_gather(own_places, "ctx", axis=0, tiled=True)
    blocks = lax.axis_size("ctx")
    key_blocks = all_keys.reshape(blocks, tok_rows, GROUPS, HEAD_DIM)
    value_blocks = all_values.reshape(blocks, tok_rows, GROUPS, HEAD_DIM)
    place_blocks = all_places.reshape(blocks, tok_rows)

    def score_block(key_blk, place_blk):
        scores = (
            jnp.einsum("igrd,jgd->grij", query_b, key_blk, preferred_element_type=jnp.float32)
            * score_scale
        )
        allowed = place_blk[None, :] <= own_places[:, None]
        return (scores, allowed)

    def max_step(state_pair, entries):
        row_top, row_total = state_pair
        scores, allowed = score_block(entries[0], entries[1])
        scores = jnp.where(allowed, scores, -1e30)
        new_top = jnp.maximum(row_top, jnp.max(scores, axis=-1))
        row_total = row_total * jnp.exp(row_top - new_top) + jnp.sum(
            jnp.where(allowed, jnp.exp(scores - new_top[..., None]), 0.0), axis=-1
        )
        return ((new_top, row_total), None)

    start_pair = (
        jnp.full((GROUPS, repeat, tok_rows), -1e30, jnp.float32),
        jnp.zeros((GROUPS, repeat, tok_rows), jnp.float32),
    )
    (row_top, row_total), _ = lax.scan(max_step, start_pair, (key_blocks, place_blocks))
    log_total = row_top + jnp.log(row_total)

    def out_step(accum, entries):
        scores, allowed = score_block(entries[0], entries[1])
        weights_b = jnp.where(allowed, jnp.exp(scores - log_total[..., None]), 0.0).astype(
            jnp.bfloat16
        )
        return (
            accum
            + jnp.einsum(
                "grij,jgd->igrd", weights_b, entries[2], preferred_element_type=jnp.float32
            ),
            None,
        )

    mixed_f, _ = lax.scan(
        out_step,
        jnp.zeros((tok_rows, GROUPS, repeat, HEAD_DIM), jnp.float32),
        (key_blocks, place_blocks, value_blocks),
    )
    mixed_b = mixed_f.reshape(tok_rows, HEADS * HEAD_DIM).astype(jnp.bfloat16)
    attn_out = jnp.dot(mixed_b, out_w, preferred_element_type=jnp.float32)
    residual = here_f + attn_out
    gateup_w, down_w = (
        lax.all_gather(w_gateup, ("dp", "ctx"), axis=0, tiled=True),
        lax.all_gather(w_down, ("dp", "ctx"), axis=0, tiled=True),
    )
    h_ffn_f, pull_ffn = jax.vjp(norm_rows, residual, ffn_gain)
    h_ffn = h_ffn_f.astype(jnp.bfloat16)
    gate_up = jnp.dot(h_ffn, gateup_w, preferred_element_type=jnp.float32)
    act_f, pull_gate = jax.vjp(gated, gate_up)
    act_b = act_f.astype(jnp.bfloat16)
    result = residual + jnp.dot(act_b, down_w, preferred_element_type=jnp.float32)
    layer_output = result.astype(jnp.bfloat16)[None]
    gateup_w, down_w = (
        lax.all_gather(w_gateup, ("dp", "ctx"), axis=0, tiled=True),
        lax.all_gather(w_down, ("dp", "ctx"), axis=0, tiled=True),
    )
    grad_out = cotangent[0]
    grad_act = jnp.dot(grad_out, down_w.T, preferred_element_type=jnp.float32)
    grad_down = jnp.dot(act_b.T, grad_out, preferred_element_type=jnp.float32)
    grad_gu_b = pull_gate(grad_act)[0].astype(jnp.bfloat16)
    grad_gateup = jnp.dot(h_ffn.T, grad_gu_b, preferred_element_type=jnp.float32)
    grad_h_ffn = jnp.dot(grad_gu_b, gateup_w.T, preferred_element_type=jnp.float32)
    grad_resid_part, grad_ffn_gain = pull_ffn(grad_h_ffn)
    grad_residual = grad_out.astype(jnp.float32) + grad_resid_part
    grad_gateup_own, grad_down_own = (
        lax.psum_scatter(grad_gateup, ("dp", "ctx"), scatter_dimension=0, tiled=True),
        lax.psum_scatter(grad_down, ("dp", "ctx"), scatter_dimension=0, tiled=True),
    )
    qkv_w, out_w = (
        lax.all_gather(w_qkv, ("dp", "ctx"), axis=0, tiled=True),
        lax.all_gather(w_out, ("dp", "ctx"), axis=0, tiled=True),
    )
    grad_attn_b = grad_residual.astype(jnp.bfloat16)
    grad_out_w = jnp.dot(mixed_b.T, grad_attn_b, preferred_element_type=jnp.float32)
    grad_mixed_b = (
        jnp.dot(grad_attn_b, out_w.T, preferred_element_type=jnp.float32)
        .astype(jnp.bfloat16)
        .reshape(tok_rows, GROUPS, repeat, HEAD_DIM)
    )
    row_delta = jnp.transpose(
        jnp.sum(grad_mixed_b.astype(jnp.float32) * mixed_f, axis=-1), (1, 2, 0)
    )

    def back_step(grad_query, entries):
        key_blk, place_blk, value_blk = entries
        scores, allowed = score_block(key_blk, place_blk)
        weights_f = jnp.where(allowed, jnp.exp(scores - log_total[..., None]), 0.0)
        weights_b = weights_f.astype(jnp.bfloat16)
        grad_value = jnp.einsum(
            "grij,igrd->jgd", weights_b, grad_mixed_b, preferred_element_type=jnp.float32
        )
        grad_prob = jnp.einsum(
            "igrd,jgd->grij", grad_mixed_b, value_blk, preferred_element_type=jnp.float32
        )
        grad_score = (weights_f * (grad_prob - row_delta[..., None])).astype(jnp.bfloat16)
        grad_query = grad_query + jnp.einsum(
            "grij,jgd->igrd", grad_score, key_blk, preferred_element_type=jnp.float32
        )
        grad_key = (
            jnp.einsum("grij,igrd->jgd", grad_score, query_b, preferred_element_type=jnp.float32)
            * score_scale
        )
        return (
            grad_query,
            jnp.concatenate(
                [
                    grad_key.reshape(tok_rows, GROUPS * HEAD_DIM),
                    grad_value.reshape(tok_rows, GROUPS * HEAD_DIM),
                ],
                axis=1,
            ),
        )

    grad_query, kv_terms = lax.scan(
        back_step,
        jnp.zeros((tok_rows, GROUPS, repeat, HEAD_DIM), jnp.float32),
        (key_blocks, place_blocks, value_blocks),
    )
    grad_query = grad_query * score_scale
    kv_own = lax.psum_scatter(
        kv_terms.reshape(blocks * tok_rows, 2 * GROUPS * HEAD_DIM).astype(jnp.bfloat16),
        "ctx",
        scatter_dimension=0,
        tiled=True,
    ).astype(jnp.float32)
    grad_key_own = kv_own[:, : GROUPS * HEAD_DIM].reshape(tok_rows, GROUPS, HEAD_DIM)
    grad_value_own = kv_own[:, GROUPS * HEAD_DIM :].reshape(tok_rows, GROUPS, HEAD_DIM)
    grad_qkv_f, grad_q_gain, grad_k_gain = pull_heads(
        (grad_query.reshape(tok_rows, HEADS, HEAD_DIM), grad_key_own, grad_value_own)
    )
    grad_qkv_b = grad_qkv_f.astype(jnp.bfloat16)
    grad_qkv_w = jnp.dot(h_attn.T, grad_qkv_b, preferred_element_type=jnp.float32)
    grad_h_attn = jnp.dot(grad_qkv_b, qkv_w.T, preferred_element_type=jnp.float32)
    grad_here_part, grad_attn_gain = pull_attn(grad_h_attn)
    grad_inputs = (grad_residual + grad_here_part).astype(jnp.bfloat16)[None]
    grad_qkv_own, grad_out_own = (
        lax.psum_scatter(grad_qkv_w, ("dp", "ctx"), scatter_dimension=0, tiled=True),
        lax.psum_scatter(grad_out_w, ("dp", "ctx"), scatter_dimension=0, tiled=True),
    )
    gain_attn, gain_query, gain_key, gain_ffn = lax.psum(
        (grad_attn_gain, grad_q_gain, grad_k_gain, grad_ffn_gain), ("dp", "ctx")
    )
    return (
        layer_output,
        grad_inputs,
        gain_attn,
        grad_qkv_own,
        gain_query,
        gain_key,
        grad_out_own,
        gain_ffn,
        grad_gateup_own,
        grad_down_own,
    )


def per_device_fast(
    inputs, places, cotangent, attn_gain, w_qkv, q_gain, k_gain, w_out, ffn_gain, w_gateup, w_down
):
    n_dev = lax.axis_size("ctx")
    own_places = places[0]
    half = HEAD_DIM // 2
    spot = jnp.arange(128)
    frequency = jnp.exp((spot % half).astype(f32) * (-2.0 * math.log(10000.0) / HEAD_DIM))
    angles = own_places.astype(f32)[:, None] * frequency[None, :]
    cosine = jnp.cos(angles)
    sine = jnp.where(spot % HEAD_DIM < half, -1.0, 1.0) * jnp.sin(angles)
    block_row = (own_places // 128)[None, :]
    gain_q, gain_k = jnp.tile(q_gain, 2)[None], jnp.tile(k_gain, 2)[None]
    layer_output, *kept = forward(
        inputs[0], cotangent[0], block_row, cosine, sine, attn_gain[None], gain_q, gain_k,
        ffn_gain[None], w_qkv, w_out, w_down, w_gateup, n_dev,
    )
    rows = [w.shape[0] for w in (w_qkv, w_out, w_gateup, w_down)]
    grad_inputs, *grads = backward(
        inputs[0], cosine, sine, attn_gain[None], gain_q, gain_k, ffn_gain[None], kept, rows, n_dev
    )
    return (layer_output[None], grad_inputs[None], *grads)


def solution(mesh):
    in_specs = (
        P("dp", "ctx", None),
        P("dp", "ctx"),
        P("dp", "ctx", None),
        P(),
        P(("dp", "ctx"), None),
        P(),
        P(),
        P(("dp", "ctx"), None),
        P(),
        P(("dp", "ctx"), None),
        P(("dp", "ctx"), None),
    )
    out_specs = (
        P("dp", "ctx", None),
        P("dp", "ctx", None),
        P(),
        P(("dp", "ctx"), None),
        P(),
        P(),
        P(("dp", "ctx"), None),
        P(),
        P(("dp", "ctx"), None),
        P(("dp", "ctx"), None),
    )
    fast = dict(mesh.shape) == {"dp": 4, "ctx": 8}
    per_device = per_device_fast if fast else per_device_plain
    return jax.shard_map(
        per_device, mesh=mesh, in_specs=in_specs, out_specs=out_specs, check_vma=False
    )
```

profile of v0, /device:TPU:0, one launch (start us, length us, event | category | flops | bytes accessed | tf_op | source)
XLA Modules:
  0.0 369.6 jit_solution(7714673061203372262)
XLA Ops:
  0.6 0.7 tile.4
  1.3 0.6 broadcast_in_dim_tile.6.refs_6_.refs_2_
  1.9 0.7 tile.5
  2.5 0.6 broadcast_in_dim_tile.7.refs_7_.refs_3_
  3.1 1.3 fusion.4
  4.5 1.2 fusion
  5.7 152.7 %forward.1 = (bf16[256,2048]{1,0:T(8,128)(2,1)}, bf16[16,64,512]{2,1,0:T(8,128)(2,1)}, bf16[16,32,512]{2,1,0:T(8,128)(2,1)}, bf16[16,64,512]{2,1,0:T(8,128)(2,1)...) custom-call(bf16[256,2048]{1,0:T(8,128)(2,1)} %bitcast.17, ...), custom_call_target="tpu_custom_call" | custom-call | flops 9126805504 | bytes 52428800 | tf_op jit(solution)/shard_map/forward/pallas_call | solution.py:808
  158.5 139.2 %backward.1 = (bf16[512,1536]{1,0:T(8,128)(2,1)}, f32[256,2048]{1,0:T(8,128)}, f32[8,2048]{1,0:T(8,128)}, f32[32,2048]{1,0:T(8,128)}, f32[64,2048]{1,0:T(8,128)}, /*index=5*/f32[32,2048]{1,0:T(8,128)}) custom-call(f32[256,128]{1,0:T(8,128)} %get-tuple-element.71.refs_3_.refs_0_, f32[256,128]{1,0:T(8,128)} %get-tuple-element.70.refs_4_.refs_1_, ...), custom_call_target="tpu_custom_call" | custom-call | flops 21474836480 | bytes 62914560 | tf_op jit(solution)/shard_map/backward/pallas_call | solution.py:1491
  297.7 64.1 %last.1 = (bf16[256,2048]{1,0:T(8,128)(2,1)}, f32[1,2048]{1,0:T(1,128)}, f32[1,64]{1,0:T(1,128)}, f32[1,64]{1,0:T(1,128)}, f32[1,2048]{1,0:T(1,128)}, /*index=5*/f32[64,1536]{1,0:T(8,128)}) custom-call(bf16[256,2048]{1,0:T(8,128)(2,1)} %bitcast.18, f32[1,2048]{1,0:T(1,128)} %bitcast.22, bf16[512,1536]{1,0:T(8,128)(2,1)} %get-tuple-element.56.refs_2_, ...), custom_call_target="tpu_custom_call" | custom-call | flops 6442450944 | bytes 20971520 | tf_op jit(solution)/shard_map/last/pallas_call | solution.py:1532
  361.8 0.0 copy-start.1
  361.8 0.0 copy-done
  361.8 0.0 copy-start.7
  361.8 0.0 copy-start.3
  361.9 1.0 copy.31
  362.9 0.6 copy-done.1
  363.4 1.0 copy.32
  364.4 0.6 copy.33
  365.0 0.7 copy.34
  365.7 0.5 copy.35
  366.3 0.5 copy.36
  366.8 0.7 copy.37
  367.5 0.6 copy.38
  368.1 0.8 copy.39
  368.9 0.7 copy.40
  (16 shorter events, 0.0 us)
Async XLA Ops:
  297.7 64.1 %copy-start = (bf16[256,2048]{1,0:T(8,128)(2,1)S(1)}, bf16[256,2048]{1,0:T(8,128)(2,1)}, u32[]{:S(2)}) copy-start(bf16[256,2048]{1,0:T(8,128)(2,1)} %get-tuple-element.40) | copy-start | bytes 3145732
  361.8 1.6 copy-start.1
  361.8 2.6 copy-start.7
  361.8 3.2 copy-start.3
  361.8 3.9 %copy-start.9 = (f32[1,64]{1,0:T(1,128)S(1)}, f32[1,64]{1,0:T(1,128)}, u32[]{:S(2)}) copy-start(f32[1,64]{1,0:T(1,128)} %get-tuple-element.64) | copy-start | bytes 772
  361.9 4.4 %copy-start.8 = (f32[1,64]{1,0:T(1,128)S(1)}, f32[1,64]{1,0:T(1,128)}, u32[]{:S(2)}) copy-start(f32[1,64]{1,0:T(1,128)} %get-tuple-element.65) | copy-start | bytes 772
  361.9 4.9 %copy-start.5 = (f32[32,2048]{1,0:T(8,128)S(1)}, f32[32,2048]{1,0:T(8,128)}, u32[]{:S(2)}) copy-start(f32[32,2048]{1,0:T(8,128)} %get-tuple-element.92) | copy-start | bytes 786436
  363.4 4.1 %copy-start.6 = (f32[1,2048]{1,0:T(1,128)S(1)}, f32[1,2048]{1,0:T(1,128)}, u32[]{:S(2)}) copy-start(f32[1,2048]{1,0:T(1,128)} %get-tuple-element.67) | copy-start | bytes 24580
  363.4 4.7 %copy-start.2 = (f32[64,2048]{1,0:T(8,128)S(1)}, f32[64,2048]{1,0:T(8,128)}, u32[]{:S(2)}) copy-start(f32[64,2048]{1,0:T(8,128)} %get-tuple-element.94) | copy-start | bytes 1572868
  363.4 5.5 %copy-start.4 = (f32[32,2048]{1,0:T(8,128)S(1)}, f32[32,2048]{1,0:T(8,128)}, u32[]{:S(2)}) copy-start(f32[32,2048]{1,0:T(8,128)} %get-tuple-element.95) | copy-start | bytes 786436
where the time goes:
time: 370 us
  Pallas kernels  356 us (96%)
  local copies, waits for them, and re-layouts  10.2 us (3%)
    pallas_call x1, Pallas kernels, forward(): pl.pallas_call(functools.partial(forward_kernel, (tok, width, n_dev, head...  153 us
    pallas_call x1, Pallas kernels, backward(): pl.pallas_call(functools.partial(backward_kernel, dims), out_shape=[shape...  139 us
    pallas_call x1, Pallas kernels, backward(): pl.pallas_call(functools.partial(last_kernel, dims), out_shape=[shape((to...  64.1 us
    unnamed x30, local copies, waits for them, and re-layouts  7.71 us

commit v1 on v0

--- a/solution.py
+++ b/solution.py
@@ -12,6 +12,38 @@
 GROUPS = 4
 HEAD_DIM = 64
 FF = 1024
+
+
+FORWARD_ORDER = [
+    "qp0", "qZ", "norm", "dp0", "qz1", "qe0", "qp1", "qz2", "gZ", "qp2", "qc0", "qe1", "oP",
+    "qz3", "qp3", "qe2", "gz1", "qs0", "gz2", "oZ", "qe3", "oe", "dZ", "qc1", "qc2", "gp2", "qc3",
+    "qs1", "qs2", "oD", "qs3", "oz12", "keys", "de0", "turn", "oz22", "kve", "gp1", "gz3", "gp0",
+    "dz1", "query", "kvc", "dp1", "oz32", "ge2", "unpack", "gp3", "oz10", "dz2", *["A"] * 3,
+    "oz20", *["A"] * 4, "oz30", *["A"] * 5, "dp2", "oz11", "ge0", "dz3", *["A"] * 3, "dc0",
+    "oz13", "ge1", "oz23", *["A"] * 5, "oz21", "de1", "A", "oc1", "gc2", *["A"] * 4, "oc2", "A",
+    "dp3", "oz31", *["A"] * 3, "oz33", "oc3", *["A"] * 2, "gc0", "A", "mix", "de2", "dc1", "ds0",
+    "res", "ge3", "de3", "gc1", "norm2", "dc2", "gc3", "gs0", "gs1", "dc3", "ds1", "ds2", "gs2",
+    "turn2", "gs3", "ds3", "gate", "act", "y",
+]
+
+BACKWARD_ORDER = [
+    "dw0", "dw1", "gw0", "gw1", "dw2", "dw3", "h", *["H"] * 6, "ga0", *["H"] * 2, "nb", "gw2",
+    "db1", "gw3", "da1", "m", "att", "ow0", "ga2", "ga1", "oa0", "B", "ow1", "da2", "oa1", "dd1",
+    "ow2", "gb0", "oa2", "da0", *["B"] * 2, "db2", "B", "oz00", *["B"] * 2, "dd2", *["B"] * 3,
+    "gb1", *["B"] * 2, "gb2", "dd0", "dx1", *["B"] * 2, "oz02", "ga3", "oz10", "oz12", "db0", "B",
+    "gd2", "oz22", *["B"] * 2, "gd1", "B", "gb3", "oz20", "B", "oz03", *["B"] * 2, "oz01", "B",
+    "oz13", "dx0", *["B"] * 2, "oz23", "dz0", *["B"] * 2, "dx2", "gd0", "dz1", "B", "gd3",
+    *["B"] * 2, "dz2", "gx2", "da3", "gx0", *["B"] * 4, "kvs", "db3", "oz11", "dd3", "gx1", "gz0",
+    "Q", "kvc", "oz21", "ow3", "oa3", "oo0", "gz1", "kve", "oo3", "df", "gz2", "Q", "oo2", "Q",
+    "oo1", *["Q"] * 2, "oS", *["Q"] * 3, "kvf", "oe", "of", "gf",
+]
+
+LAST_ORDER = [
+    "qw0", "qa0", "qw1", "qa1", "qb0", "qw2", "h", *["H"] * 2, "qd0", "H", "qb1", "H", "qa2",
+    *["H"] * 2, "qd1", "H", "qb2", "H", "nb", "qx0", "qz0", "qd2", "hs0", "qw3", "he0", "hs1",
+    "qa3", "qx1", "qz1", "qx2", "qz2", "he1", "hs2", "qb3", "qd3", "he2", "rs", "qf", "re",
+]
+
 f32 = jnp.float32
 bf16 = jnp.bfloat16
 MESH = pl.DeviceIdType.MESH
@@ -427,13 +459,46 @@
     lax.fori_loop(0, src.shape[0] // 32, body, 0)
 
 
-def ticked(tick, first, events):
-    for k, event in enumerate(events):
-        if event is not None:
-
-            @pl.when(tick == first + k)
-            def _(event=event):
-                event()
+def run_steps(order, steps, loops):
+    order = list(order)
+    while order:
+        name = order.pop(0)
+        if name not in loops:
+            steps[name]()
+            continue
+        count, body = loops[name]
+        ticks, seen = {}, 1
+        while seen < count:
+            inner = order.pop(0)
+            if inner == name:
+                seen += 1
+            else:
+                ticks.setdefault(seen - 1, []).append(inner)
+
+        def tick(i, _, body=body, ticks=ticks):
+            body(i)
+            for k, inner in ticks.items():
+
+                @pl.when(i == k)
+                def _(inner=inner):
+                    for step in inner:
+                        steps[step]()
+
+            return 0
+
+        lax.fori_loop(0, count, tick, 0)
+
+
+def line_steps(letter, g):
+    part = functools.partial
+    steps = {letter + "Z": g.own_z}
+    for i in range(NZ):
+        steps[f"{letter}p{i}"] = part(g.plane_send, i)
+        steps[f"{letter}e{i}"] = part(g.plane_event, i)
+        steps[f"{letter}c{i}"] = part(g.core_event, i)
+        if i:
+            steps[f"{letter}z{i}"] = part(g.z_event, i, False)
+    return steps
 
 
 def turn(src, rows, core, mine, theirs):
@@ -499,57 +564,36 @@
     sent_act = exchange(4, turn_b.at[:, pl.ds(0, s_down.shape[0]), :], t_act.at[:, :, back])
     sent_ggu = exchange(5, ggu2.at[pl.ds(0, tok), :], ggu2.at[back, :])
 
-    qkv.own_z()
-    qkv.plane_send(0)
-    norm_into(x_ref, g_attn, hattn_ref)
-    qkv.z_event(1)
-    sent_cot.start()
-    cot2[pl.ds(0, tok), :] = cot_ref[...]
-    turn(hattn_ref, s_qkv.shape[0], pc.core, t_attn, turn_a)
-    sent_attn.start()
-    qkv.plane_event(0)
-    qkv.z_event(2)
-    out.own_plane()
-    out.own_z()
-    down.own_z()
-    gateup.own_z()
-    qkv.z_event(3)
-    qkv.plane_event(1)
-    qkv.core_event(0)
-    down.plane_send(0)
-    gateup.plane_send(0)
-    qkv.plane_event(2)
-    qkv.core_event(1)
-    down.z_event(1)
-    gateup.z_event(1)
-    qkv.plane_event(3)
-    out.plane_event()
-
-    def qkv_step(i):
-        qkv.done_event(i)
+    def first_norm():
+        norm_into(x_ref, g_attn, hattn_ref)
+
+    def first_turn():
+        sent_cot.start()
+        cot2[pl.ds(0, tok), :] = cot_ref[...]
+        turn(hattn_ref, s_qkv.shape[0], pc.core, t_attn, turn_a)
+        sent_attn.start()
+
+    def columns_step(g, i, left, right, total, depth):
+        g.done_event(i)
         z0 = near(z, i)
-        depth = width // NZ
 
         def body(n, _):
             c = cols(n, 256)
-            w = w_qkv[z0, :, :, :, :, c].reshape(depth, 256)
-            prod = dot(hattn_ref[:, cols(z0, depth)], w)
+            w = right[z0, :, :, :, :, c].reshape(depth, 256)
+            prod = dot(left[:, cols(z0, depth)], w)
             if i == 0:
-                qkv_ref[:, c] = prod
+                total[:, c] = prod
             else:
-                qkv_ref[:, c] += prod
+                total[:, c] += prod
             return 0
 
-        lax.fori_loop(0, qkv_ref.shape[1] // 256, body, 0)
-
-    qkv_step(0)
-    qkv.core_event(2)
-    qkv_step(1)
-    qkv.core_event(3)
-    down.plane_event(0)
-    gateup.plane_event(0)
-    qkv_step(2)
-    qkv_step(3)
+        lax.fori_loop(0, total.shape[1] // 256, body, 0)
+
+    def grad_act_step(i):
+        down.done_event(i)
+        z0 = near(z, i)
+        depth = ff // NZ
+        gact[:, cols(z0, depth)] = dot_t(cot_ref[...], w_down[z0].reshape(depth, width))
 
     low = lanes((tok, 128)) < 64
 
@@ -558,17 +602,18 @@
         n = u * lax.rsqrt(head_sums(u * u) * (1.0 / 64) + EPS) * gain[...]
         return n * cos_ref[...] + swap_rot(n) * sin_ref[...]
 
-    for t in range(kv_w // 128):
-        kvb[pc.y, pc.x, pc.core, pl.ds(0, tok), pl.ds(t * 128, 128)] = head_tile(
-            heads_w // 128 + t, g_k
-        ).astype(bf16)
-    kvb[pc.y, pc.x, pc.core, pl.ds(0, tok), pl.ds(kv_w, kv_w)] = qkv_ref[
-        :, pl.ds(heads_w + kv_w, kv_w)
-    ].astype(bf16)
-    blocks_row = jnp.broadcast_to(hi_ref[...], (16, tok)).astype(bf16)
-    kvb[pc.y, pc.x, pc.core, pl.ds(tok, 16), pl.ds(0, tok)] = blocks_row
-    kvb[pc.y, pc.x, pc.core, pl.ds(tok, 16), pl.ds(tok, tok)] = blocks_row
-    seq.own()
+    def keys_out():
+        for t in range(kv_w // 128):
+            kvb[pc.y, pc.x, pc.core, pl.ds(0, tok), pl.ds(t * 128, 128)] = head_tile(
+                heads_w // 128 + t, g_k
+            ).astype(bf16)
+        kvb[pc.y, pc.x, pc.core, pl.ds(0, tok), pl.ds(kv_w, kv_w)] = qkv_ref[
+            :, pl.ds(heads_w + kv_w, kv_w)
+        ].astype(bf16)
+        blocks_row = jnp.broadcast_to(hi_ref[...], (16, tok)).astype(bf16)
+        kvb[pc.y, pc.x, pc.core, pl.ds(tok, 16), pl.ds(0, tok)] = blocks_row
+        kvb[pc.y, pc.x, pc.core, pl.ds(tok, 16), pl.ds(tok, tok)] = blocks_row
+        seq.own()
 
     def query_tile(t, _):
         q = (head_tile(t, g_q) * 0.125).astype(bf16)
@@ -577,29 +622,15 @@
         q2_ref[t, pl.ds(tok, tok), :] = jnp.where(low, zero, q)
         return 0
 
-    lax.fori_loop(0, heads_w // 128, query_tile, 0)
-    emit(qkv_ref, o_kv)
-    emit(q2_ref, o_q2)
-    emit(w_qkv, o_wqkv)
-    sent_cot.wait_recv()
-    emit(cot2, o_cot)
-    sent_attn.wait_recv()
-    emit(t_attn, o_tattn)
-
-    down.z_event(2)
-    gateup.z_event(2)
-    out.diag_event()
-    down.plane_event(1)
-    gateup.plane_event(1)
-    seq.plane_event()
-    down.z_event(3)
-    for j in range(4):
-        out.z_event(1, j)
-    gateup.z_event(3)
-    down.core_event(0)
-    gateup.core_event(0)
-    seq.core_event()
-    seq.done_event()
+    def queries():
+        lax.fori_loop(0, heads_w // 128, query_tile, 0)
+        emit(qkv_ref, o_kv)
+        emit(q2_ref, o_q2)
+        emit(w_qkv, o_wqkv)
+        sent_cot.wait_recv()
+        emit(cot2, o_cot)
+        sent_attn.wait_recv()
+        emit(t_attn, o_tattn)
 
     def unpack(b, _):
         y, x, c = b // 4, (b // 2) % 2, b % 2
@@ -627,23 +658,17 @@
                 mask_t[place, pl.ds(a * step, step)] = jnp.where(gap >= 0, 1.0, 0.0).astype(bf16)
         return 0
 
-    lax.fori_loop(0, n_dev, unpack, 0)
-    emit(kk, o_kk)
-    emit(va, o_va)
-    emit(mask_t, o_mask)
-
-    events = [part(out.z_event, 2, j) for j in range(4)] + [
-        part(out.core_event, 1), part(down.plane_event, 2), part(gateup.plane_event, 2),
-        part(down.core_event, 1), part(gateup.core_event, 1),
-    ] + [part(out.z_event, 3, j) for j in range(4)] + [
-        part(out.core_event, 2),
-        part(down.plane_event, 3), part(gateup.plane_event, 3),
-        part(down.core_event, 2), part(gateup.core_event, 2), part(out.core_event, 3),
-    ]
+    def unpack_all():
+        seq.done_event()
+        lax.fori_loop(0, n_dev, unpack, 0)
+        emit(kk, o_kk)
+        emit(va, o_va)
+        emit(mask_t, o_mask)
+
     chunk = 512
     n_chunk = n_dev * tok // chunk
 
-    def attend(tick, _):
+    def attend(tick):
         t, kc = tick // n_chunk, tick % n_chunk
         g = t // 2
         rows = pl.ds(pl.multiple_of(kc * chunk, chunk), chunk)
@@ -669,18 +694,11 @@
             mixf_ref[:, cols(t, 128)] = mixed
             mixb_ref[:, cols(t, 128)] = mixed.astype(bf16)
 
-        ticked(tick, 2, events)
-        return 0
-
-    lax.fori_loop(0, heads_w // 128 * n_chunk, attend, 0)
-
-    emit(linv_ref, o_linv)
-    emit(mixf_ref, o_mixf)
-    turn(mixb_ref, s_out.shape[0], pc.core, t_mix, turn_b)
-    sent_mix.start()
-    for i in range(NZ):
-        out.done_event(i)
-    emit(w_out, o_wout)
+    def mix_out():
+        emit(linv_ref, o_linv)
+        emit(mixf_ref, o_mixf)
+        turn(mixb_ref, s_out.shape[0], pc.core, t_mix, turn_b)
+        sent_mix.start()
 
     def residual_step(n, _):
         c = cols(n, 256)
@@ -688,48 +706,22 @@
         res_ref[:, c] = x_ref[:, c].astype(f32) + dot(mixb_ref[...], w)
         return 0
 
-    lax.fori_loop(0, width // 256, residual_step, 0)
-    norm_into(res_ref, g_ffn, hffn_ref)
-    emit(res_ref, o_res)
-    sent_mix.wait_recv()
-    emit(t_mix, o_tmix)
-    sent_attn.wait_send()
-    turn(hffn_ref, s_gu.shape[0], pc.core, t_ffn, turn_a)
-    sent_ffn.start()
-
-    def gateup_step(i):
-        gateup.done_event(i)
-        z0 = near(z, i)
-        depth = width // NZ
-
-        def body(n, _):
-            c = cols(n, 256)
-            w = w_gu[z0, :, :, :, :, c].reshape(depth, 256)
-            prod = dot(hffn_ref[:, cols(z0, depth)], w)
-            if i == 0:
-                gu[:, c] = prod
-            else:
-                gu[:, c] += prod
-            return 0
-
-        lax.fori_loop(0, 2 * ff // 256, body, 0)
-
-    def grad_act_step(i):
-        down.done_event(i)
-        z0 = near(z, i)
-        depth = ff // NZ
-        gact[:, cols(z0, depth)] = dot_t(cot_ref[...], w_down[z0].reshape(depth, width))
-
-    gateup_step(0)
-    grad_act_step(0)
-    gateup_step(1)
-    grad_act_step(1)
-    down.core_event(3)
-    gateup_step(2)
-    grad_act_step(2)
-    gateup.core_event(3)
-    grad_act_step(3)
-    gateup_step(3)
+    def residual():
+        for i in range(NZ):
+            out.done_event(i)
+        emit(w_out, o_wout)
+        lax.fori_loop(0, width // 256, residual_step, 0)
+
+    def second_norm():
+        norm_into(res_ref, g_ffn, hffn_ref)
+
+    def second_turn():
+        emit(res_ref, o_res)
+        sent_mix.wait_recv()
+        emit(t_mix, o_tmix)
+        sent_attn.wait_send()
+        turn(hffn_ref, s_gu.shape[0], pc.core, t_ffn, turn_a)
+        sent_ffn.start()
 
     def gate_step(n, _):
         c = cols(n, 256)
@@ -742,14 +734,17 @@
         ggu2[pl.ds(0, tok), c2] = (grad * silu).astype(bf16)
         return 0
 
-    lax.fori_loop(0, ff // 256, gate_step, 0)
-    sent_ggu.start()
-    sent_mix.wait_send()
-    turn(act_ref, s_down.shape[0], pc.core, t_act, turn_b)
-    sent_act.start()
-    emit(w_gu, o_wgu)
-    sent_ffn.wait_recv()
-    emit(t_ffn, o_tffn)
+    def gates():
+        lax.fori_loop(0, ff // 256, gate_step, 0)
+        sent_ggu.start()
+        emit(w_gu, o_wgu)
+
+    def act_out():
+        sent_mix.wait_send()
+        turn(act_ref, s_down.shape[0], pc.core, t_act, turn_b)
+        sent_act.start()
+        sent_ffn.wait_recv()
+        emit(t_ffn, o_tffn)
 
     def output_step(n, _):
         c = cols(n, 256)
@@ -757,12 +752,32 @@
         y_ref[:, c] = (res_ref[:, c] + dot(act_ref[...], w)).astype(bf16)
         return 0
 
-    lax.fori_loop(0, width // 256, output_step, 0)
-    emit(y_ref, o_y)
-    sent_ggu.wait_recv()
-    emit(ggu2, o_ggu)
-    sent_act.wait_recv()
-    emit(t_act, o_tact)
+    def outputs():
+        lax.fori_loop(0, width // 256, output_step, 0)
+        emit(y_ref, o_y)
+        sent_ggu.wait_recv()
+        emit(ggu2, o_ggu)
+        sent_act.wait_recv()
+        emit(t_act, o_tact)
+
+    steps = {
+        "norm": first_norm, "turn": first_turn, "keys": keys_out, "query": queries,
+        "kve": seq.plane_event, "kvc": seq.core_event, "unpack": unpack_all, "mix": mix_out,
+        "res": residual, "norm2": second_norm, "turn2": second_turn, "gate": gates,
+        "act": act_out, "y": outputs, "oP": out.own_plane, "oZ": out.own_z, "oe": out.plane_event,
+        "oD": out.diag_event,
+    }
+    for letter, g in (("q", qkv), ("d", down), ("g", gateup)):
+        steps.update(line_steps(letter, g))
+    for i in range(NZ):
+        steps[f"qs{i}"] = part(columns_step, qkv, i, hattn_ref, w_qkv, qkv_ref, width // NZ)
+        steps[f"gs{i}"] = part(columns_step, gateup, i, hffn_ref, w_gu, gu, width // NZ)
+        steps[f"ds{i}"] = part(grad_act_step, i)
+        if i:
+            steps[f"oc{i}"] = part(out.core_event, i)
+            for k in range(4):
+                steps[f"oz{i}{k}"] = part(out.z_event, i, k)
+    run_steps(FORWARD_ORDER, steps, {"A": (heads_w // 128 * n_chunk, attend)})
     for g in (qkv, out, down, gateup, seq):
         g.finish()
     for c in (sent_cot, sent_ffn, sent_act, sent_ggu):
@@ -884,9 +899,17 @@
     def y1(self, s):
         return self.cp(self.rd.at[s, 1], self.ry.at[s, 1], self.pc.yn(), SY1, s)
 
+    def plane_far(self, s):
+        self.d0(s).start()
+        self.d1(s).start()
+
+    def plane_near(self, s):
+        self.x1(s).start()
+        self.y0(s).start()
+
     def plane_first(self, s):
-        for c in (self.d0, self.d1, self.x1, self.y0):
-            c(s).start()
+        self.plane_far(s)
+        self.plane_near(s)
 
     def plane_second(self, s):
         p = self.pc
@@ -934,8 +957,11 @@
         spot = zp + (1 - (gap + NZ - 1) // NZ) * (NZ - zp)
         return self.cp(self.rx.at[zp], self.zz.at[spot], self.pc.up(), SB, zp)
 
-    def first(self, i):
-        self.plane_first(far(self.pc.z, i))
+    def far_event(self, i):
+        self.plane_far(far(self.pc.z, i))
+
+    def near_event(self, i):
+        self.plane_near(far(self.pc.z, i))
 
     def d_event(self, i):
         self.plane_second(far(self.pc.z, i))
@@ -1156,6 +1182,19 @@
     lax.fori_loop(0, src.shape[0] // 32, body, 0)
 
 
+def sum_steps(letter, g):
+    part = functools.partial
+    steps = {letter + "f": g.final}
+    for i in range(NZ):
+        steps[f"{letter}a{i}"] = part(g.far_event, i)
+        steps[f"{letter}b{i}"] = part(g.near_event, i)
+        steps[f"{letter}d{i}"] = part(g.d_event, i)
+        if i < NZ - 1:
+            steps[f"{letter}x{i}"] = part(g.xy_event, i)
+            steps[f"{letter}z{i}"] = part(g.z_event, i)
+    return steps
+
+
 def weight_grad(left, zp, right, part):
     rows, columns = part.shape[-2:]
     lhs = left[pl.ds(zp * 4, 4)].reshape(4 * rows, left.shape[-1])
@@ -1167,6 +1206,12 @@
         return 0
 
     lax.fori_loop(0, columns // step, body, 0)
+
+
+LOADS = [
+    "act", "cot", "ffn", "ggu", "wgu", "res", "mix", "mixf", "linv", "q2", "kk", "va", "mask",
+    "qkv", "wout",
+]
 
 
 def backward_kernel(dims, *refs):
@@ -1187,7 +1232,7 @@
     loads = {}
 
     def load(name, src, dst):
-        c = pltpu.make_async_copy(src, dst, lsem.at[len(loads)])
+        c = pltpu.make_async_copy(src, dst, lsem.at[LOADS.index(name)])
         loads[name] = c
         c.start()
 
@@ -1211,76 +1256,54 @@
     out = ScatterZ(pc, part_out, bufs[8:13], out_wout, send.at[2], recv.at[2])
     seq = SequenceSum(pc, terms, bufs[13:17], kv_send, kv_recv, ex_send.at[2], ex_recv.at[2])
 
-    loads["act"].wait()
-    loads["cot"].wait()
-    for i in range(NZ):
-        weight_grad(t_act, far(z, i), cot2, part_down)
-        down.first(i)
-    loads["ffn"].wait()
-    loads["ggu"].wait()
-    for i in range(NZ):
-        weight_grad(t_ffn, far(z, i), ggu2, part_gu)
-        gateup.first(i)
-        if i == 2:
-            down.d_event(0)
     own = pl.ds(0, tok)
     back = pl.ds(tok, tok)
-    loads["wgu"].wait()
-    first_events = [part(gateup.d_event, 0), None, part(down.d_event, 1), None, part(down.xy_event, 0),
-                    part(down.z_event, 0), None, None]
-
-    def h_step(n, _):
+
+    def rows_of(left, right, term, names, i):
+        for name in names:
+            if name in loads:
+                loads.pop(name).wait()
+        weight_grad(left, far(z, i), right, term)
+
+    def h_step(n):
         w = w_gu[n // 2, n % 2].reshape(width // 8, 2 * ff)
         gh[:, cols(n, width // 8)] = dot_t(ggu2[own, :], w)
-        ticked(n, 0, first_events)
-        return 0
-
-    lax.fori_loop(0, 8, h_step, 0)
-    load("wout", i_wout, w_gu.at[:, :, :, :, pl.ds(0, part_out.shape[-2]), :])
-    loads["res"].wait()
+
+    def start_h():
+        loads.pop("wgu").wait()
+        loads.pop("res").wait()
 
     def keep_residual(rows, grad):
         total = cot2[rows, :].astype(f32) + grad
         res[rows, :] = total
         gattn2[rows, :] = total.astype(bf16)
 
-    gains[...] = jnp.zeros_like(gains)
-    norm_back(res, g_ffn, gh, gains, 1, keep_residual)
     sent_attn = remote(gattn2.at[own, :], gattn2.at[back, :], pc.sn(), ex_send.at[0], ex_recv.at[0])
-    sent_attn.start()
-    gateup.d_event(1)
-    loads["wout"].wait()
+
+    def residual_back():
+        load("wout", i_wout, w_gu.at[:, :, :, :, pl.ds(0, part_out.shape[-2]), :])
+        gains[...] = jnp.zeros_like(gains)
+        norm_back(res, g_ffn, gh, gains, 1, keep_residual)
+        sent_attn.start()
+        loads.pop("wout").wait()
 
     def m_step(n, _):
         w = w_gu[n, :, :, :, pl.ds(0, part_out.shape[-2]), :].reshape(heads_w // NZ, width)
         gm[:, cols(n, heads_w // NZ)] = dot_t(gattn2[own, :], w).astype(bf16)
         return 0
 
-    lax.fori_loop(0, NZ, m_step, 0)
-    sent_attn.wait_recv()
-    loads["mix"].wait()
-    for i in range(NZ):
-        weight_grad(t_mix, far(z, i), gattn2, part_out)
-        out.first(i)
-    gateup.xy_event(0)
-    gateup.z_event(0)
-    down.d_event(2)
-    down.xy_event(1)
-    for name in ("mixf", "linv", "q2", "kk", "va", "mask", "qkv"):
-        loads[name].wait()
+    def mixed_back():
+        lax.fori_loop(0, NZ, m_step, 0)
+        sent_attn.wait_recv()
+
+    def start_attention():
+        for name in ("mixf", "linv", "q2", "kk", "va", "mask", "qkv"):
+            loads.pop(name).wait()
 
     low = lanes((tok, 128)) < 64
     chunk = 512
     n_chunk = n_dev * tok // chunk
-    events = [
-        part(down.z_event, 1), part(gateup.d_event, 2), part(gateup.xy_event, 1),
-        part(gateup.z_event, 1), part(down.d_event, 3), part(down.xy_event, 2),
-        part(down.z_event, 2),
-    ] + [part(out.z_event, 0, k) for k in range(4)] + [
-        part(gateup.d_event, 3), part(gateup.xy_event, 2), part(gateup.z_event, 2),
-    ] + [part(out.z_event, 1, k) for k in range(4)] + [part(out.z_event, 2, k) for k in range(4)]
-
-    def attend(tick, _):
+    def attend(tick):
         t, kc = tick // n_chunk, tick % n_chunk
         g = t // 2
         rows = pl.ds(pl.multiple_of(kc * chunk, chunk), chunk)
@@ -1342,11 +1365,6 @@
             turned = jnp.transpose(acc_q[...])
             gh[:, cols(t, 128)] = jnp.where(low, turned[:tok], turned[tok:]) * 0.125
 
-        ticked(tick, 1, events)
-        return 0
-
-    lax.fori_loop(0, heads_w // 128 * n_chunk, attend, 0)
-    seq.swap().start()
 
     def head_back(t, grad, gain, row):
         c = cols(t, 128)
@@ -1358,30 +1376,42 @@
         gg = grad * gain[...]
         gqkv2[own, c] = (inv * (gg - unit * head_sums(gg * unit) * (1.0 / 64))).astype(bf16)
 
-    def query_back(t, _):
+    def query_back(t):
         head_back(t, gh[:, cols(t, 128)], g_q, 2)
-        return 0
-
-    lax.fori_loop(0, heads_w // 128 // 2, query_back, 0)
-    seq.core_event()
-    lax.fori_loop(heads_w // 128 // 2, heads_w // 128, query_back, 0)
-    for k in range(4):
-        out.own_event(k)
-    seq.plane_second(0)
-    out.plane_send()
-    down.final()
-    seq.plane_arrived(0)
-    for k in range(2):
-        rows = seq.h[k]
-        gh[rows, pl.ds(0, 2 * kv_w)] = seq.plane_total(0, k)
-    for t in range(kv_w // 128):
-        head_back(heads_w // 128 + t, gh[:, pl.ds(t * 128, 128)], g_k, 3)
-    gqkv2[own, pl.ds(heads_w + kv_w, kv_w)] = gh[:, pl.ds(kv_w, kv_w)].astype(bf16)
+
     sent_qkv = remote(gqkv2.at[own, :], gqkv2.at[back, :], pc.sn(), ex_send.at[1], ex_recv.at[1])
-    sent_qkv.start()
-    out.plane_event()
-    gateup.final()
-    out.final()
+
+    def keys_back():
+        seq.plane_arrived(0)
+        for k in range(2):
+            gh[seq.h[k], pl.ds(0, 2 * kv_w)] = seq.plane_total(0, k)
+        for t in range(kv_w // 128):
+            head_back(heads_w // 128 + t, gh[:, pl.ds(t * 128, 128)], g_k, 3)
+        gqkv2[own, pl.ds(heads_w + kv_w, kv_w)] = gh[:, pl.ds(kv_w, kv_w)].astype(bf16)
+        sent_qkv.start()
+
+    steps = {
+        "h": start_h, "nb": residual_back, "m": mixed_back, "att": start_attention,
+        "kvs": seq.swap().start, "kvc": seq.core_event, "kve": part(seq.plane_second, 0),
+        "kvf": keys_back, "oS": out.plane_send, "oe": out.plane_event, "of": out.final,
+    }
+    steps.update(sum_steps("d", down))
+    steps.update(sum_steps("g", gateup))
+    for i in range(NZ):
+        steps[f"dw{i}"] = part(rows_of, t_act, cot2, part_down, ("act", "cot"), i)
+        steps[f"gw{i}"] = part(rows_of, t_ffn, ggu2, part_gu, ("ffn", "ggu"), i)
+        steps[f"ow{i}"] = part(rows_of, t_mix, gattn2, part_out, ("mix",), i)
+        steps[f"oa{i}"] = part(out.first, i)
+        steps[f"oo{i}"] = part(out.own_event, i)
+        if i < NZ - 1:
+            for k in range(4):
+                steps[f"oz{i}{k}"] = part(out.z_event, i, k)
+    loops = {
+        "H": (8, h_step),
+        "B": (heads_w // 128 * n_chunk, attend),
+        "Q": (heads_w // 128, query_back),
+    }
+    run_steps(BACKWARD_ORDER, steps, loops)
     sent_qkv.wait_recv()
     for g in (down, gateup, out, seq):
         g.finish()
@@ -1413,63 +1443,60 @@
     pl.semaphore_wait(bar, 3 + NZ - 1)
     qkv = Scatter(pc, part_qkv, refs[24:28], out_wqkv, send, recv)
     load_t.wait()
-    for i in range(NZ):
-        weight_grad(t_attn, far(z, i), gqkv2, part_qkv)
-        qkv.first(i)
-    load_w.wait()
     columns = w_qkv.shape[-1]
-    events = [None, None, part(qkv.d_event, 0), None, None, part(qkv.d_event, 1), part(qkv.xy_event, 0),
-              part(qkv.z_event, 0)]
-
-    def h_step(n, _):
+
+    def h_step(n):
         w = w_qkv[n // 2, n % 2].reshape(width // 8, columns)
         gh[:, cols(n, width // 8)] = dot_t(gqkv2[pl.ds(0, tok), :], w)
-        ticked(n, 0, events)
-        return 0
-
-    lax.fori_loop(0, 8, h_step, 0)
 
     def keep_input(rows, grad):
         dx[rows, :] = (res[rows, :] + grad).astype(bf16)
 
-    held[...] = gains[...]
-    norm_back(x_ref, g_attn, gh, held, 0, keep_input)
-
-    def hop(k, device):
+    def input_back():
+        held[...] = gains[...]
+        norm_back(x_ref, g_attn, gh, held, 0, keep_input)
+
+    def hop(k):
+        device = (pc.sn(), pc.xn(), pc.yn())[k]
         return remote(held, came.at[k], device, g_send.at[k], g_recv.at[k])
 
-    hops = [hop(0, pc.sn()), hop(1, pc.xn()), hop(2, pc.yn())]
-    between = [
-        [part(qkv.d_event, 2), part(qkv.xy_event, 1), part(qkv.z_event, 1)],
-        [part(qkv.d_event, 3), part(qkv.xy_event, 2), part(qkv.z_event, 2)],
-        [],
-    ]
-    for k, c in enumerate(hops):
-        c.start()
-        for event in between[k]:
-            event()
-        c.wait()
+    def hop_end(k):
+        hop(k).wait()
         held[...] += came[k]
-    came[3 + z] = held[...]
-    ring = []
+
+    def ring(k):
+        there = pc.at(z=(z + k) % NZ)
+        return remote(held, came.at[3 + z], there, g_send.at[2 + k], g_recv.at[3 + z])
+
+    def ring_start():
+        came[3 + z] = held[...]
+        for k in range(1, NZ):
+            ring(k).start()
+
+    def ring_end():
+        for k in range(1, NZ):
+            there = (z + k) % NZ
+            slot = came.at[3 + there]
+            remote(held, slot, pc.at(z=there), g_send.at[2 + k], g_recv.at[3 + there]).wait_recv()
+        total = came[3]
+        for k in range(1, NZ):
+            total = total + came[3 + k]
+        o_attn[...] = total[0:1]
+        o_ffn[...] = total[1:2]
+        for o, row in ((o_q, 2), (o_k, 3)):
+            v = total[:, :128]
+            o[...] = (v + roll_half(v))[row : row + 1, :64]
+
+    steps = {"h": load_w.wait, "nb": input_back, "rs": ring_start, "re": ring_end}
+    steps.update(sum_steps("q", qkv))
+    for i in range(NZ):
+        steps[f"qw{i}"] = part(weight_grad, t_attn, far(z, i), gqkv2, part_qkv)
+        if i < 3:
+            steps[f"hs{i}"] = hop(i).start
+            steps[f"he{i}"] = part(hop_end, i)
+    run_steps(LAST_ORDER, steps, {"H": (8, h_step)})
     for k in range(1, NZ):
-        c = remote(held, came.at[3 + z], pc.at(z=(z + k) % NZ), g_send.at[2 + k], g_recv.at[3 + z])
-        c.start()
-        ring.append(c)
-    qkv.final()
-    for k in range(1, NZ):
-        there = (z + k) % NZ
-        remote(held, came.at[3 + there], pc.at(z=there), g_send.at[2 + k], g_recv.at[3 + there]).wait_recv()
-    total = came[3]
-    for k in range(1, NZ):
-        total = total + came[3 + k]
-    o_attn[...] = total[0:1]
-    o_ffn[...] = total[1:2]
-    for o, row in ((o_q, 2), (o_k, 3)):
-        v = total[:, :128]
-        o[...] = (v + roll_half(v))[row : row + 1, :64]
-    for c in ring:
-        c.wait_send()
+        ring(k).wait_send()
     qkv.finish()
 
 

time: 370 us -> 274 us (0.74)
  Pallas kernels: 356 us -> 260 us
    pallas_call x1, Pallas kernels: 139 us -> 97.1 us  [backward(): pl.pallas_call(functools.partial(backward_kernel, dims), out_shape=[shape...]
    pallas_call x1, Pallas kernels: 153 us -> 120 us  [forward(): pl.pallas_call(functools.partial(forward_kernel, (tok, width, n_dev, head...]
    pallas_call x1, Pallas kernels: 64.1 us -> 43.1 us  [backward(): pl.pallas_call(functools.partial(last_kernel, dims), out_shape=[shape((to...]
where the time goes in v1:
time: 274 us
  Pallas kernels  260 us (95%)
  local copies, waits for them, and re-layouts  10.2 us (4%)
    pallas_call x1, Pallas kernels, forward(): pl.pallas_call(functools.partial(forward_kernel, (tok, width, n_dev, head...  120 us
    pallas_call x1, Pallas kernels, backward(): pl.pallas_call(functools.partial(backward_kernel, dims), out_shape=[shape...  97.1 us
    pallas_call x1, Pallas kernels, backward(): pl.pallas_call(functools.partial(last_kernel, dims), out_shape=[shape((to...  43.1 us
    unnamed x30, local copies, waits for them, and re-layouts  7.71 us

profile of v1, /device:TPU:0, one launch (start us, length us, event | category | flops | bytes accessed | tf_op | source)
XLA Modules:
  0.0 273.8 jit_solution(18140546622570384211)
XLA Ops:
  0.6 0.7 tile.4
  1.3 0.6 broadcast_in_dim_tile.6.refs_6_.refs_2_
  1.9 0.7 tile.5
  2.5 0.6 broadcast_in_dim_tile.7.refs_7_.refs_3_
  3.1 1.3 fusion.4
  4.5 1.2 fusion
  5.7 120.1 %forward.1 = (bf16[256,2048]{1,0:T(8,128)(2,1)}, bf16[16,64,512]{2,1,0:T(8,128)(2,1)}, bf16[16,32,512]{2,1,0:T(8,128)(2,1)}, bf16[16,64,512]{2,1,0:T(8,128)(2,1)...) custom-call(bf16[256,2048]{1,0:T(8,128)(2,1)} %bitcast.17, ...), custom_call_target="tpu_custom_call" | custom-call | flops 9126805504 | bytes 52428800 | tf_op jit(solution)/shard_map/forward/pallas_call | solution.py:823
  125.8 97.1 %backward.1 = (bf16[512,1536]{1,0:T(8,128)(2,1)}, f32[256,2048]{1,0:T(8,128)}, f32[8,2048]{1,0:T(8,128)}, f32[32,2048]{1,0:T(8,128)}, f32[64,2048]{1,0:T(8,128)}, /*index=5*/f32[32,2048]{1,0:T(8,128)}) custom-call(f32[256,128]{1,0:T(8,128)} %get-tuple-element.71.refs_3_.refs_0_, f32[256,128]{1,0:T(8,128)} %get-tuple-element.70.refs_4_.refs_1_, ...), custom_call_target="tpu_custom_call" | custom-call | flops 21474836480 | bytes 62914560 | tf_op jit(solution)/shard_map/backward/pallas_call | solution.py:1518
  222.9 43.1 %last.1 = (bf16[256,2048]{1,0:T(8,128)(2,1)}, f32[1,2048]{1,0:T(1,128)}, f32[1,64]{1,0:T(1,128)}, f32[1,64]{1,0:T(1,128)}, f32[1,2048]{1,0:T(1,128)}, /*index=5*/f32[64,1536]{1,0:T(8,128)}) custom-call(bf16[256,2048]{1,0:T(8,128)(2,1)} %bitcast.18, f32[1,2048]{1,0:T(1,128)} %bitcast.22, bf16[512,1536]{1,0:T(8,128)(2,1)} %get-tuple-element.56.refs_2_, ...), custom_call_target="tpu_custom_call" | custom-call | flops 6442450944 | bytes 20971520 | tf_op jit(solution)/shard_map/last/pallas_call | solution.py:1559
  266.0 0.0 copy-start.1
  266.0 0.0 copy-done
  266.0 0.0 copy-start.7
  266.0 0.0 copy-start.3
  266.1 1.0 copy.31
  267.1 0.6 copy-done.1
  267.6 1.0 copy.32
  268.6 0.6 copy.33
  269.2 0.7 copy.34
  269.9 0.5 copy.35
  270.5 0.5 copy.36
  271.0 0.7 copy.37
  271.7 0.6 copy.38
  272.3 0.8 copy.39
  273.1 0.7 copy.40
  (16 shorter events, 0.0 us)
Async XLA Ops:
  222.9 43.2 %copy-start = (bf16[256,2048]{1,0:T(8,128)(2,1)S(1)}, bf16[256,2048]{1,0:T(8,128)(2,1)}, u32[]{:S(2)}) copy-start(bf16[256,2048]{1,0:T(8,128)(2,1)} %get-tuple-element.40) | copy-start | bytes 3145732
  266.0 1.6 copy-start.1
  266.0 2.6 copy-start.7
  266.0 3.2 %copy-start.3 = (f32[64,1536]{1,0:T(8,128)S(1)}, f32[64,1536]{1,0:T(8,128)}, u32[]{:S(2)}) copy-start(f32[64,1536]{1,0:T(8,128)} %get-tuple-element.89) | copy-start | bytes 1179652
  266.0 3.9 %copy-start.9 = (f32[1,64]{1,0:T(1,128)S(1)}, f32[1,64]{1,0:T(1,128)}, u32[]{:S(2)}) copy-start(f32[1,64]{1,0:T(1,128)} %get-tuple-element.64) | copy-start | bytes 772
  266.1 4.4 %copy-start.8 = (f32[1,64]{1,0:T(1,128)S(1)}, f32[1,64]{1,0:T(1,128)}, u32[]{:S(2)}) copy-start(f32[1,64]{1,0:T(1,128)} %get-tuple-element.65) | copy-start | bytes 772
  266.1 4.9 %copy-start.5 = (f32[32,2048]{1,0:T(8,128)S(1)}, f32[32,2048]{1,0:T(8,128)}, u32[]{:S(2)}) copy-start(f32[32,2048]{1,0:T(8,128)} %get-tuple-element.92) | copy-start | bytes 786436
  267.6 4.1 %copy-start.6 = (f32[1,2048]{1,0:T(1,128)S(1)}, f32[1,2048]{1,0:T(1,128)}, u32[]{:S(2)}) copy-start(f32[1,2048]{1,0:T(1,128)} %get-tuple-element.67) | copy-start | bytes 24580
  267.6 4.7 %copy-start.2 = (f32[64,2048]{1,0:T(8,128)S(1)}, f32[64,2048]{1,0:T(8,128)}, u32[]{:S(2)}) copy-start(f32[64,2048]{1,0:T(8,128)} %get-tuple-element.94) | copy-start | bytes 1572868
  267.6 5.5 %copy-start.4 = (f32[32,2048]{1,0:T(8,128)S(1)}, f32[32,2048]{1,0:T(8,128)}, u32[]{:S(2)}) copy-start(f32[32,2048]{1,0:T(8,128)} %get-tuple-element.95) | copy-start | bytes 786436

commit v2 on v1

--- a/solution.py
+++ b/solution.py
@@ -27,21 +27,18 @@
 ]
 
 BACKWARD_ORDER = [
-    "dw0", "dw1", "gw0", "gw1", "dw2", "dw3", "h", *["H"] * 6, "ga0", *["H"] * 2, "nb", "gw2",
-    "db1", "gw3", "da1", "m", "att", "ow0", "ga2", "ga1", "oa0", "B", "ow1", "da2", "oa1", "dd1",
-    "ow2", "gb0", "oa2", "da0", *["B"] * 2, "db2", "B", "oz00", *["B"] * 2, "dd2", *["B"] * 3,
-    "gb1", *["B"] * 2, "gb2", "dd0", "dx1", *["B"] * 2, "oz02", "ga3", "oz10", "oz12", "db0", "B",
-    "gd2", "oz22", *["B"] * 2, "gd1", "B", "gb3", "oz20", "B", "oz03", *["B"] * 2, "oz01", "B",
-    "oz13", "dx0", *["B"] * 2, "oz23", "dz0", *["B"] * 2, "dx2", "gd0", "dz1", "B", "gd3",
-    *["B"] * 2, "dz2", "gx2", "da3", "gx0", *["B"] * 4, "kvs", "db3", "oz11", "dd3", "gx1", "gz0",
-    "Q", "kvc", "oz21", "ow3", "oa3", "oo0", "gz1", "kve", "oo3", "df", "gz2", "Q", "oo2", "Q",
-    "oo1", *["Q"] * 2, "oS", *["Q"] * 3, "kvf", "oe", "of", "gf",
-]
-
-LAST_ORDER = [
-    "qw0", "qa0", "qw1", "qa1", "qb0", "qw2", "h", *["H"] * 2, "qd0", "H", "qb1", "H", "qa2",
-    *["H"] * 2, "qd1", "H", "qb2", "H", "nb", "qx0", "qz0", "qd2", "hs0", "qw3", "he0", "hs1",
-    "qa3", "qx1", "qz1", "qx2", "qz2", "he1", "hs2", "qb3", "qd3", "he2", "rs", "qf", "re",
+    "dw0", "dw1", "gw0", "dw2", "ga0", "gb0", "da0", "gw1", "gw2", "h", *["H"] * 5, "ga1",
+    *["H"] * 3, "nb", "gw3", "dw3", "m", "lm", "att", *["B"] * 4, "gd0", "ga3", "ow0", "ow1",
+    "oa0", "B", "dd0", *["B"] * 4, "da2", "db0", "da3", *["B"] * 2, "oa1", "B", "ow2", "B", "ow3",
+    "B", "gx0", "ga2", "da1", "oz00", "B", "oz02", "ll", "gd3", "B", "db2", "oa2", "B", "oz10",
+    "dx0", "B", "gb1", "B", "gb3", *["B"] * 2, "oz03", *["B"] * 3, "gd2", "B", "oz12", "B",
+    "oz01", "gd1", *["B"] * 3, "oz13", "B", "oz23", "oz11", "db1", "dd3", *["B"] * 2, "kvs",
+    "dd1", "Q", "dd2", "Q", "dz0", "dx1", "Q", "kvc", "dz1", *["Q"] * 2, "oz20", *["Q"] * 3,
+    "dx2", "gx1", "kve", "gb2", "gz0", "kvf", "dz2", "db3", "oo0", "qe", "qw0", "qb0", "qa0",
+    "oa3", "qw1", "qa1", "g", "G", "qw2", "gx2", "oz21", "oz22", "qb1", "gz1", "qw3", "qa3",
+    *["G"] * 2, "qd0", "oo3", *["G"] * 2, "qa2", "oo1", "qd1", "qb2", "gz2", *["G"] * 3, "nb2",
+    "hs0", "qx0", "qz0", "oo2", "he0", "hs1", "qd2", "qx1", "qd3", "qz1", "he1", "hs2", "qb3",
+    "qx2", "qz2", "oS", "he2", "rs", "oe", "gf", "qf", "re", "of", "df",
 ]
 
 f32 = jnp.float32
@@ -1179,7 +1176,7 @@
         emit(rows, inv * (gg - unit * jnp.mean(gg * unit, axis=-1, keepdims=True)))
         return 0
 
-    lax.fori_loop(0, src.shape[0] // 32, body, 0)
+    lax.fori_loop(0, grad.shape[0] // 32, body, 0)
 
 
 def sum_steps(letter, g):
@@ -1210,50 +1207,59 @@
 
 LOADS = [
     "act", "cot", "ffn", "ggu", "wgu", "res", "mix", "mixf", "linv", "q2", "kk", "va", "mask",
-    "qkv", "wout",
+    "qkv", "wout", "attn", "wqkv", "x",
 ]
 
 
 def backward_kernel(dims, *refs):
     (tok, width, n_dev, heads_w, kv_w, ff) = dims
     (
-        cos_ref, sin_ref, g_q, g_k, g_ffn,
-        i_tmix, i_tffn, i_tact, i_cot, i_ggu, i_qkv, i_q2, i_linv, i_mixf, i_res, i_kk, i_va,
-        i_mask, i_wout, i_wgu,
-        gqkv2, res, gains, out_wout, out_wgu, out_wdown,
-        t_mix, t_ffn, t_act, cot2, ggu2, qkv, q2, linv, mixf, kk, va, mask_t, w_gu,
-        part_out, part_gu, part_down, gh, gattn2, acc_k, acc_v, acc_q, aug, gm, terms,
-        send, recv, kv_send, kv_recv, ex_send, ex_recv, lsem,
-    ) = refs[:57]
-    bufs = refs[57:]
+        cos_ref, sin_ref, g_attn, g_q, g_k, g_ffn,
+        i_x, i_tattn, i_tmix, i_tffn, i_tact, i_cot, i_ggu, i_qkv, i_q2, i_linv, i_mixf, i_res,
+        i_kk, i_va, i_mask, i_wqkv, i_wout, i_wgu,
+        o_dx, o_attn, o_q, o_k, o_ffn, out_wqkv, out_wout, out_wgu, out_wdown,
+        t_ffn, t_act, cot2, ggu2, qkv, q2, linv, mixf, kk, va, mask_t, w_gu,
+        part_qkv, part_out, part_gu, part_down, res, gains, came, gh, gattn2, acc_k, acc_v, acc_q,
+        aug, gm, terms,
+        send, recv, kv_send, kv_recv, ex_send, ex_recv, g_send, g_recv, lsem,
+    ) = refs[:69]
+    bufs = refs[69:]
     pc = Place()
     z = pc.z
     part = functools.partial
     loads = {}
 
     def load(name, src, dst):
-        c = pltpu.make_async_copy(src, dst, lsem.at[LOADS.index(name)])
-        loads[name] = c
-        c.start()
-
-    load("act", i_tact, t_act)
-    load("cot", i_cot, cot2)
-    load("ffn", i_tffn, t_ffn)
-    load("ggu", i_ggu, ggu2)
-    load("wgu", i_wgu, w_gu)
-    load("res", i_res, res)
-    load("mix", i_tmix, t_mix)
-    load("mixf", i_mixf, mixf)
-    load("linv", i_linv, linv)
-    load("q2", i_q2, q2)
-    load("kk", i_kk, kk)
-    load("va", i_va, va)
-    load("mask", i_mask, mask_t)
-    load("qkv", i_qkv, qkv)
-    barrier(pc)
+        def copy():
+            return pltpu.make_async_copy(src(), dst(), lsem.at[LOADS.index(name)])
+
+        loads[name] = lambda: copy().wait()
+        copy().start()
+
+    load("act", lambda: i_tact, lambda: t_act)
+    load("cot", lambda: i_cot, lambda: cot2)
+    load("ffn", lambda: i_tffn, lambda: t_ffn)
+    load("ggu", lambda: i_ggu, lambda: ggu2)
+    load("wgu", lambda: i_wgu, lambda: w_gu)
+    load("res", lambda: i_res, lambda: res)
+    load("mixf", lambda: i_mixf, lambda: mixf)
+    load("linv", lambda: i_linv, lambda: linv)
+    load("q2", lambda: i_q2, lambda: q2)
+    load("kk", lambda: i_kk, lambda: kk)
+    load("va", lambda: i_va, lambda: va)
+    load("mask", lambda: i_mask, lambda: mask_t)
+    load("qkv", lambda: i_qkv, lambda: qkv)
+    bar = pltpu.get_barrier_semaphore()
+    for device in (pc.xn(), pc.yn(), pc.sn()):
+        pl.semaphore_signal(bar, inc=1, device_id=device, device_id_type=MESH)
+    for k in range(1, NZ):
+        there = pc.at(z=(z + k) % NZ)
+        pl.semaphore_signal(bar, inc=1, device_id=there, device_id_type=MESH)
+    pl.semaphore_wait(bar, 3 + NZ - 1)
     down = Scatter(pc, part_down, bufs[0:4], out_wdown, send.at[0], recv.at[0])
     gateup = Scatter(pc, part_gu, bufs[4:8], out_wgu, send.at[1], recv.at[1])
     out = ScatterZ(pc, part_out, bufs[8:13], out_wout, send.at[2], recv.at[2])
+    last = Scatter(pc, part_qkv, bufs[17:21], out_wqkv, send.at[3], recv.at[3])
     seq = SequenceSum(pc, terms, bufs[13:17], kv_send, kv_recv, ex_send.at[2], ex_recv.at[2])
 
     own = pl.ds(0, tok)
@@ -1262,7 +1268,7 @@
     def rows_of(left, right, term, names, i):
         for name in names:
             if name in loads:
-                loads.pop(name).wait()
+                loads.pop(name)()
         weight_grad(left, far(z, i), right, term)
 
     def h_step(n):
@@ -1270,8 +1276,8 @@
         gh[:, cols(n, width // 8)] = dot_t(ggu2[own, :], w)
 
     def start_h():
-        loads.pop("wgu").wait()
-        loads.pop("res").wait()
+        loads.pop("wgu")()
+        loads.pop("res")()
 
     def keep_residual(rows, grad):
         total = cot2[rows, :].astype(f32) + grad
@@ -1281,11 +1287,22 @@
     sent_attn = remote(gattn2.at[own, :], gattn2.at[back, :], pc.sn(), ex_send.at[0], ex_recv.at[0])
 
     def residual_back():
-        load("wout", i_wout, w_gu.at[:, :, :, :, pl.ds(0, part_out.shape[-2]), :])
+        load("wout", lambda: i_wout, lambda: w_gu.at[:, :, :, :, pl.ds(0, part_out.shape[-2]), :])
         gains[...] = jnp.zeros_like(gains)
         norm_back(res, g_ffn, gh, gains, 1, keep_residual)
         sent_attn.start()
-        loads.pop("wout").wait()
+        loads.pop("wout")()
+
+    columns = part_qkv.shape[-1]
+    some = pl.ds(0, columns)
+
+    def load_mix():
+        load("mix", lambda: i_tmix, lambda: t_act)
+
+    def load_last():
+        load("attn", lambda: i_tattn, lambda: t_ffn)
+        load("wqkv", lambda: i_wqkv, lambda: w_gu.at[:, :, :, :, :, some])
+        load("x", lambda: i_x, lambda: cot2.at[own, :])
 
     def m_step(n, _):
         w = w_gu[n, :, :, :, pl.ds(0, part_out.shape[-2]), :].reshape(heads_w // NZ, width)
@@ -1294,11 +1311,11 @@
 
     def mixed_back():
         lax.fori_loop(0, NZ, m_step, 0)
-        sent_attn.wait_recv()
+        sent_attn.wait()
 
     def start_attention():
         for name in ("mixf", "linv", "q2", "kk", "va", "mask", "qkv"):
-            loads.pop(name).wait()
+            loads.pop(name)()
 
     low = lanes((tok, 128)) < 64
     chunk = 512
@@ -1374,12 +1391,12 @@
         grad = grad * cos_ref[...] - swap_rot(grad) * sin_ref[...]
         gains[pl.ds(row, 1), pl.ds(0, 128)] += jnp.sum(grad * unit, axis=0, keepdims=True)
         gg = grad * gain[...]
-        gqkv2[own, c] = (inv * (gg - unit * head_sums(gg * unit) * (1.0 / 64))).astype(bf16)
+        gattn2[own, c] = (inv * (gg - unit * head_sums(gg * unit) * (1.0 / 64))).astype(bf16)
 
     def query_back(t):
         head_back(t, gh[:, cols(t, 128)], g_q, 2)
 
-    sent_qkv = remote(gqkv2.at[own, :], gqkv2.at[back, :], pc.sn(), ex_send.at[1], ex_recv.at[1])
+    sent_qkv = remote(gattn2.at[own, some], gattn2.at[back, some], pc.sn(), ex_send.at[1], ex_recv.at[1])
 
     def keys_back():
         seq.plane_arrived(0)
@@ -1387,89 +1404,40 @@
             gh[seq.h[k], pl.ds(0, 2 * kv_w)] = seq.plane_total(0, k)
         for t in range(kv_w // 128):
             head_back(heads_w // 128 + t, gh[:, pl.ds(t * 128, 128)], g_k, 3)
-        gqkv2[own, pl.ds(heads_w + kv_w, kv_w)] = gh[:, pl.ds(kv_w, kv_w)].astype(bf16)
+        gattn2[own, pl.ds(heads_w + kv_w, kv_w)] = gh[:, pl.ds(kv_w, kv_w)].astype(bf16)
         sent_qkv.start()
 
-    steps = {
-        "h": start_h, "nb": residual_back, "m": mixed_back, "att": start_attention,
-        "kvs": seq.swap().start, "kvc": seq.core_event, "kve": part(seq.plane_second, 0),
-        "kvf": keys_back, "oS": out.plane_send, "oe": out.plane_event, "of": out.final,
-    }
-    steps.update(sum_steps("d", down))
-    steps.update(sum_steps("g", gateup))
-    for i in range(NZ):
-        steps[f"dw{i}"] = part(rows_of, t_act, cot2, part_down, ("act", "cot"), i)
-        steps[f"gw{i}"] = part(rows_of, t_ffn, ggu2, part_gu, ("ffn", "ggu"), i)
-        steps[f"ow{i}"] = part(rows_of, t_mix, gattn2, part_out, ("mix",), i)
-        steps[f"oa{i}"] = part(out.first, i)
-        steps[f"oo{i}"] = part(out.own_event, i)
-        if i < NZ - 1:
-            for k in range(4):
-                steps[f"oz{i}{k}"] = part(out.z_event, i, k)
-    loops = {
-        "H": (8, h_step),
-        "B": (heads_w // 128 * n_chunk, attend),
-        "Q": (heads_w // 128, query_back),
-    }
-    run_steps(BACKWARD_ORDER, steps, loops)
-    sent_qkv.wait_recv()
-    for g in (down, gateup, out, seq):
-        g.finish()
-    sent_attn.wait_send()
-    sent_qkv.wait_send()
-
-
-def last_kernel(dims, *refs):
-    (tok, width, n_dev, heads_w, kv_w, ff) = dims
-    (
-        x_ref, g_attn, gqkv2, res, gains, i_tattn, i_wqkv,
-        dx, o_attn, o_q, o_k, o_ffn, out_wqkv,
-        t_attn, w_qkv, part_qkv, gh, held, came,
-        send, recv, g_send, g_recv, lsem,
-    ) = refs[:24]
-    pc = Place()
-    z = pc.z
-    part = functools.partial
-    load_t = pltpu.make_async_copy(i_tattn, t_attn, lsem.at[0])
-    load_w = pltpu.make_async_copy(i_wqkv, w_qkv, lsem.at[1])
-    load_t.start()
-    load_w.start()
-    bar = pltpu.get_barrier_semaphore()
-    for device in (pc.xn(), pc.yn(), pc.sn()):
-        pl.semaphore_signal(bar, inc=1, device_id=device, device_id_type=MESH)
-    for k in range(1, NZ):
-        there = pc.at(z=(z + k) % NZ)
-        pl.semaphore_signal(bar, inc=1, device_id=there, device_id_type=MESH)
-    pl.semaphore_wait(bar, 3 + NZ - 1)
-    qkv = Scatter(pc, part_qkv, refs[24:28], out_wqkv, send, recv)
-    load_t.wait()
-    columns = w_qkv.shape[-1]
-
-    def h_step(n):
-        w = w_qkv[n // 2, n % 2].reshape(width // 8, columns)
-        gh[:, cols(n, width // 8)] = dot_t(gqkv2[pl.ds(0, tok), :], w)
+    def g_step(n):
+        w = w_gu[n // 2, n % 2, :, :, :, some].reshape(width // 8, columns)
+        gh[:, cols(n, width // 8)] = dot_t(gattn2[own, some], w)
 
     def keep_input(rows, grad):
-        dx[rows, :] = (res[rows, :] + grad).astype(bf16)
+        cot2[pl.ds(rows.start + tok, rows.size), :] = (res[rows, :] + grad).astype(bf16)
+
+    sent_dx = pltpu.make_async_copy(cot2.at[back, :], o_dx, lsem.at[len(LOADS)])
 
     def input_back():
-        held[...] = gains[...]
-        norm_back(x_ref, g_attn, gh, held, 0, keep_input)
+        loads.pop("x")()
+        norm_back(cot2, g_attn, gh, gains, 0, keep_input)
+        sent_dx.start()
+
+    def start_g():
+        loads.pop("wqkv")()
 
     def hop(k):
         device = (pc.sn(), pc.xn(), pc.yn())[k]
-        return remote(held, came.at[k], device, g_send.at[k], g_recv.at[k])
+        return remote(gains, came.at[k], device, g_send.at[k], g_recv.at[k])
 
     def hop_end(k):
         hop(k).wait()
-        held[...] += came[k]
+        gains[...] += came[k]
 
     def ring(k):
         there = pc.at(z=(z + k) % NZ)
-        return remote(held, came.at[3 + z], there, g_send.at[2 + k], g_recv.at[3 + z])
+        return remote(gains, came.at[3 + z], there, g_send.at[2 + k], g_recv.at[3 + z])
 
     def ring_start():
-        came[3 + z] = held[...]
+        came[3 + z] = gains[...]
         for k in range(1, NZ):
             ring(k).start()
 
@@ -1477,7 +1445,7 @@
         for k in range(1, NZ):
             there = (z + k) % NZ
             slot = came.at[3 + there]
-            remote(held, slot, pc.at(z=there), g_send.at[2 + k], g_recv.at[3 + there]).wait_recv()
+            remote(gains, slot, pc.at(z=there), g_send.at[2 + k], g_recv.at[3 + there]).wait_recv()
         total = came[3]
         for k in range(1, NZ):
             total = total + came[3 + k]
@@ -1487,17 +1455,41 @@
             v = total[:, :128]
             o[...] = (v + roll_half(v))[row : row + 1, :64]
 
-    steps = {"h": load_w.wait, "nb": input_back, "rs": ring_start, "re": ring_end}
-    steps.update(sum_steps("q", qkv))
+    steps = {
+        "h": start_h, "nb": residual_back, "m": mixed_back, "att": start_attention,
+        "kvs": seq.swap().start, "kvc": seq.core_event, "kve": part(seq.plane_second, 0),
+        "kvf": keys_back, "oS": out.plane_send, "oe": out.plane_event, "of": out.final,
+        "lm": load_mix, "ll": load_last, "qe": sent_qkv.wait_recv, "g": start_g,
+        "nb2": input_back, "rs": ring_start, "re": ring_end,
+    }
+    steps.update(sum_steps("q", last))
+    steps.update(sum_steps("d", down))
+    steps.update(sum_steps("g", gateup))
     for i in range(NZ):
-        steps[f"qw{i}"] = part(weight_grad, t_attn, far(z, i), gqkv2, part_qkv)
-        if i < 3:
+        steps[f"dw{i}"] = part(rows_of, t_act, cot2, part_down, ("act", "cot"), i)
+        steps[f"gw{i}"] = part(rows_of, t_ffn, ggu2, part_gu, ("ffn", "ggu"), i)
+        steps[f"ow{i}"] = part(rows_of, t_act, gattn2, part_out, ("mix",), i)
+        steps[f"qw{i}"] = part(rows_of, t_ffn, gattn2, part_qkv, ("attn",), i)
+        steps[f"oa{i}"] = part(out.first, i)
+        steps[f"oo{i}"] = part(out.own_event, i)
+        if i < NZ - 1:
+            for k in range(4):
+                steps[f"oz{i}{k}"] = part(out.z_event, i, k)
             steps[f"hs{i}"] = hop(i).start
             steps[f"he{i}"] = part(hop_end, i)
-    run_steps(LAST_ORDER, steps, {"H": (8, h_step)})
+    loops = {
+        "H": (8, h_step),
+        "B": (heads_w // 128 * n_chunk, attend),
+        "Q": (heads_w // 128, query_back),
+        "G": (8, g_step),
+    }
+    run_steps(BACKWARD_ORDER, steps, loops)
+    for g in (down, gateup, out, seq, last):
+        g.finish()
+    sent_qkv.wait_send()
     for k in range(1, NZ):
         ring(k).wait_send()
-    qkv.finish()
+    sent_dx.wait()
 
 
 def backward(x, cosine, sine, g_attn, g_q, g_k, g_ffn, kept, rows, n_dev):
@@ -1513,23 +1505,35 @@
     anyw = pl.BlockSpec(memory_space=pl.ANY)
     dma = pltpu.SemaphoreType.DMA
     r_qkv, r_out, r_gu, r_down = rows
-    partial = [VMEM((NZ, 2, 2, r, width), bf16) for r in (r_out, r_gu, r_down)]
-    like = [VMEM(v.shape, v.dtype) for v in (t_mix, t_ffn, t_act, cot2, ggu2, qkv, q2, linv, mixf, kk, va, mask_t, w_gu)]
-    gqkv2, grad_res, gains, own_out, own_gu, own_down = pl.pallas_call(
+    partial = [
+        VMEM((NZ, 2, 2, r, c), bf16)
+        for r, c in ((r_qkv, columns), (r_out, width), (r_gu, width), (r_down, width))
+    ]
+    like = [
+        VMEM(v.shape, v.dtype)
+        for v in (t_ffn, t_act, cot2, ggu2, qkv, q2, linv, mixf, kk, va, mask_t, w_gu)
+    ]
+    dx, grad_attn, grad_q, grad_k, grad_ffn, own_qkv, own_out, own_gu, own_down = pl.pallas_call(
         functools.partial(backward_kernel, dims),
         out_shape=[
-            shape((2 * tok, columns), bf16),
-            shape((tok, width), f32),
-            shape((8, width), f32),
+            shape((tok, width), bf16),
+            shape((1, width), f32),
+            shape((1, 64), f32),
+            shape((1, 64), f32),
+            shape((1, width), f32),
+            shape((r_qkv, columns), f32),
             shape((r_out, width), f32),
             shape((r_gu, width), f32),
             shape((r_down, width), f32),
         ],
-        in_specs=[vm] * 5 + [anyw] * 15,
-        out_specs=[vm] * 6,
+        in_specs=[vm] * 6 + [anyw] * 18,
+        out_specs=[anyw] + [vm] * 8,
         scratch_shapes=like
         + partial
         + [
+            VMEM((tok, width), f32),
+            VMEM((8, width), f32),
+            VMEM((3 + NZ, 8, width), f32),
             VMEM((tok, width), f32),
             VMEM((2 * tok, width), bf16),
             VMEM((length, 128), f32),
@@ -1538,57 +1542,32 @@
             VMEM((2 * tok, 128), bf16),
             VMEM((tok, heads_w), bf16),
             VMEM((2, 2, 2, tok, 2 * kv_w), bf16),
-            dma((3, 16, NZ)),
-            dma((3, 16, NZ)),
+            dma((4, 16, NZ)),
+            dma((4, 16, NZ)),
             dma((8, 1)),
             dma((8, 1)),
             dma((3,)),
             dma((3,)),
-            dma((15,)),
+            dma((3 + NZ,)),
+            dma((3 + NZ,)),
+            dma((len(LOADS) + 1,)),
         ]
         + Scatter.scratch(r_down, width)
         + Scatter.scratch(r_gu, width)
         + ScatterZ.scratch(r_out, width)
-        + SequenceSum.scratch(tok, 2 * kv_w),
-        compiler_params=pltpu.CompilerParams(
-            collective_id=1, has_side_effects=True, vmem_limit_bytes=63 << 20
-        ),
-        cost_estimate=pl.CostEstimate(flops=20 * tok * width * width, bytes_accessed=60 << 20, transcendentals=0),
-        name="backward",
-    )(cosine, sine, g_q, g_k, g_ffn, t_mix, t_ffn, t_act, cot2, ggu2, qkv, q2, linv, mixf, res, kk, va, mask_t, w_out, w_gu)
-    last = pl.pallas_call(
-        functools.partial(last_kernel, dims),
-        out_shape=[
-            shape((tok, width), bf16),
-            shape((1, width), f32),
-            shape((1, 64), f32),
-            shape((1, 64), f32),
-            shape((1, width), f32),
-            shape((r_qkv, columns), f32),
-        ],
-        in_specs=[vm] * 5 + [anyw] * 2,
-        out_specs=[vm] * 6,
-        scratch_shapes=[
-            VMEM(t_attn.shape, bf16),
-            VMEM(w_qkv.shape, bf16),
-            VMEM((NZ, 2, 2, r_qkv, columns), bf16),
-            VMEM((tok, width), f32),
-            VMEM((8, width), f32),
-            VMEM((3 + NZ, 8, width), f32),
-            dma((8, NZ)),
-            dma((8, NZ)),
-            dma((3 + NZ,)),
-            dma((3 + NZ,)),
-            dma((2,)),
-        ]
+        + SequenceSum.scratch(tok, 2 * kv_w)
         + Scatter.scratch(r_qkv, columns),
         compiler_params=pltpu.CompilerParams(
-            collective_id=2, has_side_effects=True, vmem_limit_bytes=60 << 20
+            collective_id=1, has_side_effects=True, vmem_limit_bytes=64 << 20
         ),
-        cost_estimate=pl.CostEstimate(flops=8 * tok * width * columns, bytes_accessed=20 << 20, transcendentals=0),
-        name="last",
-    )(x, g_attn, gqkv2, grad_res, gains, t_attn, w_qkv)
-    dx, grad_attn, grad_q, grad_k, grad_ffn, own_qkv = last
+        cost_estimate=pl.CostEstimate(
+            flops=20 * tok * width * width, bytes_accessed=60 << 20, transcendentals=0
+        ),
+        name="backward",
+    )(
+        cosine, sine, g_attn, g_q, g_k, g_ffn, x, t_attn, t_mix, t_ffn, t_act, cot2, ggu2, qkv, q2,
+        linv, mixf, res, kk, va, mask_t, w_qkv, w_out, w_gu,
+    )
     return dx, grad_attn[0], own_qkv, grad_q[0], grad_k[0], own_out, grad_ffn[0], own_gu, own_down
 
 

time: 274 us -> 262 us (0.956)
  Pallas kernels: 260 us -> 248 us
    pallas_call x1 -> x0, Pallas kernels: 43.1 us -> none  [backward(): pl.pallas_call(functools.partial(last_kernel, dims), out_shape=[shape((to...]
    pallas_call x1, Pallas kernels: 97.1 us -> 128 us  [backward(): pl.pallas_call(functools.partial(backward_kernel, dims), out_shape=[shape...]
    unnamed x30 -> x28, local copies, waits for them, and re-layouts: 7.71 us -> 8.6 us
where the time goes in v2:
time: 262 us
  Pallas kernels  248 us (95%)
  local copies, waits for them, and re-layouts  11.1 us (4%)
    pallas_call x1, Pallas kernels, backward(): pl.pallas_call(functools.partial(backward_kernel, dims), out_shape=[shape...  128 us
    pallas_call x1, Pallas kernels, forward(): pl.pallas_call(functools.partial(forward_kernel, (tok, width, n_dev, head...  120 us
    unnamed x28, local copies, waits for them, and re-layouts  8.6 us

profile of v2, /device:TPU:0, one launch (start us, length us, event | category | flops | bytes accessed | tf_op | source)
XLA Modules:
  0.0 262.1 jit_solution(5338948758239022406)
XLA Ops:
  0.6 0.7 tile.4
  1.3 0.6 broadcast_in_dim_tile.6.refs_6_.refs_3_
  1.9 0.7 tile.5
  2.5 0.6 broadcast_in_dim_tile.7.refs_7_.refs_4_
  3.1 1.3 fusion.4
  4.5 1.2 fusion
  5.7 120.2 %forward.1 = (bf16[256,2048]{1,0:T(8,128)(2,1)}, bf16[16,64,512]{2,1,0:T(8,128)(2,1)}, bf16[16,32,512]{2,1,0:T(8,128)(2,1)}, bf16[16,64,512]{2,1,0:T(8,128)(2,1)...) custom-call(bf16[256,2048]{1,0:T(8,128)(2,1)} %bitcast.17, ...), custom_call_target="tpu_custom_call" | custom-call | flops 9126805504 | bytes 52428800 | tf_op jit(solution)/shard_map/forward/pallas_call | solution.py:820
  125.9 127.5 %backward.1 = (bf16[256,2048]{1,0:T(8,128)(2,1)}, f32[1,2048]{1,0:T(1,128)}, f32[1,64]{1,0:T(1,128)}, f32[1,64]{1,0:T(1,128)}, f32[1,2048]{1,0:T(1,128)}, /*inde...) custom-call(f32[256,128]{1,0:T(8,128)} %get-tuple-element.65.refs_3_.refs_0_, ...), custom_call_target="tpu_custom_call" | custom-call | flops 21474836480 | bytes 62914560 | tf_op jit(solution)/shard_map/backward/pallas_call | solution.py:1516
  253.4 0.0 copy-start
  253.4 0.0 copy-start.6
  253.4 0.0 copy-start.2
  253.4 0.0 copy-start.8
  253.5 2.4 copy.31
  255.9 1.0 copy.32
  256.9 0.0 copy-done.6
  256.9 0.6 copy.33
  257.5 0.7 copy.34
  258.2 0.5 copy.35
  258.8 0.5 copy.36
  259.3 0.7 copy.37
  260.0 0.0 copy-done.5
  260.0 0.6 copy.38
  260.6 0.8 copy.39
  261.4 0.7 copy.40
  (13 shorter events, 0.0 us)
Async XLA Ops:
  253.4 2.5 copy-start
  253.4 3.5 %copy-start.6 = (f32[1,2048]{1,0:T(1,128)S(1)}, f32[1,2048]{1,0:T(1,128)}, u32[]{:S(2)}) copy-start(f32[1,2048]{1,0:T(1,128)} %get-tuple-element.56) | copy-start | bytes 24580
  253.4 4.1 %copy-start.2 = (f32[64,1536]{1,0:T(8,128)S(1)}, f32[64,1536]{1,0:T(8,128)}, u32[]{:S(2)}) copy-start(f32[64,1536]{1,0:T(8,128)} %get-tuple-element.83) | copy-start | bytes 1179652
  253.4 4.8 %copy-start.8 = (f32[1,64]{1,0:T(1,128)S(1)}, f32[1,64]{1,0:T(1,128)}, u32[]{:S(2)}) copy-start(f32[1,64]{1,0:T(1,128)} %get-tuple-element.58) | copy-start | bytes 772
  253.5 5.3 %copy-start.7 = (f32[1,64]{1,0:T(1,128)S(1)}, f32[1,64]{1,0:T(1,128)}, u32[]{:S(2)}) copy-start(f32[1,64]{1,0:T(1,128)} %get-tuple-element.59) | copy-start | bytes 772
  253.5 5.8 %copy-start.4 = (f32[32,2048]{1,0:T(8,128)S(1)}, f32[32,2048]{1,0:T(8,128)}, u32[]{:S(2)}) copy-start(f32[32,2048]{1,0:T(8,128)} %get-tuple-element.86) | copy-start | bytes 786436
  255.9 4.1 %copy-start.5 = (f32[1,2048]{1,0:T(1,128)S(1)}, f32[1,2048]{1,0:T(1,128)}, u32[]{:S(2)}) copy-start(f32[1,2048]{1,0:T(1,128)} %get-tuple-element.61) | copy-start | bytes 24580
  255.9 4.7 %copy-start.1 = (f32[64,2048]{1,0:T(8,128)S(1)}, f32[64,2048]{1,0:T(8,128)}, u32[]{:S(2)}) copy-start(f32[64,2048]{1,0:T(8,128)} %get-tuple-element.88) | copy-start | bytes 1572868
  255.9 5.5 %copy-start.3 = (f32[32,2048]{1,0:T(8,128)S(1)}, f32[32,2048]{1,0:T(8,128)}, u32[]{:S(2)}) copy-start(f32[32,2048]{1,0:T(8,128)} %get-tuple-element.89) | copy-start | bytes 786436

commit v3 on v2

--- a/solution.py
+++ b/solution.py
@@ -3,6 +3,7 @@
 
 import jax
 import jax.numpy as jnp
+import numpy as np
 from jax import lax
 from jax.experimental import pallas as pl
 from jax.experimental.pallas import tpu as pltpu
@@ -15,30 +16,29 @@
 
 
 FORWARD_ORDER = [
-    "qp0", "qZ", "norm", "dp0", "qz1", "qe0", "qp1", "qz2", "gZ", "qp2", "qc0", "qe1", "oP",
-    "qz3", "qp3", "qe2", "gz1", "qs0", "gz2", "oZ", "qe3", "oe", "dZ", "qc1", "qc2", "gp2", "qc3",
-    "qs1", "qs2", "oD", "qs3", "oz12", "keys", "de0", "turn", "oz22", "kve", "gp1", "gz3", "gp0",
-    "dz1", "query", "kvc", "dp1", "oz32", "ge2", "unpack", "gp3", "oz10", "dz2", *["A"] * 3,
-    "oz20", *["A"] * 4, "oz30", *["A"] * 5, "dp2", "oz11", "ge0", "dz3", *["A"] * 3, "dc0",
-    "oz13", "ge1", "oz23", *["A"] * 5, "oz21", "de1", "A", "oc1", "gc2", *["A"] * 4, "oc2", "A",
-    "dp3", "oz31", *["A"] * 3, "oz33", "oc3", *["A"] * 2, "gc0", "A", "mix", "de2", "dc1", "ds0",
-    "res", "ge3", "de3", "gc1", "norm2", "dc2", "gc3", "gs0", "gs1", "dc3", "ds1", "ds2", "gs2",
-    "turn2", "gs3", "ds3", "gate", "act", "y",
+    "qp0", "oP", "qZ", "dZ", "qz1", "qe0", "qp1", "dp0", "qz2", "gZ", "trig", "qp2", "norm",
+    "qc0", "qe1", "turn", "qz3", "dz1", "qp3", "qe2", "gz1", "gz2", "oZ", "qc1", "qe3", "oe",
+    "qc2", "gp2", "qs0", "qc3", "oz10", "oD", "qs1", "qs2", "qs3", "keys", "de0", "gz3", "oz11",
+    "kve", "gp0", "oz12", "ge2", "dz2", "query", "oz22", "kvc", "gp1", "dc0", "oz13", "gp3",
+    "oz21", "unpack", "oz32", "A", "dp2", *["A"] * 3, "oz31", *["A"] * 5, "oz20", *["A"] * 4,
+    "ge0", "A", "oz30", "ge1", "A", "gc2", *["A"] * 4, "oz23", *["A"] * 5, "dp1", "oc1", "oz33",
+    *["A"] * 2, "oc3", "ge3", "A", "oc2", "de2", "A", "dz3", *["A"] * 2, "gc1", "dp3", "A", "gc0",
+    "A", "res", "norm2", "gc3", "de1", "gs0", "ds0", "mix", "gs1", "de3", "dc2", "gs2", "dc1",
+    "gs3", "dc3", "turn2", "ds1", "ds2", "ds3", "gate", "act", "y",
 ]
 
 BACKWARD_ORDER = [
-    "dw0", "dw1", "gw0", "dw2", "ga0", "gb0", "da0", "gw1", "gw2", "h", *["H"] * 5, "ga1",
-    *["H"] * 3, "nb", "gw3", "dw3", "m", "lm", "att", *["B"] * 4, "gd0", "ga3", "ow0", "ow1",
-    "oa0", "B", "dd0", *["B"] * 4, "da2", "db0", "da3", *["B"] * 2, "oa1", "B", "ow2", "B", "ow3",
-    "B", "gx0", "ga2", "da1", "oz00", "B", "oz02", "ll", "gd3", "B", "db2", "oa2", "B", "oz10",
-    "dx0", "B", "gb1", "B", "gb3", *["B"] * 2, "oz03", *["B"] * 3, "gd2", "B", "oz12", "B",
-    "oz01", "gd1", *["B"] * 3, "oz13", "B", "oz23", "oz11", "db1", "dd3", *["B"] * 2, "kvs",
-    "dd1", "Q", "dd2", "Q", "dz0", "dx1", "Q", "kvc", "dz1", *["Q"] * 2, "oz20", *["Q"] * 3,
-    "dx2", "gx1", "kve", "gb2", "gz0", "kvf", "dz2", "db3", "oo0", "qe", "qw0", "qb0", "qa0",
-    "oa3", "qw1", "qa1", "g", "G", "qw2", "gx2", "oz21", "oz22", "qb1", "gz1", "qw3", "qa3",
-    *["G"] * 2, "qd0", "oo3", *["G"] * 2, "qa2", "oo1", "qd1", "qb2", "gz2", *["G"] * 3, "nb2",
-    "hs0", "qx0", "qz0", "oo2", "he0", "hs1", "qd2", "qx1", "qd3", "qz1", "he1", "hs2", "qb3",
-    "qx2", "qz2", "oS", "he2", "rs", "oe", "gf", "qf", "re", "of", "df",
+    "dw0", "dw1", "gw0", "dw2", "gw1", "dw3", "h", "gb0", *["H"] * 8, "ga1", "nb", "lm", "db0",
+    "db2", "ga0", "gw2", "db1", "da2", "da0", "m", "ow0", "ow1", "oa0", "gd1", "att", "B", "ga2",
+    "gw3", "B", "oz00", "B", "dd0", "gd0", "oa1", "B", "da1", *["B"] * 2, "oz03", "B", "gb3",
+    "oz01", "da3", "ow2", "dx0", "ga3", "oa2", "gb1", "ll", "B", "gd2", "ow3", *["B"] * 4, "oz13",
+    "dd1", "B", "gx0", *["B"] * 2, "gb2", "oz02", "B", "kvs", "dx1", "Q", "dd3", "dd2", "Q",
+    "dz0", "Q", "kvc", "Q", "dz1", "Q", "oz23", "Q", "oz10", "oz12", "Q", "oz22", "Q", "oz11",
+    "kve", "dx2", "db3", "gd3", "oz21", "gz0", "kvf", "g", *["G"] * 2, "qe", "qw0", "qa0", "gx2",
+    "qw1", "qw2", "qb0", "G", "dz2", "G", "oz20", "oa3", "qa1", "gx1", "qb1", "G", "qa2", "G",
+    "qb2", *["G"] * 2, "gz1", "qd0", "nb2", "qw3", "gz2", "oo0", "hs0", "qd1", "he0", "oo3",
+    "oo1", "hs1", "qb3", "qd2", "qx0", "oo2", "qz0", "df", "he1", "qx1", "hs2", "qa3", "qz1",
+    "oS", "he2", "qx2", "rs", "qz2", "qd3", "oe", "of", "gf", "qf", "re",
 ]
 
 f32 = jnp.float32
@@ -439,6 +439,10 @@
     high = v.astype(bf16)
     low = (v - high.astype(f32)).astype(bf16)
     return dot(high, ones) + dot(low, ones)
+
+
+def twice(gain):
+    return jnp.concatenate([gain[...], gain[...]], axis=1)
 
 
 def cols(i, width):
@@ -515,13 +519,13 @@
 def forward_kernel(dims, *refs):
     (tok, width, n_dev, heads_w, kv_w, ff) = dims
     (
-        x_ref, cot_ref, hi_ref, cos_ref, sin_ref, g_attn, g_q, g_k, g_ffn,
+        x_ref, cot_ref, place_ref, freq_ref, g_attn, one_q, one_k, g_ffn,
         s_qkv, s_out, s_down, s_gu,
         o_y, o_tattn, o_tmix, o_tffn, o_tact, o_cot, o_ggu, o_kv, o_q2, o_linv, o_mixf, o_res,
-        o_kk, o_va, o_mask, o_wqkv, o_wout, o_wgu,
+        o_kk, o_va, o_mask, o_wqkv, o_wout, o_wgu, o_cos, o_sin,
         w_qkv, w_out, w_down, w_gu, kk, va, mask, mask_t, o2, gu, gact,
         y_ref, hattn_ref, qkv_ref, q2_ref, kvb, linv_ref, mixf_ref, mixb_ref, res_ref, hffn_ref,
-        act_ref, cot2, ggu2, t_attn, t_mix, t_ffn, t_act, turn_a, turn_b,
+        act_ref, cot2, ggu2, cos_ref, sin_ref, t_attn, t_mix, t_ffn, t_act, turn_a, turn_b,
         send, recv, kv_send, kv_recv, lsem, osem, ex_send, ex_recv,
     ) = refs
     pc = Place()
@@ -561,6 +565,22 @@
     sent_act = exchange(4, turn_b.at[:, pl.ds(0, s_down.shape[0]), :], t_act.at[:, :, back])
     sent_ggu = exchange(5, ggu2.at[pl.ds(0, tok), :], ggu2.at[back, :])
 
+    g_q, g_k = twice(one_q), twice(one_k)
+
+    def block_row(a):
+        return jnp.right_shift(place_ref[:, a * (tok // 2) : (a + 1) * (tok // 2)], 7).astype(f32)
+
+    def tables():
+        step = tok // 2
+        sign = jnp.where(lanes((step, 128)) % 64 < 32, -1.0, 1.0)
+        row = lax.broadcasted_iota(jnp.int32, (step, 128), 0).astype(f32)
+        for a in range(2):
+            angle = (block_row(a) * 128.0 + row) * freq_ref[...]
+            cos_ref[pl.ds(a * step, step), :] = jnp.cos(angle)
+            sin_ref[pl.ds(a * step, step), :] = sign * jnp.sin(angle)
+        emit(cos_ref, o_cos)
+        emit(sin_ref, o_sin)
+
     def first_norm():
         norm_into(x_ref, g_attn, hattn_ref)
 
@@ -596,7 +616,7 @@
 
     def head_tile(t, gain):
         u = qkv_ref[:, cols(t, 128)]
-        n = u * lax.rsqrt(head_sums(u * u) * (1.0 / 64) + EPS) * gain[...]
+        n = u * lax.rsqrt(head_sums(u * u) * (1.0 / 64) + EPS) * gain
         return n * cos_ref[...] + swap_rot(n) * sin_ref[...]
 
     def keys_out():
@@ -607,7 +627,8 @@
         kvb[pc.y, pc.x, pc.core, pl.ds(0, tok), pl.ds(kv_w, kv_w)] = qkv_ref[
             :, pl.ds(heads_w + kv_w, kv_w)
         ].astype(bf16)
-        blocks_row = jnp.broadcast_to(hi_ref[...], (16, tok)).astype(bf16)
+        both_rows = jnp.concatenate([block_row(0), block_row(1)], axis=1)
+        blocks_row = jnp.broadcast_to(both_rows, (16, tok)).astype(bf16)
         kvb[pc.y, pc.x, pc.core, pl.ds(tok, 16), pl.ds(0, tok)] = blocks_row
         kvb[pc.y, pc.x, pc.core, pl.ds(tok, 16), pl.ds(tok, tok)] = blocks_row
         seq.own()
@@ -643,7 +664,7 @@
         step = tok // 2
         key_hi = kvb[y, x, c, pl.ds(tok, 16), pl.ds(0, tok)].astype(f32)[:1, :]
         for a in range(2):
-            own = hi_ref[:, a * step : (a + 1) * step].astype(f32)
+            own = block_row(a)
             row = lax.broadcasted_iota(jnp.int32, (step, step), 0).astype(f32)
             col = lanes((step, step)).astype(f32)
             for d in range(2):
@@ -758,7 +779,7 @@
         emit(t_act, o_tact)
 
     steps = {
-        "norm": first_norm, "turn": first_turn, "keys": keys_out, "query": queries,
+        "norm": first_norm, "trig": tables, "turn": first_turn, "keys": keys_out, "query": queries,
         "kve": seq.plane_event, "kvc": seq.core_event, "unpack": unpack_all, "mix": mix_out,
         "res": residual, "norm2": second_norm, "turn2": second_turn, "gate": gates,
         "act": act_out, "y": outputs, "oP": out.own_plane, "oZ": out.own_z, "oe": out.plane_event,
@@ -783,7 +804,7 @@
         c.wait()
 
 
-def forward(x, cot, blocks, cosine, sine, g_attn, g_q, g_k, g_ffn, s_qkv, s_out, s_down, s_gu, n_dev):
+def forward(x, cot, places, frequency, g_attn, g_q, g_k, g_ffn, s_qkv, s_out, s_down, s_gu, n_dev):
     tok, width = x.shape
     heads_w, kv_w = HEADS * HEAD_DIM, GROUPS * HEAD_DIM
     ff = s_down.shape[0] * n_dev * NZ
@@ -811,6 +832,8 @@
         (seven[0], bf16),
         (seven[1], bf16),
         (seven[3], bf16),
+        ((tok, 128), f32),
+        ((tok, 128), f32),
     ]
     outs = [shape(*k) for k in keep]
     vm = pl.BlockSpec(memory_space=VMEM)
@@ -820,7 +843,7 @@
     return pl.pallas_call(
         functools.partial(forward_kernel, (tok, width, n_dev, heads_w, kv_w, ff)),
         out_shape=outs,
-        in_specs=[vm] * 9 + [anyw] * 4,
+        in_specs=[vm] * 8 + [anyw] * 4,
         out_specs=[anyw] * len(outs),
         scratch_shapes=[VMEM(s, bf16) for s in seven]
         + [
@@ -844,6 +867,8 @@
             VMEM((tok, ff), bf16),
             VMEM((2 * tok, width), bf16),
             VMEM((2 * tok, 2 * ff), bf16),
+            VMEM((tok, 128), f32),
+            VMEM((tok, 128), f32),
             *[VMEM(*t) for t in turned],
             VMEM((spots, qkv_rows, tok), bf16),
             VMEM((spots, out_rows, tok), bf16),
@@ -861,7 +886,7 @@
         ),
         cost_estimate=pl.CostEstimate(flops=flops, bytes_accessed=50 << 20, transcendentals=0),
         name="forward",
-    )(x, cot, blocks, cosine, sine, g_attn, g_q, g_k, g_ffn, s_qkv, s_out, s_down, s_gu)
+    )(x, cot, places, frequency, g_attn, g_q, g_k, g_ffn, s_qkv, s_out, s_down, s_gu)
 
 
 SD0, SD1, SX0, SX1, SY0, SY1, SA, SB = range(8)
@@ -1214,16 +1239,17 @@
 def backward_kernel(dims, *refs):
     (tok, width, n_dev, heads_w, kv_w, ff) = dims
     (
-        cos_ref, sin_ref, g_attn, g_q, g_k, g_ffn,
+        cos_ref, sin_ref, g_attn, one_q, one_k, g_ffn,
         i_x, i_tattn, i_tmix, i_tffn, i_tact, i_cot, i_ggu, i_qkv, i_q2, i_linv, i_mixf, i_res,
         i_kk, i_va, i_mask, i_wqkv, i_wout, i_wgu,
         o_dx, o_attn, o_q, o_k, o_ffn, out_wqkv, out_wout, out_wgu, out_wdown,
         t_ffn, t_act, cot2, ggu2, qkv, q2, linv, mixf, kk, va, mask_t, w_gu,
-        part_qkv, part_out, part_gu, part_down, res, gains, came, gh, gattn2, acc_k, acc_v, acc_q,
+        part_qkv, part_out, part_gu, part_down, res, gains, came, gh, gattn2, acc_q,
         aug, gm, terms,
         send, recv, kv_send, kv_recv, ex_send, ex_recv, g_send, g_recv, lsem,
-    ) = refs[:69]
-    bufs = refs[69:]
+    ) = refs[:67]
+    bufs = refs[67:]
+    g_q, g_k = twice(one_q), twice(one_k)
     pc = Place()
     z = pc.z
     part = functools.partial
@@ -1321,53 +1347,44 @@
     chunk = 512
     n_chunk = n_dev * tok // chunk
     def attend(tick):
-        t, kc = tick // n_chunk, tick % n_chunk
-        g = t // 2
+        g, kc = tick // n_chunk, tick % n_chunk
         rows = pl.ds(pl.multiple_of(kc * chunk, chunk), chunk)
 
         @pl.when(kc == 0)
         def _():
-            c = cols(t, 128)
-            grad = gm[:, c].astype(f32)
-            delta = head_sums(grad * mixf[:, c]) * linv[:, c]
-            grad = grad * linv[:, c]
             lane = lanes((tok, 128))
-            for half in range(2):
-                d = roll_half(delta) if half == 0 else delta
-                v = grad if half == 0 else roll_half(grad)
-                high = d.astype(bf16).astype(f32)
-                rest = jnp.where(lane == 64, -high, jnp.where(lane == 65, high - d, 0.0))
-                aug[pl.ds(half * tok, tok), :] = jnp.where(low, v, rest).astype(bf16)
-
+            for k in range(2):
+                c = cols(2 * g + k, 128)
+                grad = gm[:, c].astype(f32)
+                delta = head_sums(grad * mixf[:, c]) * linv[:, c]
+                grad = grad * linv[:, c]
+                for half in range(2):
+                    d = roll_half(delta) if half == 0 else delta
+                    v = grad if half == 0 else roll_half(grad)
+                    high = d.astype(bf16).astype(f32)
+                    rest = jnp.where(lane == 64, -high, jnp.where(lane == 65, high - d, 0.0))
+                    aug[pl.ds((2 * k + half) * tok, tok), :] = jnp.where(low, v, rest).astype(bf16)
+
+        q = q2[pl.ds(2 * g, 2)].reshape(4 * tok, 128)
         seen = mask_t[rows, :]
-        e = jnp.exp2(dot_t(kk[g, rows, :], q2[t]) * LOG2E).astype(bf16)
-        e = e * jnp.concatenate([seen, seen], axis=1)
+        e = jnp.exp2(dot_t(kk[g, rows, :], q) * LOG2E).astype(bf16)
+        e = e * jnp.concatenate([seen] * 4, axis=1)
+        ds = e * dot_t(va[g, rows, :], aug[...]).astype(bf16)
         dv = dot(e, aug[...])
-        ds = e * dot_t(va[g, rows, :], aug[...]).astype(bf16)
-        dk = dot(ds, q2[t])
+        dk = dot(ds, q)
         dq = lax.dot_general(kk[g, rows, :], ds, (((0,), (0,)), ((), ())), preferred_element_type=f32)
-
-        @pl.when(t % 2 == 0)
-        def _():
-            acc_k[rows, :] = dk
-            acc_v[rows, :] = dv
-
-        @pl.when(t % 2 == 1)
-        def _():
-            both_k = acc_k[rows, :] + dk
-            both_v = acc_v[rows, :] + dv
-            both_k = both_k + roll_half(both_k)
-            lower = lanes((chunk, 128)) < 64
-            both_v = jnp.where(lower, both_v, roll_half(both_v))
-            mine = (lanes((chunk, 128)) // 64) == (g % 2)
-            for b in range(chunk // tok):
-                spot = kc * (chunk // tok) + b
-                y, x, c = spot // 4, (spot // 2) % 2, spot % 2
-                cut = slice(b * tok, (b + 1) * tok)
-                for base, value in ((0, both_k), (kv_w, both_v)):
-                    place = pl.ds(pl.multiple_of(base + (g // 2) * 128, 128), 128)
-                    old = terms[y, x, c, :, place].astype(f32)
-                    terms[y, x, c, :, place] = jnp.where(mine[cut], value[cut], old).astype(bf16)
+        dk = dk + roll_half(dk)
+        lower = lanes((chunk, 128)) < 64
+        dv = jnp.where(lower, dv, roll_half(dv))
+        mine = (lanes((chunk, 128)) // 64) == (g % 2)
+        for b in range(chunk // tok):
+            spot = kc * (chunk // tok) + b
+            y, x, c = spot // 4, (spot // 2) % 2, spot % 2
+            cut = slice(b * tok, (b + 1) * tok)
+            for base, value in ((0, dk), (kv_w, dv)):
+                place = pl.ds(pl.multiple_of(base + (g // 2) * 128, 128), 128)
+                old = terms[y, x, c, :, place].astype(f32)
+                terms[y, x, c, :, place] = jnp.where(mine[cut], value[cut], old).astype(bf16)
 
         @pl.when(kc == 0)
         def _():
@@ -1380,8 +1397,9 @@
         @pl.when(kc == n_chunk - 1)
         def _():
             turned = jnp.transpose(acc_q[...])
-            gh[:, cols(t, 128)] = jnp.where(low, turned[:tok], turned[tok:]) * 0.125
-
+            for k in range(2):
+                even, odd = [turned[(2 * k + h) * tok : (2 * k + h + 1) * tok] for h in range(2)]
+                gh[:, cols(2 * g + k, 128)] = jnp.where(low, even, odd) * 0.125
 
     def head_back(t, grad, gain, row):
         c = cols(t, 128)
@@ -1390,7 +1408,7 @@
         unit = u * inv
         grad = grad * cos_ref[...] - swap_rot(grad) * sin_ref[...]
         gains[pl.ds(row, 1), pl.ds(0, 128)] += jnp.sum(grad * unit, axis=0, keepdims=True)
-        gg = grad * gain[...]
+        gg = grad * gain
         gattn2[own, c] = (inv * (gg - unit * head_sums(gg * unit) * (1.0 / 64))).astype(bf16)
 
     def query_back(t):
@@ -1479,7 +1497,7 @@
             steps[f"he{i}"] = part(hop_end, i)
     loops = {
         "H": (8, h_step),
-        "B": (heads_w // 128 * n_chunk, attend),
+        "B": (GROUPS * n_chunk, attend),
         "Q": (heads_w // 128, query_back),
         "G": (8, g_step),
     }
@@ -1492,8 +1510,8 @@
     sent_dx.wait()
 
 
-def backward(x, cosine, sine, g_attn, g_q, g_k, g_ffn, kept, rows, n_dev):
-    (t_attn, t_mix, t_ffn, t_act, cot2, ggu2, qkv, q2, linv, mixf, res, kk, va, mask_t, w_qkv, w_out, w_gu) = kept
+def backward(x, g_attn, g_q, g_k, g_ffn, kept, rows, n_dev):
+    (t_attn, t_mix, t_ffn, t_act, cot2, ggu2, qkv, q2, linv, mixf, res, kk, va, mask_t, w_qkv, w_out, w_gu, cosine, sine) = kept
     tok, width = x.shape
     heads_w, kv_w = HEADS * HEAD_DIM, GROUPS * HEAD_DIM
     ff = ggu2.shape[1] // 2
@@ -1513,7 +1531,7 @@
         VMEM(v.shape, v.dtype)
         for v in (t_ffn, t_act, cot2, ggu2, qkv, q2, linv, mixf, kk, va, mask_t, w_gu)
     ]
-    dx, grad_attn, grad_q, grad_k, grad_ffn, own_qkv, own_out, own_gu, own_down = pl.pallas_call(
+    return pl.pallas_call(
         functools.partial(backward_kernel, dims),
         out_shape=[
             shape((tok, width), bf16),
@@ -1536,10 +1554,8 @@
             VMEM((3 + NZ, 8, width), f32),
             VMEM((tok, width), f32),
             VMEM((2 * tok, width), bf16),
-            VMEM((length, 128), f32),
-            VMEM((length, 128), f32),
-            VMEM((128, 2 * tok), f32),
-            VMEM((2 * tok, 128), bf16),
+            VMEM((128, 4 * tok), f32),
+            VMEM((4 * tok, 128), bf16),
             VMEM((tok, heads_w), bf16),
             VMEM((2, 2, 2, tok, 2 * kv_w), bf16),
             dma((4, 16, NZ)),
@@ -1568,7 +1584,30 @@
         cosine, sine, g_attn, g_q, g_k, g_ffn, x, t_attn, t_mix, t_ffn, t_act, cot2, ggu2, qkv, q2,
         linv, mixf, res, kk, va, mask_t, w_qkv, w_out, w_gu,
     )
-    return dx, grad_attn[0], own_qkv, grad_q[0], grad_k[0], own_out, grad_ffn[0], own_gu, own_down
+
+
+def settle_kernel(count, *refs):
+    copies = [
+        pltpu.make_async_copy(a, b, refs[-1].at[k])
+        for k, (a, b) in enumerate(zip(refs[:count], refs[count : 2 * count]))
+    ]
+    for c in copies:
+        c.start()
+    for c in copies:
+        c.wait()
+
+
+def settle(arrays):
+    count = len(arrays)
+    anyw = pl.BlockSpec(memory_space=pl.ANY)
+    return pl.pallas_call(
+        functools.partial(settle_kernel, count),
+        out_shape=[jax.ShapeDtypeStruct(a.shape, a.dtype) for a in arrays],
+        in_specs=[pl.BlockSpec(memory_space=VMEM)] * count,
+        out_specs=[anyw] * count,
+        scratch_shapes=[pltpu.SemaphoreType.DMA((count,))],
+        name="settle",
+    )(*arrays)
 
 
 epsilon = 1e-06
@@ -1811,24 +1850,23 @@
     inputs, places, cotangent, attn_gain, w_qkv, q_gain, k_gain, w_out, ffn_gain, w_gateup, w_down
 ):
     n_dev = lax.axis_size("ctx")
-    own_places = places[0]
     half = HEAD_DIM // 2
-    spot = jnp.arange(128)
-    frequency = jnp.exp((spot % half).astype(f32) * (-2.0 * math.log(10000.0) / HEAD_DIM))
-    angles = own_places.astype(f32)[:, None] * frequency[None, :]
-    cosine = jnp.cos(angles)
-    sine = jnp.where(spot % HEAD_DIM < half, -1.0, 1.0) * jnp.sin(angles)
-    block_row = (own_places // 128)[None, :]
-    gain_q, gain_k = jnp.tile(q_gain, 2)[None], jnp.tile(k_gain, 2)[None]
+    spot = np.arange(128) % half
+    step = np.float32(-2.0 * math.log(10000.0) / HEAD_DIM)
+    frequency = np.exp(spot.astype(np.float32) * step).astype(np.float32)[None]
+    gain_q, gain_k = q_gain[None], k_gain[None]
     layer_output, *kept = forward(
-        inputs[0], cotangent[0], block_row, cosine, sine, attn_gain[None], gain_q, gain_k,
+        inputs[0], cotangent[0], places, frequency, attn_gain[None], gain_q, gain_k,
         ffn_gain[None], w_qkv, w_out, w_down, w_gateup, n_dev,
     )
     rows = [w.shape[0] for w in (w_qkv, w_out, w_gateup, w_down)]
-    grad_inputs, *grads = backward(
-        inputs[0], cosine, sine, attn_gain[None], gain_q, gain_k, ffn_gain[None], kept, rows, n_dev
-    )
-    return (layer_output[None], grad_inputs[None], *grads)
+    grads = backward(inputs[0], attn_gain[None], gain_q, gain_k, ffn_gain[None], kept, rows, n_dev)
+    layer_output, dx, g_attn, g_q, g_k, g_ffn, d_qkv, d_out, d_gu, d_down = settle(
+        [layer_output, *grads]
+    )
+    return (
+        layer_output[None], dx[None], g_attn[0], d_qkv, g_q[0], g_k[0], d_out, g_ffn[0], d_gu, d_down
+    )
 
 
 def solution(mesh):

time: 262 us -> 242 us (0.924)
  local copies, waits for them, and re-layouts: 11.1 us -> 0 us
  Pallas kernels: 248 us -> 241 us
    pallas_call x1, Pallas kernels: 128 us -> 117 us  [backward(): pl.pallas_call(functools.partial(backward_kernel, dims), out_shape=[shape...]
    unnamed x28 -> x0, local copies, waits for them, and re-layouts: 8.6 us -> none
    pallas_call x0 -> x1, Pallas kernels: none -> 3.87 us  [settle(): pl.pallas_call(functools.partial(settle_kernel, count), out_shape=[jax.Sh...]
where the time goes in v3:
time: 242 us
  Pallas kernels  241 us (100%)
    pallas_call x1, Pallas kernels, forward(): pl.pallas_call(functools.partial(forward_kernel, (tok, width, n_dev, head...  120 us
    pallas_call x1, Pallas kernels, backward(): pl.pallas_call(functools.partial(backward_kernel, dims), out_shape=[shape...  117 us

profile of v3, /device:TPU:0, one launch (start us, length us, event | category | flops | bytes accessed | tf_op | source)
XLA Modules:
  0.0 241.9 jit_solution(17186174191494091319)
XLA Ops:
  0.6 120.1 %forward.1 = (bf16[256,2048]{1,0:T(8,128)(2,1)}, bf16[16,64,512]{2,1,0:T(8,128)(2,1)}, bf16[16,32,512]{2,1,0:T(8,128)(2,1)}, bf16[16,64,512]{2,1,0:T(8,128)(2,1)...) custom-call(bf16[256,2048]{1,0:T(8,128)(2,1)} %bitcast.13, ...), custom_call_target="tpu_custom_call" | custom-call | flops 9126805504 | bytes 52428800 | tf_op jit(solution)/shard_map/forward/pallas_call | solution.py:843
  120.8 117.1 %backward.1 = (bf16[256,2048]{1,0:T(8,128)(2,1)}, f32[1,2048]{1,0:T(1,128)}, f32[1,64]{1,0:T(1,128)}, f32[1,64]{1,0:T(1,128)}, f32[1,2048]{1,0:T(1,128)}, /*inde...) custom-call(f32[256,128]{1,0:T(8,128)} %get-tuple-element.50.refs_0_, ...), custom_call_target="tpu_custom_call" | custom-call | flops 21474836480 | bytes 62914560 | tf_op jit(solution)/shard_map/backward/pallas_call | solution.py:1534
  237.9 3.9 %settle.1 = (bf16[256,2048]{1,0:T(8,128)(2,1)}, bf16[256,2048]{1,0:T(8,128)(2,1)}, f32[1,2048]{1,0:T(1,128)}, f32[1,64]{1,0:T(1,128)}, f32[1,64]{1,0:T(1,128)}, ...) custom-call(bf16[256,2048]{1,0:T(8,128)(2,1)} %get-tuple-element.49., ...), custom_call_target="tpu_custom_call" | custom-call | tf_op jit(solution)/shard_map/settle/pallas_call | solution.py:1603

commit v4 on v3

--- a/solution.py
+++ b/solution.py
@@ -15,31 +15,65 @@
 FF = 1024
 
 
+(
+    f_qZ, f_qp0, f_qp1, f_qp2, f_qp3, f_qe0, f_qe1, f_qe2, f_qe3, f_qc0, f_qc1, f_qc2, f_qc3,
+    f_qz0, f_qz1, f_qz2, f_qz3, f_dZ, f_dp0, f_dp1, f_dp2, f_dp3, f_de0, f_de1, f_de2, f_de3,
+    f_dc0, f_dc1, f_dc2, f_dc3, f_dz0, f_dz1, f_dz2, f_dz3, f_gZ, f_gp0, f_gp1, f_gp2, f_gp3,
+    f_ge0, f_ge1, f_ge2, f_ge3, f_gc0, f_gc1, f_gc2, f_gc3, f_gz0, f_gz1, f_gz2, f_gz3, f_qs0,
+    f_qs1, f_qs2, f_qs3, f_gs0, f_gs1, f_gs2, f_gs3, f_ds0, f_ds1, f_ds2, f_ds3, f_oc0, f_oc1,
+    f_oc2, f_oc3, f_oz00, f_oz01, f_oz02, f_oz03, f_oz10, f_oz11, f_oz12, f_oz13, f_oz20, f_oz21,
+    f_oz22, f_oz23, f_oz30, f_oz31, f_oz32, f_oz33, f_kc0, f_kc1, f_kc2, f_kc3, f_kz00, f_kz01,
+    f_kz02, f_kz03, f_kz10, f_kz11, f_kz12, f_kz13, f_kz20, f_kz21, f_kz22, f_kz23, f_kz30,
+    f_kz31, f_kz32, f_kz33, f_kP, f_kZ, f_ke, f_kD, f_A, f_norm, f_trig, f_turn, f_keys, f_query,
+    f_kve, f_kvc, f_unpack, f_mix, f_res, f_norm2, f_turn2, f_gate, f_act, f_y, f_oP, f_oZ, f_oe,
+    f_oD,
+) = range(127)
+
+(
+    b_df, b_da0, b_da1, b_da2, b_da3, b_db0, b_db1, b_db2, b_db3, b_dd0, b_dd1, b_dd2, b_dd3,
+    b_dx0, b_dx1, b_dx2, b_dx3, b_dz0, b_dz1, b_dz2, b_dz3, b_gf, b_ga0, b_ga1, b_ga2, b_ga3,
+    b_gb0, b_gb1, b_gb2, b_gb3, b_gd0, b_gd1, b_gd2, b_gd3, b_gx0, b_gx1, b_gx2, b_gx3, b_gz0,
+    b_gz1, b_gz2, b_gz3, b_qf, b_qa0, b_qa1, b_qa2, b_qa3, b_qb0, b_qb1, b_qb2, b_qb3, b_qd0,
+    b_qd1, b_qd2, b_qd3, b_qx0, b_qx1, b_qx2, b_qx3, b_qz0, b_qz1, b_qz2, b_qz3, b_dw0, b_dw1,
+    b_dw2, b_dw3, b_gw0, b_gw1, b_gw2, b_gw3, b_ow0, b_ow1, b_ow2, b_ow3, b_qw0, b_qw1, b_qw2,
+    b_qw3, b_oa0, b_oa1, b_oa2, b_oa3, b_oo0, b_oo1, b_oo2, b_oo3, b_hs0, b_hs1, b_hs2, b_he0,
+    b_he1, b_he2, b_oz00, b_oz01, b_oz02, b_oz03, b_oz10, b_oz11, b_oz12, b_oz13, b_oz20, b_oz21,
+    b_oz22, b_oz23, b_ka0, b_ka1, b_ka2, b_ka3, b_ko0, b_ko1, b_ko2, b_ko3, b_kz00, b_kz01,
+    b_kz02, b_kz03, b_kz10, b_kz11, b_kz12, b_kz13, b_kz20, b_kz21, b_kz22, b_kz23, b_kS, b_ke,
+    b_kf, b_H, b_B, b_Q, b_G, b_h, b_nb, b_m, b_att, b_kvs, b_kvc, b_kve, b_kvf, b_oS, b_oe, b_of,
+    b_lm, b_ll, b_qe, b_g, b_nb2, b_rs, b_re,
+) = range(150)
+
 FORWARD_ORDER = [
-    "qp0", "oP", "qZ", "dZ", "qz1", "qe0", "qp1", "dp0", "qz2", "gZ", "trig", "qp2", "norm",
-    "qc0", "qe1", "turn", "qz3", "dz1", "qp3", "qe2", "gz1", "gz2", "oZ", "qc1", "qe3", "oe",
-    "qc2", "gp2", "qs0", "qc3", "oz10", "oD", "qs1", "qs2", "qs3", "keys", "de0", "gz3", "oz11",
-    "kve", "gp0", "oz12", "ge2", "dz2", "query", "oz22", "kvc", "gp1", "dc0", "oz13", "gp3",
-    "oz21", "unpack", "oz32", "A", "dp2", *["A"] * 3, "oz31", *["A"] * 5, "oz20", *["A"] * 4,
-    "ge0", "A", "oz30", "ge1", "A", "gc2", *["A"] * 4, "oz23", *["A"] * 5, "dp1", "oc1", "oz33",
-    *["A"] * 2, "oc3", "ge3", "A", "oc2", "de2", "A", "dz3", *["A"] * 2, "gc1", "dp3", "A", "gc0",
-    "A", "res", "norm2", "gc3", "de1", "gs0", "ds0", "mix", "gs1", "de3", "dc2", "gs2", "dc1",
-    "gs3", "dc3", "turn2", "ds1", "ds2", "ds3", "gate", "act", "y",
+    f_kP, f_qZ, f_qp0, f_oP, f_norm, f_oZ, f_qz1, f_qp1, f_qe0, f_qz2, f_trig, f_oz10, f_dZ,
+    f_qp2, f_oz20, f_qz3, f_qe1, f_qp3, f_turn, f_gZ, f_qe2, f_ke, f_kZ, f_qc0, f_qe3, f_oe,
+    f_qc1, f_qs0, f_gp0, f_qc2, f_qc3, f_qs1, f_qs2, f_oD, f_gz1, f_dz1, f_qs3, f_keys, f_dz2,
+    f_dp2, f_gz2, f_dp1, f_kve, f_gp1, f_gz3, f_kz11, f_query, f_de1, f_gp2, f_dz3, f_oz12,
+    f_kz10, f_oz11, f_oz13, f_kvc, f_dp0, f_oz22, f_kz12, f_ge0, f_kD, f_gp3, f_unpack, f_oz23,
+    *[f_A] * 5, f_kz22, *[f_A] * 2, f_oz21, *[f_A] * 3, f_ge2, f_oc1, f_ge1, f_A, f_oz30,
+    *[f_A] * 5, f_kz20, f_gc0, *[f_A] * 2, f_oz31, f_A, f_de2, *[f_A] * 3, f_oc2, f_dp3, f_oz32,
+    *[f_A] * 6, f_oz33, f_oc3, f_dc1, *[f_A] * 2, f_kz13, f_ge3, f_kc1, f_gc2, f_kz32, *[f_A] * 2,
+    f_gc1, f_de0, f_dc2, f_kz30, f_res, f_kz21, f_de3, f_mix, f_kz23, f_gc3, f_norm2, f_kz33,
+    f_gs0, f_dc0, f_gs1, f_kz31, f_kc3, f_gs2, f_dc3, f_kc2, f_turn2, f_ds0, f_gs3, f_ds1, f_ds2,
+    f_ds3, f_gate, f_act, f_y,
 ]
 
 BACKWARD_ORDER = [
-    "dw0", "dw1", "gw0", "dw2", "gw1", "dw3", "h", "gb0", *["H"] * 8, "ga1", "nb", "lm", "db0",
-    "db2", "ga0", "gw2", "db1", "da2", "da0", "m", "ow0", "ow1", "oa0", "gd1", "att", "B", "ga2",
-    "gw3", "B", "oz00", "B", "dd0", "gd0", "oa1", "B", "da1", *["B"] * 2, "oz03", "B", "gb3",
-    "oz01", "da3", "ow2", "dx0", "ga3", "oa2", "gb1", "ll", "B", "gd2", "ow3", *["B"] * 4, "oz13",
-    "dd1", "B", "gx0", *["B"] * 2, "gb2", "oz02", "B", "kvs", "dx1", "Q", "dd3", "dd2", "Q",
-    "dz0", "Q", "kvc", "Q", "dz1", "Q", "oz23", "Q", "oz10", "oz12", "Q", "oz22", "Q", "oz11",
-    "kve", "dx2", "db3", "gd3", "oz21", "gz0", "kvf", "g", *["G"] * 2, "qe", "qw0", "qa0", "gx2",
-    "qw1", "qw2", "qb0", "G", "dz2", "G", "oz20", "oa3", "qa1", "gx1", "qb1", "G", "qa2", "G",
-    "qb2", *["G"] * 2, "gz1", "qd0", "nb2", "qw3", "gz2", "oo0", "hs0", "qd1", "he0", "oo3",
-    "oo1", "hs1", "qb3", "qd2", "qx0", "oo2", "qz0", "df", "he1", "qx1", "hs2", "qa3", "qz1",
-    "oS", "he2", "qx2", "rs", "qz2", "qd3", "oe", "of", "gf", "qf", "re",
+    b_dw0, b_dw1, b_dw2, b_da1, b_ka1, b_dw3, b_gw0, b_gw1, b_ka0, b_h, *[b_H] * 6, b_ga0,
+    *[b_H] * 2, b_nb, b_lm, b_gw2, b_gw3, b_gb1, b_kz03, b_gb0, b_m, b_db1, b_att, b_gb2, b_kz02,
+    b_da2, b_ow0, b_B, b_oa0, *[b_B] * 2, b_ow1, *[b_B] * 2, b_kz13, b_B, b_da0, b_ga2, b_ll, b_B,
+    b_oa1, b_ga1, b_B, b_gd0, b_B, b_gd2, b_kz00, b_kz01, b_B, b_ow2, b_B, b_gb3, b_B, b_oa2,
+    b_ga3, *[b_B] * 3, b_oz01, b_gd1, b_ow3, b_B, b_kvs, b_Q, b_da3, b_ka2, b_kz12, b_dd1, b_kz22,
+    b_kz23, b_kz11, b_Q, b_dd0, b_db0, b_Q, b_db3, b_Q, b_oz00, b_gx0, b_dx1, b_oz10, b_oz11,
+    b_kvc, b_kz10, b_oz03, *[b_Q] * 2, b_oz21, b_oz13, b_Q, b_kz21, b_Q, b_kve, b_gd3, b_gz0,
+    b_kvf, b_kz20, b_ko3, b_dd2, b_g, b_db2, b_gx1, b_oz02, b_gx2, b_dd3, b_G, b_dx0, b_G, b_dz0,
+    b_qe, b_ko1, b_qw0, b_qa0, b_qb0, b_oz20, b_dx2, b_oz23, b_oz12, b_qw1, b_qw2, b_dz1, b_qa1,
+    b_qb1, b_G, b_oz22, b_qa2, b_dz2, *[b_G] * 2, b_qd0, b_gz1, b_ko0, b_qw3, b_qb2, *[b_G] * 2,
+    b_ko2, b_gz2, b_G, b_qd1, b_nb2, b_oo3, b_hs0, b_kS, b_oo1, b_oo2, b_qd2, b_qx0, b_he0, b_oo0,
+    b_qz0, b_hs1, b_qx1, b_oS, b_qa3, b_qz1, b_he1, b_hs2, b_qx2, b_df, b_gf, b_ka3, b_qz2, b_ke,
+    b_oe, b_he2, b_rs, b_qb3, b_oa3, b_qd3, b_qf, b_kf, b_re, b_of,
 ]
+
 
 f32 = jnp.float32
 bf16 = jnp.bfloat16
@@ -120,13 +154,20 @@
     return pl.ds(0, rows // 2), pl.ds(rows // 2, rows // 2)
 
 
+def cuts(shape, some=None):
+    rows, columns = shape[-2:]
+    if some is None:
+        return (pl.ds(0, rows),), tuple((h,) for h in halves(rows))
+    return (some,), tuple((some, h) for h in halves(columns))
+
+
 KZ, KX, KY, KD0, KD1, KS, KU = range(7)
 
 
 class Gather:
-    def __init__(self, pc, buf, send, recv):
+    def __init__(self, pc, buf, send, recv, some=None):
         self.pc, self.buf, self.send, self.recv = pc, buf, send, recv
-        self.h = halves(buf.shape[-2])
+        self.full, self.h = cuts(buf.shape, some)
 
     def cp(self, idx, dev, ks, kr, slot):
         ref = self.buf.at[idx]
@@ -134,31 +175,31 @@
 
     def c_up(self, z0):
         p = self.pc
-        return self.cp((z0, p.y, p.x, p.core), p.up(), KU, KZ, z0)
+        return self.cp((z0, p.y, p.x, p.core, *self.full), p.up(), KU, KZ, z0)
 
     def c_down(self, z0):
         p = self.pc
-        return self.cp((z0, p.y, p.x, p.core), p.down(), KZ, KZ, z0)
+        return self.cp((z0, p.y, p.x, p.core, *self.full), p.down(), KZ, KZ, z0)
 
     def c_x(self, z0):
         p = self.pc
-        return self.cp((z0, p.y, p.x, p.core), p.xn(), KX, KX, z0)
+        return self.cp((z0, p.y, p.x, p.core, *self.full), p.xn(), KX, KX, z0)
 
     def c_y(self, z0):
         p = self.pc
-        return self.cp((z0, p.y, p.x, p.core), p.yn(), KY, KY, z0)
+        return self.cp((z0, p.y, p.x, p.core, *self.full), p.yn(), KY, KY, z0)
 
     def c_d0(self, z0):
         p = self.pc
-        return self.cp((z0, p.y, 1 - p.x, p.core, self.h[0]), p.yn(), KD0, KD0, z0)
+        return self.cp((z0, p.y, 1 - p.x, p.core, *self.h[0]), p.yn(), KD0, KD0, z0)
 
     def c_d1(self, z0):
         p = self.pc
-        return self.cp((z0, 1 - p.y, p.x, p.core, self.h[1]), p.xn(), KD1, KD1, z0)
+        return self.cp((z0, 1 - p.y, p.x, p.core, *self.h[1]), p.xn(), KD1, KD1, z0)
 
     def c_s(self, z0):
         p = self.pc
-        return self.cp((z0, slice(None), slice(None), p.core), p.sn(), KS, KS, z0)
+        return self.cp((z0, slice(None), slice(None), p.core, *self.full), p.sn(), KS, KS, z0)
 
     def plane_send(self, i):
         z0 = near(self.pc.z, i)
@@ -231,9 +272,9 @@
 
 
 class GatherPlane:
-    def __init__(self, pc, buf, send, recv):
+    def __init__(self, pc, buf, send, recv, some=None):
         self.pc, self.buf, self.send, self.recv = pc, buf, send, recv
-        self.h = halves(buf.shape[-2])
+        self.full, self.h = cuts(buf.shape, some)
 
     def cp(self, idx, dev, s, r):
         ref = self.buf.at[idx]
@@ -245,33 +286,33 @@
 
     def c_x(self):
         p = self.pc
-        return self.cp((p.z, p.y, p.x, p.core), p.xn(), (KX, 0), (KX, 0))
+        return self.cp((p.z, p.y, p.x, p.core, *self.full), p.xn(), (KX, 0), (KX, 0))
 
     def c_y(self):
         p = self.pc
-        return self.cp((p.z, p.y, p.x, p.core), p.yn(), (KY, 0), (KY, 0))
+        return self.cp((p.z, p.y, p.x, p.core, *self.full), p.yn(), (KY, 0), (KY, 0))
 
     def c_d0(self):
         p = self.pc
-        return self.cp((p.z, p.y, 1 - p.x, p.core, self.h[0]), p.yn(), (KD0, 0), (KD0, 0))
+        return self.cp((p.z, p.y, 1 - p.x, p.core, *self.h[0]), p.yn(), (KD0, 0), (KD0, 0))
 
     def c_d1(self):
         p = self.pc
-        return self.cp((p.z, 1 - p.y, p.x, p.core, self.h[1]), p.xn(), (KD1, 0), (KD1, 0))
+        return self.cp((p.z, 1 - p.y, p.x, p.core, *self.h[1]), p.xn(), (KD1, 0), (KD1, 0))
 
     def c_up(self, z0, k):
         p = self.pc
         y, x = self.yx(k)
-        return self.cp((z0, y, x, p.core), p.up(), (10 + z0, k), (10 + z0, k))
+        return self.cp((z0, y, x, p.core, *self.full), p.up(), (10 + z0, k), (10 + z0, k))
 
     def c_down(self, z0, k):
         p = self.pc
         y, x = self.yx(k)
-        return self.cp((z0, y, x, p.core), p.down(), (14 + z0, k), (10 + z0, k))
+        return self.cp((z0, y, x, p.core, *self.full), p.down(), (14 + z0, k), (10 + z0, k))
 
     def c_s(self, z0):
         p = self.pc
-        return self.cp((z0, slice(None), slice(None), p.core), p.sn(), (KS, z0), (KS, z0))
+        return self.cp((z0, slice(None), slice(None), p.core, *self.full), p.sn(), (KS, z0), (KS, z0))
 
     def z_send(self, k):
         z = self.pc.z
@@ -490,15 +531,15 @@
         lax.fori_loop(0, count, tick, 0)
 
 
-def line_steps(letter, g):
+def line_steps(first, g):
     part = functools.partial
-    steps = {letter + "Z": g.own_z}
+    steps = {first: g.own_z}
     for i in range(NZ):
-        steps[f"{letter}p{i}"] = part(g.plane_send, i)
-        steps[f"{letter}e{i}"] = part(g.plane_event, i)
-        steps[f"{letter}c{i}"] = part(g.core_event, i)
+        steps[first + 1 + i] = part(g.plane_send, i)
+        steps[first + 5 + i] = part(g.plane_event, i)
+        steps[first + 9 + i] = part(g.core_event, i)
         if i:
-            steps[f"{letter}z{i}"] = part(g.z_event, i, False)
+            steps[first + 13 + i] = part(g.z_event, i, False)
     return steps
 
 
@@ -542,7 +583,9 @@
         c.wait()
     qkv = Gather(pc, w_qkv, send.at[0], recv.at[0])
     out = GatherPlane(pc, w_out, send.at[1], recv.at[1])
-    down = Gather(pc, w_down, send.at[2], recv.at[2])
+    half = s_down.shape[0] // 2
+    down = Gather(pc, w_down, send.at[2], recv.at[2], pl.ds(0, half))
+    rest = GatherPlane(pc, w_down, send.at[4], recv.at[4], pl.ds(half, half))
     gateup = Gather(pc, w_gu, send.at[3], recv.at[3])
     seq = GatherSequence(pc, kvb, kv_send, kv_recv)
     part = functools.partial
@@ -608,6 +651,7 @@
 
     def grad_act_step(i):
         down.done_event(i)
+        rest.done_event(i)
         z0 = near(z, i)
         depth = ff // NZ
         gact[:, cols(z0, depth)] = dot_t(cot_ref[...], w_down[z0].reshape(depth, width))
@@ -779,24 +823,27 @@
         emit(t_act, o_tact)
 
     steps = {
-        "norm": first_norm, "trig": tables, "turn": first_turn, "keys": keys_out, "query": queries,
-        "kve": seq.plane_event, "kvc": seq.core_event, "unpack": unpack_all, "mix": mix_out,
-        "res": residual, "norm2": second_norm, "turn2": second_turn, "gate": gates,
-        "act": act_out, "y": outputs, "oP": out.own_plane, "oZ": out.own_z, "oe": out.plane_event,
-        "oD": out.diag_event,
+        f_norm: first_norm, f_trig: tables, f_turn: first_turn, f_keys: keys_out, f_query: queries,
+        f_kve: seq.plane_event, f_kvc: seq.core_event, f_unpack: unpack_all, f_mix: mix_out,
+        f_res: residual, f_norm2: second_norm, f_turn2: second_turn, f_gate: gates,
+        f_act: act_out, f_y: outputs, f_oP: out.own_plane, f_oZ: out.own_z, f_oe: out.plane_event,
+        f_oD: out.diag_event, f_kP: rest.own_plane, f_kZ: rest.own_z, f_ke: rest.plane_event,
+        f_kD: rest.diag_event,
     }
-    for letter, g in (("q", qkv), ("d", down), ("g", gateup)):
-        steps.update(line_steps(letter, g))
+    for first, g in ((f_qZ, qkv), (f_dZ, down), (f_gZ, gateup)):
+        steps.update(line_steps(first, g))
     for i in range(NZ):
-        steps[f"qs{i}"] = part(columns_step, qkv, i, hattn_ref, w_qkv, qkv_ref, width // NZ)
-        steps[f"gs{i}"] = part(columns_step, gateup, i, hffn_ref, w_gu, gu, width // NZ)
-        steps[f"ds{i}"] = part(grad_act_step, i)
+        steps[f_qs0 + i] = part(columns_step, qkv, i, hattn_ref, w_qkv, qkv_ref, width // NZ)
+        steps[f_gs0 + i] = part(columns_step, gateup, i, hffn_ref, w_gu, gu, width // NZ)
+        steps[f_ds0 + i] = part(grad_act_step, i)
         if i:
-            steps[f"oc{i}"] = part(out.core_event, i)
+            steps[f_oc0 + i] = part(out.core_event, i)
+            steps[f_kc0 + i] = part(rest.core_event, i)
             for k in range(4):
-                steps[f"oz{i}{k}"] = part(out.z_event, i, k)
-    run_steps(FORWARD_ORDER, steps, {"A": (heads_w // 128 * n_chunk, attend)})
-    for g in (qkv, out, down, gateup, seq):
+                steps[f_oz00 + 4 * i + k] = part(out.z_event, i, k)
+                steps[f_kz00 + 4 * i + k] = part(rest.z_event, i, k)
+    run_steps(FORWARD_ORDER, steps, {f_A: (heads_w // 128 * n_chunk, attend)})
+    for g in (qkv, out, down, rest, gateup, seq):
         g.finish()
     for c in (sent_cot, sent_ffn, sent_act, sent_ggu):
         c.wait_send()
@@ -872,8 +919,8 @@
             *[VMEM(*t) for t in turned],
             VMEM((spots, qkv_rows, tok), bf16),
             VMEM((spots, out_rows, tok), bf16),
-            dma((4, 18, NZ)),
-            dma((4, 14, NZ)),
+            dma((5, 18, NZ)),
+            dma((5, 14, NZ)),
             dma((8,)),
             dma((8,)),
             dma((4,)),
@@ -957,19 +1004,20 @@
 
 
 class Scatter(PlaneSum):
-    def __init__(self, pc, part, bufs, out, send, recv):
+    def __init__(self, pc, part, bufs, out, send, recv, some=None):
         rd, rx, ry, self.zz = bufs
         self.plane_setup(pc, rd, rx, ry, send, recv)
         self.part, self.out = part, out
-        self.h = halves(part.shape[-2])
+        self.full, self.h = cuts(part.shape, some)
 
     @staticmethod
-    def scratch(rows, columns):
-        half = VMEM((NZ, 2, rows // 2, columns), bf16)
-        return [half, half, half, VMEM((NZ + 1, 2, rows // 2, columns), bf16)]
+    def scratch(rows, columns, wide=True):
+        shape = (2, rows // 2, columns) if wide else (2, rows, columns // 2)
+        half = VMEM((NZ, *shape), bf16)
+        return [half, half, half, VMEM((NZ + 1, *shape), bf16)]
 
     def piece(self, s, y, x, k):
-        return self.part.at[s, y, x, self.h[k]]
+        return self.part.at[(s, y, x, *self.h[k])]
 
     def down(self, zp):
         return self.cp(self.rx.at[zp], self.zz.at[zp], self.pc.down(), SA, zp)
@@ -1020,19 +1068,19 @@
         z = self.pc.z
         self.plane_arrived(z)
         for k in range(2):
-            self.out[self.h[k], :] = self.plane_total(z, k)
+            self.out[self.h[k]] = self.plane_total(z, k)
 
         @pl.when(z < NZ - 1)
         def _():
             self.down(z).wait_recv()
             for k in range(2):
-                self.out[self.h[k], :] += self.zz[z, k].astype(f32)
+                self.out[self.h[k]] += self.zz[z, k].astype(f32)
 
         @pl.when(z > 0)
         def _():
             self.up(z).wait_recv()
             for k in range(2):
-                self.out[self.h[k], :] += self.zz[NZ, k].astype(f32)
+                self.out[self.h[k]] += self.zz[NZ, k].astype(f32)
 
     def finish(self):
         z = self.pc.z
@@ -1049,19 +1097,23 @@
 
 
 class ScatterZ(PlaneSum):
-    def __init__(self, pc, part, bufs, out, send, recv):
+    def __init__(self, pc, part, bufs, out, send, recv, some=None):
         rd, rx, ry, self.zz, self.sm = bufs
+        wide = some is None
+        whole = pl.ds(0, self.sm.shape[-2])
+        axis = self.sm.shape[-2 if wide else -1]
+        self.inner = [(h,) if wide else (whole, h) for h in halves(axis)]
         self.plane_setup(pc, rd, rx, ry, send, recv)
         self.part, self.out = part, out
-        self.h = halves(part.shape[-2])
+        self.full, self.h = cuts(part.shape, some)
 
     @staticmethod
-    def scratch(rows, columns):
-        half = VMEM((1, 2, rows // 2, columns), bf16)
+    def scratch(rows, columns, wide=True):
+        half = VMEM((1, 2, rows // 2, columns) if wide else (1, 2, rows, columns // 2), bf16)
         return [half, half, half, VMEM((NZ + 1, 4, rows, columns), bf16), VMEM((4, rows, columns), bf16)]
 
     def piece(self, s, y, x, k):
-        return self.sm.at[y * 2 + x, self.h[k]]
+        return self.sm.at[(y * 2 + x, *self.inner[k])]
 
     def down(self, zp, k, src):
         return self.cp(src, self.zz.at[zp, k], self.pc.down(), 8 + zp, k)
@@ -1075,7 +1127,7 @@
         z = self.pc.z
         zp = far(z, i)
         for k in range(4):
-            src = self.part.at[zp, k // 2, k % 2]
+            src = self.part.at[(zp, k // 2, k % 2, *self.full)]
 
             @pl.when((z == NZ - 1) & (zp < z))
             def _():
@@ -1093,13 +1145,13 @@
         @pl.when((zp < z) & (z < NZ - 1))
         def _():
             self.down(zp, k, held).wait_recv()
-            self.zz[zp, k] = self.zz[zp, k] + self.part[zp, k // 2, k % 2]
+            self.zz[zp, k] = self.zz[zp, k] + self.part[(zp, k // 2, k % 2, *self.full)]
             self.down(zp, k, held).start()
 
         @pl.when((zp > z) & (z > 0))
         def _():
             self.up(zp, k, held).wait_recv()
-            self.zz[zp, k] = self.zz[zp, k] + self.part[zp, k // 2, k % 2]
+            self.zz[zp, k] = self.zz[zp, k] + self.part[(zp, k // 2, k % 2, *self.full)]
             self.up(zp, k, held).start()
 
     def own_event(self, k):
@@ -1113,7 +1165,7 @@
         def _():
             self.up(z, k, self.zz.at[z, k]).wait_recv()
 
-        own = self.part[z, k // 2, k % 2].astype(f32)
+        own = self.part[(z, k // 2, k % 2, *self.full)].astype(f32)
 
         @pl.when(z == 0)
         def _():
@@ -1137,7 +1189,7 @@
     def final(self):
         self.plane_arrived(0)
         for k in range(2):
-            self.out[self.h[k], :] = self.plane_total(0, k)
+            self.out[self.h[k]] = self.plane_total(0, k)
 
     def finish(self):
         z = self.pc.z
@@ -1204,16 +1256,16 @@
     lax.fori_loop(0, grad.shape[0] // 32, body, 0)
 
 
-def sum_steps(letter, g):
+def sum_steps(first, g):
     part = functools.partial
-    steps = {letter + "f": g.final}
+    steps = {first: g.final}
     for i in range(NZ):
-        steps[f"{letter}a{i}"] = part(g.far_event, i)
-        steps[f"{letter}b{i}"] = part(g.near_event, i)
-        steps[f"{letter}d{i}"] = part(g.d_event, i)
+        steps[first + 1 + i] = part(g.far_event, i)
+        steps[first + 5 + i] = part(g.near_event, i)
+        steps[first + 9 + i] = part(g.d_event, i)
         if i < NZ - 1:
-            steps[f"{letter}x{i}"] = part(g.xy_event, i)
-            steps[f"{letter}z{i}"] = part(g.z_event, i)
+            steps[first + 13 + i] = part(g.xy_event, i)
+            steps[first + 17 + i] = part(g.z_event, i)
     return steps
 
 
@@ -1243,12 +1295,12 @@
         i_x, i_tattn, i_tmix, i_tffn, i_tact, i_cot, i_ggu, i_qkv, i_q2, i_linv, i_mixf, i_res,
         i_kk, i_va, i_mask, i_wqkv, i_wout, i_wgu,
         o_dx, o_attn, o_q, o_k, o_ffn, out_wqkv, out_wout, out_wgu, out_wdown,
-        t_ffn, t_act, cot2, ggu2, qkv, q2, linv, mixf, kk, va, mask_t, w_gu,
+        t_ffn, t_act, cot2, ggu2, qkv, q2, linv, kk, va, mask_t, w_gu,
         part_qkv, part_out, part_gu, part_down, res, gains, came, gh, gattn2, acc_q,
         aug, gm, terms,
         send, recv, kv_send, kv_recv, ex_send, ex_recv, g_send, g_recv, lsem,
-    ) = refs[:67]
-    bufs = refs[67:]
+    ) = refs[:66]
+    bufs = refs[66:]
     g_q, g_k = twice(one_q), twice(one_k)
     pc = Place()
     z = pc.z
@@ -1268,7 +1320,6 @@
     load("ggu", lambda: i_ggu, lambda: ggu2)
     load("wgu", lambda: i_wgu, lambda: w_gu)
     load("res", lambda: i_res, lambda: res)
-    load("mixf", lambda: i_mixf, lambda: mixf)
     load("linv", lambda: i_linv, lambda: linv)
     load("q2", lambda: i_q2, lambda: q2)
     load("kk", lambda: i_kk, lambda: kk)
@@ -1282,7 +1333,9 @@
         there = pc.at(z=(z + k) % NZ)
         pl.semaphore_signal(bar, inc=1, device_id=there, device_id_type=MESH)
     pl.semaphore_wait(bar, 3 + NZ - 1)
-    down = Scatter(pc, part_down, bufs[0:4], out_wdown, send.at[0], recv.at[0])
+    cut = part_down.shape[-2] // 2
+    down = Scatter(pc, part_down, bufs[0:4], out_wdown, send.at[0], recv.at[0], pl.ds(0, cut))
+    rest = ScatterZ(pc, part_down, bufs[21:26], out_wdown, send.at[4], recv.at[4], pl.ds(cut, cut))
     gateup = Scatter(pc, part_gu, bufs[4:8], out_wgu, send.at[1], recv.at[1])
     out = ScatterZ(pc, part_out, bufs[8:13], out_wout, send.at[2], recv.at[2])
     last = Scatter(pc, part_qkv, bufs[17:21], out_wqkv, send.at[3], recv.at[3])
@@ -1316,6 +1369,7 @@
         load("wout", lambda: i_wout, lambda: w_gu.at[:, :, :, :, pl.ds(0, part_out.shape[-2]), :])
         gains[...] = jnp.zeros_like(gains)
         norm_back(res, g_ffn, gh, gains, 1, keep_residual)
+        load("mixf", lambda: i_mixf, lambda: gh.at[:, pl.ds(heads_w, heads_w)])
         sent_attn.start()
         loads.pop("wout")()
 
@@ -1356,7 +1410,8 @@
             for k in range(2):
                 c = cols(2 * g + k, 128)
                 grad = gm[:, c].astype(f32)
-                delta = head_sums(grad * mixf[:, c]) * linv[:, c]
+                mixed = gh[:, cols(2 * g + k + heads_w // 128, 128)]
+                delta = head_sums(grad * mixed) * linv[:, c]
                 grad = grad * linv[:, c]
                 for half in range(2):
                     d = roll_half(delta) if half == 0 else delta
@@ -1474,35 +1529,39 @@
             o[...] = (v + roll_half(v))[row : row + 1, :64]
 
     steps = {
-        "h": start_h, "nb": residual_back, "m": mixed_back, "att": start_attention,
-        "kvs": seq.swap().start, "kvc": seq.core_event, "kve": part(seq.plane_second, 0),
-        "kvf": keys_back, "oS": out.plane_send, "oe": out.plane_event, "of": out.final,
-        "lm": load_mix, "ll": load_last, "qe": sent_qkv.wait_recv, "g": start_g,
-        "nb2": input_back, "rs": ring_start, "re": ring_end,
+        b_h: start_h, b_nb: residual_back, b_m: mixed_back, b_att: start_attention,
+        b_kvs: seq.swap().start, b_kvc: seq.core_event, b_kve: part(seq.plane_second, 0),
+        b_kvf: keys_back, b_oS: out.plane_send, b_oe: out.plane_event, b_of: out.final, b_kS: rest.plane_send,
+        b_ke: rest.plane_event, b_kf: rest.final,
+        b_lm: load_mix, b_ll: load_last, b_qe: sent_qkv.wait_recv, b_g: start_g,
+        b_nb2: input_back, b_rs: ring_start, b_re: ring_end,
     }
-    steps.update(sum_steps("q", last))
-    steps.update(sum_steps("d", down))
-    steps.update(sum_steps("g", gateup))
+    steps.update(sum_steps(b_qf, last))
+    steps.update(sum_steps(b_df, down))
+    steps.update(sum_steps(b_gf, gateup))
     for i in range(NZ):
-        steps[f"dw{i}"] = part(rows_of, t_act, cot2, part_down, ("act", "cot"), i)
-        steps[f"gw{i}"] = part(rows_of, t_ffn, ggu2, part_gu, ("ffn", "ggu"), i)
-        steps[f"ow{i}"] = part(rows_of, t_act, gattn2, part_out, ("mix",), i)
-        steps[f"qw{i}"] = part(rows_of, t_ffn, gattn2, part_qkv, ("attn",), i)
-        steps[f"oa{i}"] = part(out.first, i)
-        steps[f"oo{i}"] = part(out.own_event, i)
+        steps[b_dw0 + i] = part(rows_of, t_act, cot2, part_down, ("act", "cot"), i)
+        steps[b_gw0 + i] = part(rows_of, t_ffn, ggu2, part_gu, ("ffn", "ggu"), i)
+        steps[b_ow0 + i] = part(rows_of, t_act, gattn2, part_out, ("mix",), i)
+        steps[b_qw0 + i] = part(rows_of, t_ffn, gattn2, part_qkv, ("attn",), i)
+        steps[b_oa0 + i] = part(out.first, i)
+        steps[b_oo0 + i] = part(out.own_event, i)
+        steps[b_ka0 + i] = part(rest.first, i)
+        steps[b_ko0 + i] = part(rest.own_event, i)
         if i < NZ - 1:
             for k in range(4):
-                steps[f"oz{i}{k}"] = part(out.z_event, i, k)
-            steps[f"hs{i}"] = hop(i).start
-            steps[f"he{i}"] = part(hop_end, i)
+                steps[b_oz00 + 4 * i + k] = part(out.z_event, i, k)
+                steps[b_kz00 + 4 * i + k] = part(rest.z_event, i, k)
+            steps[b_hs0 + i] = hop(i).start
+            steps[b_he0 + i] = part(hop_end, i)
     loops = {
-        "H": (8, h_step),
-        "B": (GROUPS * n_chunk, attend),
-        "Q": (heads_w // 128, query_back),
-        "G": (8, g_step),
+        b_H: (8, h_step),
+        b_B: (GROUPS * n_chunk, attend),
+        b_Q: (heads_w // 128, query_back),
+        b_G: (8, g_step),
     }
     run_steps(BACKWARD_ORDER, steps, loops)
-    for g in (down, gateup, out, seq, last):
+    for g in (down, rest, gateup, out, seq, last):
         g.finish()
     sent_qkv.wait_send()
     for k in range(1, NZ):
@@ -1529,7 +1588,7 @@
     ]
     like = [
         VMEM(v.shape, v.dtype)
-        for v in (t_ffn, t_act, cot2, ggu2, qkv, q2, linv, mixf, kk, va, mask_t, w_gu)
+        for v in (t_ffn, t_act, cot2, ggu2, qkv, q2, linv, kk, va, mask_t, w_gu)
     ]
     return pl.pallas_call(
         functools.partial(backward_kernel, dims),
@@ -1558,8 +1617,8 @@
             VMEM((4 * tok, 128), bf16),
             VMEM((tok, heads_w), bf16),
             VMEM((2, 2, 2, tok, 2 * kv_w), bf16),
-            dma((4, 16, NZ)),
-            dma((4, 16, NZ)),
+            dma((5, 16, NZ)),
+            dma((5, 16, NZ)),
             dma((8, 1)),
             dma((8, 1)),
             dma((3,)),
@@ -1568,11 +1627,12 @@
             dma((3 + NZ,)),
             dma((len(LOADS) + 1,)),
         ]
-        + Scatter.scratch(r_down, width)
+        + Scatter.scratch(r_down // 2, width, False)
         + Scatter.scratch(r_gu, width)
         + ScatterZ.scratch(r_out, width)
         + SequenceSum.scratch(tok, 2 * kv_w)
-        + Scatter.scratch(r_qkv, columns),
+        + Scatter.scratch(r_qkv, columns)
+        + ScatterZ.scratch(r_down // 2, width, False),
         compiler_params=pltpu.CompilerParams(
             collective_id=1, has_side_effects=True, vmem_limit_bytes=64 << 20
         ),

time: 242 us -> 241 us (level)
  no operation moved by 1% of the time
where the time goes in v4:
time: 241 us; the launch traced here: 240 us
  Pallas kernels  240 us (100%)
    pallas_call x1, Pallas kernels, forward(): pl.pallas_call(functools.partial(forward_kernel, (tok, width, n_dev, head...  120 us
    pallas_call x1, Pallas kernels, backward(): pl.pallas_call(functools.partial(backward_kernel, dims), out_shape=[shape...  116 us

profile of v4, /device:TPU:0, one launch (start us, length us, event | category | flops | bytes accessed | tf_op | source)
XLA Modules:
  0.0 240.4 jit_solution(7634643210985829772)
XLA Ops:
  0.6 119.8 %forward.1 = (bf16[256,2048]{1,0:T(8,128)(2,1)}, bf16[16,64,512]{2,1,0:T(8,128)(2,1)}, bf16[16,32,512]{2,1,0:T(8,128)(2,1)}, bf16[16,64,512]{2,1,0:T(8,128)(2,1)...) custom-call(bf16[256,2048]{1,0:T(8,128)(2,1)} %bitcast.13, ...), custom_call_target="tpu_custom_call" | custom-call | flops 9126805504 | bytes 52428800 | tf_op jit(solution)/shard_map/forward/pallas_call | solution.py:890
  120.5 115.8 %backward.1 = (bf16[256,2048]{1,0:T(8,128)(2,1)}, f32[1,2048]{1,0:T(1,128)}, f32[1,64]{1,0:T(1,128)}, f32[1,64]{1,0:T(1,128)}, f32[1,2048]{1,0:T(1,128)}, /*inde...) custom-call(f32[256,128]{1,0:T(8,128)} %get-tuple-element.50.refs_0_, ...), custom_call_target="tpu_custom_call" | custom-call | flops 21474836480 | bytes 62914560 | tf_op jit(solution)/shard_map/backward/pallas_call | solution.py:1593
  236.4 3.9 %settle.1 = (bf16[256,2048]{1,0:T(8,128)(2,1)}, bf16[256,2048]{1,0:T(8,128)(2,1)}, f32[1,2048]{1,0:T(1,128)}, f32[1,64]{1,0:T(1,128)}, f32[1,64]{1,0:T(1,128)}, ...) custom-call(bf16[256,2048]{1,0:T(8,128)(2,1)} %get-tuple-element.49., ...), custom_call_target="tpu_custom_call" | custom-call | tf_op jit(solution)/shard_map/settle/pallas_call | solution.py:1663

commit v5 on v4

--- a/solution.py
+++ b/solution.py
@@ -34,15 +34,17 @@
     b_dx0, b_dx1, b_dx2, b_dx3, b_dz0, b_dz1, b_dz2, b_dz3, b_gf, b_ga0, b_ga1, b_ga2, b_ga3,
     b_gb0, b_gb1, b_gb2, b_gb3, b_gd0, b_gd1, b_gd2, b_gd3, b_gx0, b_gx1, b_gx2, b_gx3, b_gz0,
     b_gz1, b_gz2, b_gz3, b_qf, b_qa0, b_qa1, b_qa2, b_qa3, b_qb0, b_qb1, b_qb2, b_qb3, b_qd0,
-    b_qd1, b_qd2, b_qd3, b_qx0, b_qx1, b_qx2, b_qx3, b_qz0, b_qz1, b_qz2, b_qz3, b_dw0, b_dw1,
-    b_dw2, b_dw3, b_gw0, b_gw1, b_gw2, b_gw3, b_ow0, b_ow1, b_ow2, b_ow3, b_qw0, b_qw1, b_qw2,
-    b_qw3, b_oa0, b_oa1, b_oa2, b_oa3, b_oo0, b_oo1, b_oo2, b_oo3, b_hs0, b_hs1, b_hs2, b_he0,
-    b_he1, b_he2, b_oz00, b_oz01, b_oz02, b_oz03, b_oz10, b_oz11, b_oz12, b_oz13, b_oz20, b_oz21,
-    b_oz22, b_oz23, b_ka0, b_ka1, b_ka2, b_ka3, b_ko0, b_ko1, b_ko2, b_ko3, b_kz00, b_kz01,
-    b_kz02, b_kz03, b_kz10, b_kz11, b_kz12, b_kz13, b_kz20, b_kz21, b_kz22, b_kz23, b_kS, b_ke,
-    b_kf, b_H, b_B, b_Q, b_G, b_h, b_nb, b_m, b_att, b_kvs, b_kvc, b_kve, b_kvf, b_oS, b_oe, b_of,
-    b_lm, b_ll, b_qe, b_g, b_nb2, b_rs, b_re,
-) = range(150)
+    b_qd1, b_qd2, b_qd3, b_qx0, b_qx1, b_qx2, b_qx3, b_qz0, b_qz1, b_qz2, b_qz3, b_rf, b_ra0,
+    b_ra1, b_ra2, b_ra3, b_rb0, b_rb1, b_rb2, b_rb3, b_rd0, b_rd1, b_rd2, b_rd3, b_rx0, b_rx1,
+    b_rx2, b_rx3, b_rz0, b_rz1, b_rz2, b_rz3, b_dw0, b_dw1, b_dw2, b_dw3, b_gw0, b_gw1, b_gw2,
+    b_gw3, b_ow0, b_ow1, b_ow2, b_ow3, b_qw0, b_qw1, b_qw2, b_qw3, b_rw0, b_rw1, b_rw2, b_rw3,
+    b_oa0, b_oa1, b_oa2, b_oa3, b_oo0, b_oo1, b_oo2, b_oo3, b_hs0, b_hs1, b_hs2, b_he0, b_he1,
+    b_he2, b_oz00, b_oz01, b_oz02, b_oz03, b_oz10, b_oz11, b_oz12, b_oz13, b_oz20, b_oz21, b_oz22,
+    b_oz23, b_ka0, b_ka1, b_ka2, b_ka3, b_ko0, b_ko1, b_ko2, b_ko3, b_kz00, b_kz01, b_kz02,
+    b_kz03, b_kz10, b_kz11, b_kz12, b_kz13, b_kz20, b_kz21, b_kz22, b_kz23, b_kS, b_ke, b_kf, b_H,
+    b_B, b_Q, b_G, b_h, b_nb, b_m, b_att, b_kvs, b_kvc, b_kve, b_kvf, b_oS, b_oe, b_of, b_lm,
+    b_ll, b_qs, b_qe, b_qk, b_g, b_nb2, b_rs, b_re,
+) = range(177)
 
 FORWARD_ORDER = [
     f_kP, f_qZ, f_qp0, f_oP, f_norm, f_oZ, f_qz1, f_qp1, f_qe0, f_qz2, f_trig, f_oz10, f_dZ,
@@ -59,19 +61,21 @@
 ]
 
 BACKWARD_ORDER = [
-    b_dw0, b_dw1, b_dw2, b_da1, b_ka1, b_dw3, b_gw0, b_gw1, b_ka0, b_h, *[b_H] * 6, b_ga0,
-    *[b_H] * 2, b_nb, b_lm, b_gw2, b_gw3, b_gb1, b_kz03, b_gb0, b_m, b_db1, b_att, b_gb2, b_kz02,
-    b_da2, b_ow0, b_B, b_oa0, *[b_B] * 2, b_ow1, *[b_B] * 2, b_kz13, b_B, b_da0, b_ga2, b_ll, b_B,
-    b_oa1, b_ga1, b_B, b_gd0, b_B, b_gd2, b_kz00, b_kz01, b_B, b_ow2, b_B, b_gb3, b_B, b_oa2,
-    b_ga3, *[b_B] * 3, b_oz01, b_gd1, b_ow3, b_B, b_kvs, b_Q, b_da3, b_ka2, b_kz12, b_dd1, b_kz22,
-    b_kz23, b_kz11, b_Q, b_dd0, b_db0, b_Q, b_db3, b_Q, b_oz00, b_gx0, b_dx1, b_oz10, b_oz11,
-    b_kvc, b_kz10, b_oz03, *[b_Q] * 2, b_oz21, b_oz13, b_Q, b_kz21, b_Q, b_kve, b_gd3, b_gz0,
-    b_kvf, b_kz20, b_ko3, b_dd2, b_g, b_db2, b_gx1, b_oz02, b_gx2, b_dd3, b_G, b_dx0, b_G, b_dz0,
-    b_qe, b_ko1, b_qw0, b_qa0, b_qb0, b_oz20, b_dx2, b_oz23, b_oz12, b_qw1, b_qw2, b_dz1, b_qa1,
-    b_qb1, b_G, b_oz22, b_qa2, b_dz2, *[b_G] * 2, b_qd0, b_gz1, b_ko0, b_qw3, b_qb2, *[b_G] * 2,
-    b_ko2, b_gz2, b_G, b_qd1, b_nb2, b_oo3, b_hs0, b_kS, b_oo1, b_oo2, b_qd2, b_qx0, b_he0, b_oo0,
-    b_qz0, b_hs1, b_qx1, b_oS, b_qa3, b_qz1, b_he1, b_hs2, b_qx2, b_df, b_gf, b_ka3, b_qz2, b_ke,
-    b_oe, b_he2, b_rs, b_qb3, b_oa3, b_qd3, b_qf, b_kf, b_re, b_of,
+    b_dw0, b_ka0, b_gw0, b_gw1, b_dw1, b_ga0, b_dw2, b_gb0, b_dw3, b_da1, b_h, *[b_H] * 2, b_kz00,
+    b_da0, *[b_H] * 3, b_kz03, b_H, b_ka1, b_da2, *[b_H] * 2, b_nb, b_gw2, b_gw3, b_ga3, b_kz02,
+    b_db1, b_lm, b_ka2, b_m, b_att, b_ll, b_ow0, b_ga1, b_ga2, b_dd0, b_oa0, b_kz12, b_kz13,
+    *[b_B] * 2, b_ow1, b_oa1, b_B, b_gd0, b_B, b_kz22, *[b_B] * 3, b_db0, b_gd2, b_oz00, b_oz01,
+    b_B, b_kz10, b_B, b_ow2, b_gb2, b_gd3, b_kz20, b_gx0, b_gb1, b_oa2, b_B, b_gd1, *[b_B] * 3,
+    b_gb3, b_ow3, b_oz02, b_kz01, b_oa3, *[b_B] * 3, b_kz11, b_dx0, b_kvs, b_Q, b_dd1, b_oz12,
+    b_oz11, b_db2, b_oz22, b_oz10, b_Q, b_db3, b_dd2, b_Q, b_oz03, b_da3, b_gx1, *[b_Q] * 3,
+    b_kz21, b_oz13, b_gx2, b_ko0, b_kvc, b_dx1, b_ko2, b_oz21, b_dz0, *[b_Q] * 2, b_qs, b_kve,
+    b_qe, b_kz23, b_qw0, b_qw1, b_qw2, b_dz1, b_qb2, b_qa0, b_qa1, b_oz23, b_qb1, b_qw3, b_qa2,
+    b_gz0, b_kvf, b_qb0, b_qk, b_rw0, b_rw1, b_ra0, b_rw2, b_ra2, b_rb2, b_rb0, b_dx2, b_g, b_ka3,
+    b_dd3, b_oz20, b_gz1, b_qd1, b_ra1, *[b_G] * 2, b_oo3, b_rw3, b_G, b_rb1, *[b_G] * 2, b_gz2,
+    b_qd0, *[b_G] * 2, b_rd0, b_G, b_ko1, b_qd2, b_ko3, b_rb3, b_rd2, b_ra3, b_nb2, b_oo0, b_rd1,
+    b_kS, b_dz2, b_qa3, b_qx0, b_hs0, b_qz0, b_he0, b_qx2, b_rx0, b_rz0, b_hs1, b_oo2, b_oo1,
+    b_qx1, b_oS, b_qz1, b_ke, b_rx1, b_rz1, b_qz2, b_he1, b_rx2, b_rz2, b_hs2, b_gf, b_oe, b_rd3,
+    b_he2, b_qd3, b_df, b_rs, b_qb3, b_qf, b_re, b_rf, b_kf, b_of,
 ]
 
 
@@ -1269,14 +1273,15 @@
     return steps
 
 
-def weight_grad(left, zp, right, part):
+def weight_grad(left, zp, right, part, first=0):
     rows, columns = part.shape[-2:]
     lhs = left[pl.ds(zp * 4, 4)].reshape(4 * rows, left.shape[-1])
     step = 512
 
     def body(n, _):
         c = cols(n, step)
-        part[zp, :, :, :, c] = dot(lhs, right[:, c]).astype(bf16).reshape(2, 2, rows, step)
+        grad = dot(lhs, right[:, cols(n + first // step, step)])
+        part[zp, :, :, :, c] = grad.astype(bf16).reshape(2, 2, rows, step)
         return 0
 
     lax.fori_loop(0, columns // step, body, 0)
@@ -1296,11 +1301,11 @@
         i_kk, i_va, i_mask, i_wqkv, i_wout, i_wgu,
         o_dx, o_attn, o_q, o_k, o_ffn, out_wqkv, out_wout, out_wgu, out_wdown,
         t_ffn, t_act, cot2, ggu2, qkv, q2, linv, kk, va, mask_t, w_gu,
-        part_qkv, part_out, part_gu, part_down, res, gains, came, gh, gattn2, acc_q,
+        part_q, part_kv, part_out, part_gu, part_down, res, gains, came, gh, gattn2, acc_q,
         aug, gm, terms,
         send, recv, kv_send, kv_recv, ex_send, ex_recv, g_send, g_recv, lsem,
-    ) = refs[:66]
-    bufs = refs[66:]
+    ) = refs[:67]
+    bufs = refs[67:]
     g_q, g_k = twice(one_q), twice(one_k)
     pc = Place()
     z = pc.z
@@ -1338,17 +1343,19 @@
     rest = ScatterZ(pc, part_down, bufs[21:26], out_wdown, send.at[4], recv.at[4], pl.ds(cut, cut))
     gateup = Scatter(pc, part_gu, bufs[4:8], out_wgu, send.at[1], recv.at[1])
     out = ScatterZ(pc, part_out, bufs[8:13], out_wout, send.at[2], recv.at[2])
-    last = Scatter(pc, part_qkv, bufs[17:21], out_wqkv, send.at[3], recv.at[3])
+    out_q, out_kv = out_wqkv.at[:, pl.ds(0, heads_w)], out_wqkv.at[:, pl.ds(heads_w, 2 * kv_w)]
+    last = Scatter(pc, part_q, bufs[17:21], out_q, send.at[3], recv.at[3])
+    last_kv = Scatter(pc, part_kv, bufs[26:30], out_kv, send.at[5], recv.at[5])
     seq = SequenceSum(pc, terms, bufs[13:17], kv_send, kv_recv, ex_send.at[2], ex_recv.at[2])
 
     own = pl.ds(0, tok)
     back = pl.ds(tok, tok)
 
-    def rows_of(left, right, term, names, i):
+    def rows_of(left, right, term, names, i, first=0):
         for name in names:
             if name in loads:
                 loads.pop(name)()
-        weight_grad(left, far(z, i), right, term)
+        weight_grad(left, far(z, i), right, term, first)
 
     def h_step(n):
         w = w_gu[n // 2, n % 2].reshape(width // 8, 2 * ff)
@@ -1373,7 +1380,7 @@
         sent_attn.start()
         loads.pop("wout")()
 
-    columns = part_qkv.shape[-1]
+    columns = heads_w + 2 * kv_w
     some = pl.ds(0, columns)
 
     def load_mix():
@@ -1469,7 +1476,13 @@
     def query_back(t):
         head_back(t, gh[:, cols(t, 128)], g_q, 2)
 
-    sent_qkv = remote(gattn2.at[own, some], gattn2.at[back, some], pc.sn(), ex_send.at[1], ex_recv.at[1])
+    def swap_columns(k, c):
+        return remote(
+            gattn2.at[own, c], gattn2.at[back, c], pc.sn(), ex_send.at[k], ex_recv.at[k]
+        )
+
+    sent_q = swap_columns(1, pl.ds(0, heads_w))
+    sent_kv = swap_columns(3, pl.ds(heads_w, 2 * kv_w))
 
     def keys_back():
         seq.plane_arrived(0)
@@ -1478,7 +1491,7 @@
         for t in range(kv_w // 128):
             head_back(heads_w // 128 + t, gh[:, pl.ds(t * 128, 128)], g_k, 3)
         gattn2[own, pl.ds(heads_w + kv_w, kv_w)] = gh[:, pl.ds(kv_w, kv_w)].astype(bf16)
-        sent_qkv.start()
+        sent_kv.start()
 
     def g_step(n):
         w = w_gu[n // 2, n % 2, :, :, :, some].reshape(width // 8, columns)
@@ -1533,17 +1546,19 @@
         b_kvs: seq.swap().start, b_kvc: seq.core_event, b_kve: part(seq.plane_second, 0),
         b_kvf: keys_back, b_oS: out.plane_send, b_oe: out.plane_event, b_of: out.final, b_kS: rest.plane_send,
         b_ke: rest.plane_event, b_kf: rest.final,
-        b_lm: load_mix, b_ll: load_last, b_qe: sent_qkv.wait_recv, b_g: start_g,
+        b_lm: load_mix, b_ll: load_last, b_qs: sent_q.start, b_qe: sent_q.wait_recv, b_qk: sent_kv.wait_recv, b_g: start_g,
         b_nb2: input_back, b_rs: ring_start, b_re: ring_end,
     }
     steps.update(sum_steps(b_qf, last))
+    steps.update(sum_steps(b_rf, last_kv))
     steps.update(sum_steps(b_df, down))
     steps.update(sum_steps(b_gf, gateup))
     for i in range(NZ):
         steps[b_dw0 + i] = part(rows_of, t_act, cot2, part_down, ("act", "cot"), i)
         steps[b_gw0 + i] = part(rows_of, t_ffn, ggu2, part_gu, ("ffn", "ggu"), i)
         steps[b_ow0 + i] = part(rows_of, t_act, gattn2, part_out, ("mix",), i)
-        steps[b_qw0 + i] = part(rows_of, t_ffn, gattn2, part_qkv, ("attn",), i)
+        steps[b_qw0 + i] = part(rows_of, t_ffn, gattn2, part_q, ("attn",), i)
+        steps[b_rw0 + i] = part(rows_of, t_ffn, gattn2, part_kv, ("attn",), i, heads_w)
         steps[b_oa0 + i] = part(out.first, i)
         steps[b_oo0 + i] = part(out.own_event, i)
         steps[b_ka0 + i] = part(rest.first, i)
@@ -1561,9 +1576,10 @@
         b_G: (8, g_step),
     }
     run_steps(BACKWARD_ORDER, steps, loops)
-    for g in (down, rest, gateup, out, seq, last):
+    for g in (down, rest, gateup, out, seq, last, last_kv):
         g.finish()
-    sent_qkv.wait_send()
+    sent_q.wait_send()
+    sent_kv.wait_send()
     for k in range(1, NZ):
         ring(k).wait_send()
     sent_dx.wait()
@@ -1584,7 +1600,7 @@
     r_qkv, r_out, r_gu, r_down = rows
     partial = [
         VMEM((NZ, 2, 2, r, c), bf16)
-        for r, c in ((r_qkv, columns), (r_out, width), (r_gu, width), (r_down, width))
+        for r, c in ((r_qkv, heads_w), (r_qkv, 2 * kv_w), (r_out, width), (r_gu, width), (r_down, width))
     ]
     like = [
         VMEM(v.shape, v.dtype)
@@ -1617,12 +1633,12 @@
             VMEM((4 * tok, 128), bf16),
             VMEM((tok, heads_w), bf16),
             VMEM((2, 2, 2, tok, 2 * kv_w), bf16),
-            dma((5, 16, NZ)),
-            dma((5, 16, NZ)),
+            dma((6, 16, NZ)),
+            dma((6, 16, NZ)),
             dma((8, 1)),
             dma((8, 1)),
-            dma((3,)),
-            dma((3,)),
+            dma((4,)),
+            dma((4,)),
             dma((3 + NZ,)),
             dma((3 + NZ,)),
             dma((len(LOADS) + 1,)),
@@ -1631,8 +1647,9 @@
         + Scatter.scratch(r_gu, width)
         + ScatterZ.scratch(r_out, width)
         + SequenceSum.scratch(tok, 2 * kv_w)
-        + Scatter.scratch(r_qkv, columns)
-        + ScatterZ.scratch(r_down // 2, width, False),
+        + Scatter.scratch(r_qkv, heads_w)
+        + ScatterZ.scratch(r_down // 2, width, False)
+        + Scatter.scratch(r_qkv, 2 * kv_w),
         compiler_params=pltpu.CompilerParams(
             collective_id=1, has_side_effects=True, vmem_limit_bytes=64 << 20
         ),

time: 241 us -> 236 us (0.979)
  Pallas kernels: 240 us -> 235 us
    pallas_call x1, Pallas kernels: 116 us -> 111 us  [backward(): pl.pallas_call(functools.partial(backward_kernel, dims), out_shape=[shape...]
where the time goes in v5:
time: 236 us; the launch traced here: 235 us
  Pallas kernels  235 us (100%)
    pallas_call x1, Pallas kernels, forward(): pl.pallas_call(functools.partial(forward_kernel, (tok, width, n_dev, head...  120 us
    pallas_call x1, Pallas kernels, backward(): pl.pallas_call(functools.partial(backward_kernel, dims), out_shape=[shape...  111 us

profile of v5, /device:TPU:0, one launch (start us, length us, event | category | flops | bytes accessed | tf_op | source)
XLA Modules:
  0.0 235.4 jit_solution(1171712863588865157)
XLA Ops:
  0.6 119.8 %forward.1 = (bf16[256,2048]{1,0:T(8,128)(2,1)}, bf16[16,64,512]{2,1,0:T(8,128)(2,1)}, bf16[16,32,512]{2,1,0:T(8,128)(2,1)}, bf16[16,64,512]{2,1,0:T(8,128)(2,1)...) custom-call(bf16[256,2048]{1,0:T(8,128)(2,1)} %bitcast.13, ...), custom_call_target="tpu_custom_call" | custom-call | flops 9126805504 | bytes 52428800 | tf_op jit(solution)/shard_map/forward/pallas_call | solution.py:894
  120.5 110.9 %backward.1 = (bf16[256,2048]{1,0:T(8,128)(2,1)}, f32[1,2048]{1,0:T(1,128)}, f32[1,64]{1,0:T(1,128)}, f32[1,64]{1,0:T(1,128)}, f32[1,2048]{1,0:T(1,128)}, /*inde...) custom-call(f32[256,128]{1,0:T(8,128)} %get-tuple-element.50.refs_0_, ...), custom_call_target="tpu_custom_call" | custom-call | flops 21474836480 | bytes 62914560 | tf_op jit(solution)/shard_map/backward/pallas_call | solution.py:1609
  231.4 3.9 %settle.1 = (bf16[256,2048]{1,0:T(8,128)(2,1)}, bf16[256,2048]{1,0:T(8,128)(2,1)}, f32[1,2048]{1,0:T(1,128)}, f32[1,64]{1,0:T(1,128)}, f32[1,64]{1,0:T(1,128)}, ...) custom-call(bf16[256,2048]{1,0:T(8,128)(2,1)} %get-tuple-element.49., ...), custom_call_target="tpu_custom_call" | custom-call | tf_op jit(solution)/shard_map/settle/pallas_call | solution.py:1680
